TPU v7x, 256 devices: a whole 4x4x8 slice. The times are simulated.
256 devices in a mesh: req: 64 (over z, y, core), tp: 4 (over x).
Axes of the slice: x: 4, y: 4, z: 8, core: 2. Of those that a mesh axis runs over, the one named last changes fastest.
Arguments:
- projected: bfloat16 [8448, 3, 2048], P('req', None, 'tp'), may hold values from -400 to 400
- residual: bfloat16 [8448, 2048], P('req'), may hold values from -8 to 8
- query_gain: float32 [2048], P('tp'), may hold values from 0.6 to 2
- key_gain: float32 [2048], P('tp'), may hold values from 0.6 to 2
- context_cache: bfloat16 [64, 512, 2, 2048], P('req', None, None, 'tp'), may hold values from -6 to 6
- decode_cache: bfloat16 [256, 512, 2, 2048], P('req', None, None, 'tp'), may hold values from -6 to 6
- offsets: int32 [64], P('req'), may hold values from 0 to 512, as said below
- lengths: int32 [256], P('req'), may hold values from 1 to 512, as said below
- group_order: int32 [64], replicated, may hold values from 0 to 63, each once
- expert_ids: int32 [8448, 8], P('req'), may hold values from 0 to 63, all different within a row; in each aligned block of 132 rows (0 to 131, 132 to 263, ...) at most 32 rows name the same one
- out_weight: bfloat16 [2048, 2048], P('tp'), may hold values from -0.125 to 0.125
- post_gain: float32 [2048], replicated, may hold values from 0.25 to 1.75
- router: bfloat16 [2048, 64], replicated, may hold values from -12 to 12
- gate_weight: bfloat16 [64, 2048, 1024], P('req', None, 'tp'), may hold values from -0.125 to 0.125
- up_weight: bfloat16 [64, 2048, 1024], P('req', None, 'tp'), may hold values from -0.125 to 0.125
- down_weight: bfloat16 [64, 1024, 2048], P('req', 'tp'), may hold values from -0.1875 to 0.1875
Outputs:
- out: bfloat16 [8448, 2048], P('req', 'tp')
Inputs may be any that keep to these rules, and one draw needn't show every extreme that they name: `offsets`: some group has exactly 512 cached tokens. `lengths`: some decode request has exactly 512 cached tokens. `group_order`: each group index appears once. `expert_ids`: each token names 8 different experts. Among the 132 rows of one device no expert is named more than 32 times, and some device's rows name one expert exactly 32 times.
All inputs are finite; a program needn't handle non-finite values.
Results may differ from a plain program's by a relative error of at most 0.02.
The roundings to bfloat16 on the way count: a program that leaves them out, or rounds other values in their place, can miss the bound.
Values may be sent and summed in bfloat16 or wider, within the bound.
No kernel may reach another device: no remote copies, remote signals or barrier semaphores. Data moves between devices by JAX's collectives and lax.ppermute only.
A program may use at most 128 MiB of HBM per device.

v0:
```python
import math

import jax
import jax.numpy as jnp
from jax import lax
from jax.sharding import PartitionSpec as P

HEAD_DIM = 128


def rotate_rows(values, positions, head_size):
    row_count = values.shape[0]
    head_count = values.shape[1] // head_size
    half_size = head_size // 2
    shaped = values.reshape(row_count, head_count, head_size)
    frequency = 10000.0 ** (-2.0 * jnp.arange(half_size, dtype=jnp.float32) / head_size)
    angles = positions.astype(jnp.float32)[:, None] * frequency[None, :]
    cosine = jnp.cos(angles)[:, None, :]
    sine_part = jnp.sin(angles)[:, None, :]
    first_half = shaped[:, :, :half_size]
    second_half = shaped[:, :, half_size:]
    turned = jnp.concatenate(
        [
            first_half * cosine - second_half * sine_part,
            second_half * cosine + first_half * sine_part,
        ],
        axis=2,
    )
    return turned.reshape(row_count, head_count * head_size)


def attend(queries, key_rows, value_rows, usable):
    factor = 1.0 / math.sqrt(queries.shape[-1])
    scores = (
        jnp.einsum("qhd,khd->hqk", queries, key_rows, preferred_element_type=jnp.float32) * factor
    )
    scores = jnp.where(usable[None, :, :], scores, -jnp.inf)
    largest = jnp.max(scores, axis=2, keepdims=True)
    weights = jnp.exp(scores - largest)
    shares = (weights / jnp.sum(weights, axis=2, keepdims=True)).astype(jnp.bfloat16)
    mixture = jnp.einsum("hqk,khd->qhd", shares, value_rows, preferred_element_type=jnp.float32)
    return mixture.astype(jnp.bfloat16)


def group_attention(
    query_rows,
    key_new,
    value_new,
    context,
    decode_cache,
    offset,
    decode_lengths,
    head_size,
    prefill_rows,
):
    width_here = query_rows.shape[1]
    head_count = width_here // head_size
    context_size = context.shape[0]

    def heads_view(matrix):
        return matrix.reshape(matrix.shape[:-1] + (head_count, head_size))

    prefill_keys = jnp.concatenate([context[:, 0], key_new[:prefill_rows]], axis=0)
    prefill_values = jnp.concatenate([context[:, 1], value_new[:prefill_rows]], axis=0)
    key_spot = jnp.arange(context_size + prefill_rows, dtype=jnp.int32)[None, :]
    query_spot = jnp.arange(prefill_rows, dtype=jnp.int32)[:, None]
    prefill_usable = jnp.where(
        key_spot < context_size, key_spot < offset, key_spot - context_size <= query_spot
    )
    prefill_out = attend(
        heads_view(query_rows[:prefill_rows]),
        heads_view(prefill_keys),
        heads_view(prefill_values),
        prefill_usable,
    )
    decode_count = decode_cache.shape[0]
    cache_slots = decode_cache.shape[1]
    decode_keys = jnp.concatenate([decode_cache[:, :, 0], key_new[prefill_rows:, None, :]], axis=1)
    decode_values = jnp.concatenate(
        [decode_cache[:, :, 1], value_new[prefill_rows:, None, :]], axis=1
    )
    slot_index = jnp.arange(cache_slots + 1, dtype=jnp.int32)[None, :]
    decode_usable = (slot_index < decode_lengths[:, None]) | (slot_index == cache_slots)
    decode_out = jax.vmap(attend)(
        heads_view(query_rows[prefill_rows:, None, :]),
        heads_view(decode_keys),
        heads_view(decode_values),
        decode_usable[:, None, :],
    )
    return jnp.concatenate(
        [
            prefill_out.reshape(prefill_rows, width_here),
            decode_out.reshape(decode_count, width_here),
        ],
        axis=0,
    )


def per_device(
    projected,
    residual,
    query_gain,
    key_gain,
    context_cache,
    decode_cache,
    offsets,
    lengths,
    group_order,
    expert_ids,
    out_weight,
    post_gain,
    router,
    gate_weight,
    up_weight,
    down_weight,
):
    row_count = projected.shape[0]
    decode_count = lengths.shape[0]
    prefill_rows = row_count - decode_count
    width_here = projected.shape[2]
    width_full = width_here * lax.axis_size("tp")
    column_start = lax.axis_index("tp") * width_here
    query_raw = projected[:, 0].astype(jnp.float32)
    key_raw = projected[:, 1].astype(jnp.float32)
    square_sums = lax.psum(
        (jnp.sum(query_raw * query_raw, axis=1), jnp.sum(key_raw * key_raw, axis=1)), "tp"
    )
    query_norm = query_raw * lax.rsqrt(square_sums[0] / width_full + 1e-05)[:, None] * query_gain
    key_norm = key_raw * lax.rsqrt(square_sums[1] / width_full + 1e-05)[:, None] * key_gain
    row_spot = jnp.arange(row_count, dtype=jnp.int32)
    decode_slot = jnp.clip(row_spot - prefill_rows, 0, decode_count - 1)
    positions = jnp.where(row_spot < prefill_rows, offsets[0] + row_spot, lengths[decode_slot])
    query_rot = rotate_rows(query_norm, positions, HEAD_DIM).astype(jnp.bfloat16)
    key_rot = rotate_rows(key_norm, positions, HEAD_DIM).astype(jnp.bfloat16)
    attention = group_attention(
        query_rot,
        key_rot,
        projected[:, 2],
        context_cache[0],
        decode_cache,
        offsets[0],
        lengths,
        HEAD_DIM,
        prefill_rows,
    )
    partial_out = jnp.dot(attention, out_weight, preferred_element_type=jnp.float32)
    total_out = lax.psum(partial_out, "tp")
    state_full = (residual.astype(jnp.float32) + total_out).astype(jnp.bfloat16)
    state_wide = state_full.astype(jnp.float32)
    normed_full = (
        state_wide
        * lax.rsqrt(jnp.sum(state_wide * state_wide, axis=1) / width_full + 1e-05)[:, None]
        * post_gain
    ).astype(jnp.bfloat16)
    logits = jnp.dot(normed_full, router, preferred_element_type=jnp.float32)
    state_cols = lax.dynamic_slice_in_dim(state_full, column_start, width_here, 1)
    expert_count = router.shape[1]
    top_count = expert_ids.shape[1]
    chosen_mask = expert_ids[:, :, None] == jnp.arange(expert_count, dtype=jnp.int32)[None, None, :]
    picked = jnp.sum(jnp.where(chosen_mask, logits[:, None, :], 0.0), axis=2)
    largest = jnp.max(picked, axis=1, keepdims=True)
    raised = jnp.exp(picked - largest)
    gates = raised / jnp.sum(raised, axis=1, keepdims=True)
    pair_count = row_count * top_count
    capacity = min(
        row_count, 8 * ((3 * row_count * top_count + 16 * expert_count - 1) // (16 * expert_count))
    )
    flat_ids = expert_ids.reshape(pair_count)
    matches = (flat_ids[:, None] == jnp.arange(expert_count, dtype=jnp.int32)[None, :]).astype(
        jnp.int32
    )
    slot_of = jnp.sum(jnp.cumsum(matches, axis=0) * matches, axis=1) - 1
    owner_row = jnp.arange(pair_count, dtype=jnp.int32) // top_count
    outgoing = (
        jnp.zeros((expert_count, capacity, normed_full.shape[1]), jnp.bfloat16)
        .at[flat_ids, slot_of]
        .set(normed_full[owner_row])
    )
    arrived = lax.all_to_all(outgoing, "req", split_axis=0, concat_axis=0, tiled=True)
    source_count = arrived.shape[0]
    item_count = arrived.shape[1]
    flattened = arrived.reshape(source_count * item_count, arrived.shape[2])
    gate_pre = jnp.dot(flattened, gate_weight[0], preferred_element_type=jnp.float32)
    up_pre = jnp.dot(flattened, up_weight[0], preferred_element_type=jnp.float32)
    hidden = (jax.nn.silu(gate_pre) * up_pre).astype(jnp.bfloat16)
    terms = jnp.dot(hidden, down_weight[0], preferred_element_type=jnp.float32)
    answered = lax.psum_scatter(
        terms.astype(jnp.bfloat16), "tp", scatter_dimension=1, tiled=True
    ).reshape(source_count, item_count, width_here)
    returned = lax.all_to_all(answered, "req", split_axis=0, concat_axis=0, tiled=True)
    gathered = returned[flat_ids, slot_of]
    expert_part = jnp.sum(
        gathered.astype(jnp.float32).reshape(row_count, top_count, width_here) * gates[:, :, None],
        axis=1,
    )
    placed = (state_cols.astype(jnp.float32) + expert_part).astype(jnp.bfloat16)
    group_total = group_order.shape[0]
    inverse = (
        jnp.zeros((group_total,), jnp.int32)
        .at[group_order]
        .set(jnp.arange(group_total, dtype=jnp.int32))
    )
    own_start = inverse[lax.axis_index("req")] * row_count
    segment = lax.all_gather(placed, "req", axis=0, tiled=True)
    segment_rows = segment.shape[0]
    border = jnp.zeros((row_count, segment.shape[1]), segment.dtype)
    padded = jnp.concatenate([border, segment, border], axis=0)
    source_row = own_start + jnp.arange(row_count, dtype=jnp.int32)
    inside = (source_row >= 0) & (source_row < segment_rows)
    window_start = jnp.clip(own_start + row_count, 0, segment_rows + row_count)
    window = lax.dynamic_slice_in_dim(padded, window_start, row_count, 0)
    return jnp.where(inside[:, None], window, jnp.zeros((row_count, width_here), jnp.bfloat16))


def solution(mesh):
    return jax.shard_map(
        per_device,
        mesh=mesh,
        in_specs=(
            P("req", None, "tp"),
            P("req", None),
            P("tp"),
            P("tp"),
            P("req", None, None, "tp"),
            P("req", None, None, "tp"),
            P("req"),
            P("req"),
            P(),
            P("req", None),
            P("tp", None),
            P(),
            P(),
            P("req", None, "tp"),
            P("req", None, "tp"),
            P("req", "tp", None),
        ),
        out_specs=P("req", "tp"),
        check_vma=False,
    )
```

profile of v0, /device:TPU:32, one launch (start us, length us, event | category | flops | bytes accessed | tf_op | source)
XLA Modules:
  0.0 687.2 jit_solution(18254325276036758896)
XLA Ops:
  6.6 1.3 multiply_reduce_fusion.1
  7.8 1.0 slice_convert_fusion.1
  8.9 0.6 iota_add_fusion
  9.5 0.9 slice.67
  10.4 1.5 fusion.89
  12.5 0.1 reshape.464
  12.6 0.1 reshape.463
  12.7 2.5 compare_select_fusion.4
  15.2 0.3 multiply_cosine_fusion
  15.5 10.5 %all-reduce.1 = (f32[132]{0:T(256)S(1)}, f32[132]{0:T(256)S(1)}) all-reduce(f32[132]{0:T(256)S(1)} %get-tuple-element.6, f32[132]{0:T(256)S(1)} %get-tuple-element.5), channel_id=1, replica_groups=mesh['req'=64,'tp'=4] {'tp'}, use_global_device_ids=true, to_apply=%region_4.5 | all-reduce | flops 264 | bytes 2112 | tf_op jit(solution)/shard_map/psum | solution.py:125
  26.2 0.3 subtract_convert_fusion.1
  26.5 0.8 fusion.50
  27.3 0.7 fusion.64
  27.9 0.5 iota_compare_fusion.5
  28.5 1.3 slice.78
  29.8 0.5 iota_compare_fusion.6
  30.3 2.4 copy.67
  32.8 1.1 fusion.88
  33.8 1.3 copy.71
  35.1 0.8 copy.68
  35.9 1.0 copy.75
  36.9 10.5 %fusion.87 = (bf16[4,512,1,512]{3,2,1,0:T(2,128)(2,1)}, bf16[4,512,1,512]{3,2,1,0:T(2,128)(2,1)}) fusion(bf16[4,512,2,512]{3,2,1,0:T(2,128)(2,1)} %param.21), kind=kLoop, calls=%fused_computation.153 | loop fusion | bytes 8388608 | tf_op jit(solution)/shard_map/slice | solution.py:78
  47.4 10.5 %copy.86 = bf16[4,512,1,512]{1,3,0,2:T(8,128)(2,1)} copy(bf16[4,512,1,512]{3,2,1,0:T(2,128)(2,1)} %get-tuple-element.13) | data formatting | bytes 4194304
  58.0 10.5 %copy.85 = bf16[4,512,1,512]{1,3,0,2:T(8,128)(2,1)} copy(bf16[4,512,1,512]{3,2,1,0:T(2,128)(2,1)} %get-tuple-element.14) | data formatting | bytes 4194304
  68.4 1.8 concatenate.66
  70.3 2.1 fusion.10
  72.4 0.2 fusion.26
  72.6 3.3 fusion.6
  75.9 0.9 copy.84
  76.9 1.4 fusion.39
  78.2 3.3 fusion.90
  81.5 1.8 convolution_convert_fusion.1
  83.3 1.5 fusion.43
  85.3 18.1 %reduce-window.6 = s32[64,9,128]{2,1,0:T(8,128)S(1)} reduce-window(s32[64,9,128]{2,1,0:T(8,128)S(1)} %reshape.465, s32[]{:T(128)} %constant.30.clone.1), window={size=1x1x128 pad=0_0x0_0x127_0}, to_apply=%region_10.11 | reduce-window | flops 9363456 | bytes 589828 | tf_op jit(solution)/shard_map/reduce-window
  103.5 0.2 slice.104
  103.7 0.3 copy.78
  104.0 0.1 copy.79
  104.1 0.2 broadcast_add_fusion
  104.3 0.1 reshape.454
  104.4 0.1 copy.105
  104.7 0.1 and_reduce_fusion
  104.8 31.9 %all-reduce.4.cloned.1.call-done = f32[132,2048]{1,0:T(8,128)} async-done(((f32[132,2048]{1,0:T(8,128)}), f32[132,2048]{1,0:T(8,128)}) %all-reduce.4.cloned.1.call-update) | async-done | bytes 1081360 | tf_op jit(solution)/shard_map/psum | solution.py:147
  136.7 1.5 fusion.22
  138.2 0.8 copy-done.3
  139.0 0.2 fusion.24
  139.2 34.9 %scatter_custom_fusion.1 = bf16[2048,2048]{1,0:T(8,128)(2,1)} fusion(s32[1056]{0:T(1024)S(1)} %broadcast_select_fusion, bf16[132,2048]{1,0:T(8,128)(2,1)S(1)} %fusion.24, s32[2048]{0:T(1024)S(1)} %pad_clamp_fusion, bf16[]{:T(256)} %constant.36.clone.1), kind=kCustom, calls=%fused_computation.8 | custom fusion | bytes 8388610
  174.1 195.8 %all_to_all.10 = bf16[64,32,2048]{2,1,0:T(8,128)(2,1)S(1)} all-to-all(bf16[64,32,2048]{2,1,0:T(8,128)(2,1)} %bitcast.77), channel_id=1, replica_groups=mesh['req'=64,'tp'=4] {'req'}, dimensions={0} | all-to-all | bytes 16777216 | tf_op jit(solution)/shard_map/all_to_all | solution.py:179
  370.0 3.2 copy-done.2
  373.2 3.8 fusion.30
  377.0 13.2 %convolution_convert_fusion = bf16[2048,2048]{1,0:T(8,128)(2,1)} fusion(bf16[2048,2048]{1,0:T(8,128)(2,1)} %bitcast.79, f32[2048,256]{1,0:T(8,128)} %fusion.30, bf16[1,256,2048]{2,1,0:T(8,128)(2,1)S(1)} %copy-done.17, bf16[1,2048,256]{2,1,0:T(8,128)(2,1)S(1)} %copy-done.18), kind=kOutput, calls=%fused_computation.7 | convolution fusion | flops 4302307328 | bytes 20971520 | tf_op jit(solution)/shard_map/dot_general | solution.py:186
  390.2 79.9 %reduce-scatter.2.cloned.1.call-done = bf16[2048,512]{1,0:T(8,128)(2,1)} async-done(((bf16[2048,2048]{1,0:T(8,128)(2,1)}), bf16[2048,512]{1,0:T(8,128)(2,1)}) %reduce-scatter.2.cloned.1.call-update) | async-done | bytes 2097168 | tf_op jit(solution)/shard_map/reduce_scatter | solution.py:187
  470.1 10.6 %all-to-all-start.1 = ((bf16[64,32,512]{2,1,0:T(8,128)(2,1)}), bf16[64,32,512]{2,1,0:T(8,128)(2,1)S(1)}, u32[]{:S(2)}, u32[]{:S(2)}) async-start(bf16[64,32,512]{2,1,0:T(8,128)(2,1)} %bitcast.83), calls=%async_computation.2 | async-start | bytes 4194304 | tf_op jit(solution)/shard_map/all_to_all | solution.py:190
  480.8 0.3 fusion.97
  481.3 0.1 copy.80
  481.4 49.8 %all-to-all-done.1 = bf16[64,32,512]{2,1,0:T(8,128)(2,1)S(1)} async-done(((bf16[64,32,512]{2,1,0:T(8,128)(2,1)}), bf16[64,32,512]{2,1,0:T(8,128)(2,1)S(1)}, u32[]{:S(2)}, u32[]{:S(2)}) %all-to-all-start.1) | async-done | bytes 2097184 | tf_op jit(solution)/shard_map/all_to_all | solution.py:190
  531.1 12.7 %gather_fusion = bf16[1056,512]{1,0:T(8,128)(2,1)S(1)} fusion(bf16[64,32,512]{2,1,0:T(8,128)(2,1)S(1)} %all-to-all-done.1, s32[1056]{0:T(1024)S(1)} %get-tuple-element.9), kind=kCustom, calls=%fused_computation.1 | custom fusion | bytes 2171136 | tf_op jit(solution)/shard_map/gather | solution.py:191
  543.9 0.7 fusion.15
  544.6 1.6 fusion.47
  546.3 0.8 scatter_custom_fusion
  547.1 0.6 dynamic_slice.9
  548.3 77.7 %all-gather.3.cloned.1.call-done = bf16[64,132,512]{2,1,0:T(8,128)(2,1)} async-done(((bf16[1,132,512]{2,1,0:T(8,128)(2,1)}), bf16[64,132,512]{2,1,0:T(8,128)(2,1)}) %all-gather.3.cloned.1.call-update) | async-done | bytes 8650768 | tf_op jit(solution)/shard_map/all_gather | solution.py:204
  626.0 12.5 %reshape.521 = bf16[8448,512]{1,0:T(8,128)(2,1)} reshape(bf16[64,132,512]{2,1,0:T(8,128)(2,1)} %all-gather.3.cloned.1.call-done) | data formatting | bytes 17301504
  638.6 40.4 %concatenate.63 = bf16[8712,512]{1,0:T(8,128)(2,1)} concatenate(bf16[132,512]{1,0:T(8,128)(2,1)S(1)} %broadcast.391, bf16[8448,512]{1,0:T(8,128)(2,1)} %reshape.521, bf16[132,512]{1,0:T(8,128)(2,1)S(1)} %broadcast.391), dimensions={0} | concatenate | bytes 17842176 | tf_op jit(solution)/shard_map/concatenate | solution.py:207
  679.0 1.7 dynamic-slice_select_fusion
  (73 shorter events, 1.3 us)
Async XLA Ops:
  6.5 76.8 %copy-start = (bf16[512,2048]{1,0:T(8,128)(2,1)S(1)}, bf16[512,2048]{1,0:T(8,128)(2,1)}, u32[]{:S(2)}) copy-start(bf16[512,2048]{1,0:T(8,128)(2,1)} %param.26) | copy-start | bytes 6291460
  6.5 19.5 %copy-start.11 = (f32[512]{0:T(512)S(1)}, f32[512]{0:T(512)}, u32[]{:S(2)}) copy-start(f32[512]{0:T(512)} %param.19) | copy-start | bytes 6148
  6.5 19.6 %copy-start.12 = (f32[512]{0:T(512)S(1)}, f32[512]{0:T(512)}, u32[]{:S(2)}) copy-start(f32[512]{0:T(512)} %param.18) | copy-start | bytes 6148
  6.5 130.2 %all-reduce.4.cloned.1.call-start = ((), (), s32[]{:S(2)}) async-start(), calls=%async_computation.3 | async-start | bytes 2228224 | tf_op jit(solution)/shard_map/psum | solution.py:147
  47.4 10.5 %copy-start.9 = (s32[4]{0:T(128)S(1)}, s32[4]{0:T(128)}, u32[]{:S(2)}) copy-start(s32[4]{0:T(128)} %param.23) | copy-start | bytes 52
  47.4 10.5 %copy-start.13 = (pred[513]{0:T(1024)(128)(4,1)S(1)}, pred[513]{0:T(1024)(128)(4,1)}, u32[]{:S(2)}) copy-start(pred[513]{0:T(1024)(128)(4,1)} %iota_compare_fusion.5) | copy-start | bytes 1543
  58.0 10.5 %copy-start.8 = (bf16[4,1,512]{2,0,1:T(4,128)(2,1)S(1)}, bf16[4,1,512]{2,0,1:T(4,128)(2,1)}, u32[]{:S(2)}) copy-start(bf16[4,1,512]{2,0,1:T(4,128)(2,1)} %slice.78) | copy-start | bytes 12292
  75.9 5.6 copy-start.5
  83.3 1.7 copy-start.7
  84.9 385.2 %reduce-scatter.2.cloned.1.call-start = ((), (), s32[]{:S(2)}) async-start(), calls=%async_computation.4 | async-start | bytes 10485760 | tf_op jit(solution)/shard_map/reduce_scatter | solution.py:187
  103.5 1.2 copy-start.15
  103.5 1.3 copy-start.14
  103.5 33.2 %copy-start.4 = (bf16[132,2048]{1,0:T(8,128)(2,1)S(1)}, bf16[132,2048]{1,0:T(8,128)(2,1)}, u32[]{:S(2)}) copy-start(bf16[132,2048]{1,0:T(8,128)(2,1)} %param.17) | copy-start | bytes 1622020
  104.1 34.9 %copy-start.10 = (f32[2048]{0:T(1024)S(1)}, f32[2048]{0:T(1024)}, u32[]{:S(2)}) copy-start(f32[2048]{0:T(1024)} %param.27) | copy-start | bytes 24580
  138.2 0.8 copy-start.3
  174.1 199.1 %copy-start.16 = (bf16[1,2048,256]{2,1,0:T(8,128)(2,1)S(1)}, bf16[1,2048,256]{2,1,0:T(8,128)(2,1)}, u32[]{:S(2)}) copy-start(bf16[1,2048,256]{2,1,0:T(8,128)(2,1)} %param.29) | copy-start | bytes 3145732
  370.0 3.2 copy-start.2
  373.2 3.8 copy-start.17
  373.2 3.8 copy-start.18
  470.1 10.7 %copy-start.6 = (bf16[2048,64]{0,1:T(8,128)(2,1)S(1)}, bf16[2048,64]{0,1:T(8,128)(2,1)}, u32[]{:S(2)}) copy-start(bf16[2048,64]{0,1:T(8,128)(2,1)} %param.28) | copy-start | bytes 786436
  470.1 61.0 %all-to-all-start.1 = ((bf16[64,32,512]{2,1,0:T(8,128)(2,1)}), bf16[64,32,512]{2,1,0:T(8,128)(2,1)S(1)}, u32[]{:S(2)}, u32[]{:S(2)}) async-start(bf16[64,32,512]{2,1,0:T(8,128)(2,1)} %bitcast.83), calls=%async_computation.2 | async-start | bytes 4194304 | tf_op jit(solution)/shard_map/all_to_all | solution.py:190
  480.7 145.3 %all-gather.3.cloned.1.call-start = ((), (), s32[]{:S(2)}) async-start(), calls=%async_computation.5 | async-start | bytes 9052160 | tf_op jit(solution)/shard_map/all_gather | solution.py:204
  543.9 2.4 copy-start.19
  638.6 42.1 %copy-start.1 = (bf16[512,2048]{1,0:T(8,128)(2,1)S(1)}, bf16[512,2048]{1,0:T(8,128)(2,1)}, u32[]{:S(2)}) copy-start(bf16[512,2048]{1,0:T(8,128)(2,1)} %param.26) | copy-start | bytes 6291460
Sparse Core Ops, SparseCore 0:
  85.0 51.6 all-reduce.3
  390.3 79.7 reduce-scatter.1
  546.4 79.6 all-gather.2
where the time goes:
time: 691 us; the launch traced here: 687 us
  waiting for transfers between devices  239 us (35%)
  blocking collectives  206 us (30%)
  local copies, waits for them, and re-layouts  152 us (22%)
  other arithmetic  35 us (5%)
  matrix products  29.3 us (4%)
  between operations  14.8 us (2%)
  starting transfers between devices  10.7 us (2%)
    all_to_all x1, blocking collectives, per_device(): lax.all_to_all(outgoing, 'req', split_axis=0, concat_axis=0, tiled=True)  196 us
    reduce_scatter x1, waiting for transfers between devices, per_device(): lax.psum_scatter(terms.astype(jnp.bfloat16), 'tp', scatter_dimension=1, t...  79.9 us
    all_gather x1, waiting for transfers between devices, per_device(): segment = lax.all_gather(placed, 'req', axis=0, tiled=True)  77.7 us
    unnamed x47, local copies, waits for them, and re-layouts  75.1 us
    all_to_all x1, waiting for transfers between devices, per_device(): lax.all_to_all(answered, 'req', split_axis=0, concat_axis=0, tiled=True)  49.8 us
    concatenate x1, local copies, waits for them, and re-layouts, per_device(): padded = jnp.concatenate([border, segment, border], axis=0)  40.4 us
    psum x1, waiting for transfers between devices, per_device(): total_out = lax.psum(partial_out, 'tp')  31.9 us
    another operation x5, other arithmetic  18.6 us
  transfers between devices with their start and end apart: 4, of which 4 were waited for; matrix products, arithmetic and copies ran while one was open for 3% of the time, Pallas kernels for 0%

commit v1 on v0

v1 whole, which is shorter than its diff:
```python
import functools
import math

import jax
import jax.numpy as jnp
from jax import lax
from jax.experimental import pallas as pl
from jax.experimental.pallas import tpu as pltpu
from jax.sharding import Mesh, PartitionSpec as P

HEAD_DIM = 128
HEADS_HERE = 4
PRE = 128
DEC = 4
ROWS = PRE + DEC
SLOTS = 512
COLS = 512
FULL = 2048
EXPERTS = 64
CAP = 32
PLANES = 8
TP = 4
QUARTER = 8
PAIR_LANES = 512
VMEM_LIMIT = 56 * 1024 * 1024
NEAR = (0, -1, 1, -2, 2, -3, 3, 4)
BF = jnp.bfloat16
F32 = jnp.float32
VM = pl.BlockSpec(memory_space=pltpu.VMEM)
SM = pl.BlockSpec(memory_space=pltpu.SMEM)
HB = pl.BlockSpec(memory_space=pl.ANY)


def dot(a, b, contract_a=1, contract_b=0):
    return lax.dot_general(
        a, b, (((contract_a,), (contract_b,)), ((), ())), preferred_element_type=F32
    )


def iota(shape, axis):
    return lax.broadcasted_iota(jnp.int32, shape, axis)


def attention_kernel(
    numbers, proj, inv, cosine, sine, q_gain, k_gain, context, cache, weight, own, *rest
):
    sends, total = rest[:3], rest[3]
    head = pl.program_id(0)
    factor = 1.0 / math.sqrt(HEAD_DIM)
    cos_v, sin_v = cosine[...], sine[...]

    def rotated(part, gain, column):
        norm = proj[part].astype(F32) * inv[:, column : column + 1] * gain[...]
        return (norm * cos_v + pltpu.roll(norm, HEAD_DIM // 2, 1) * sin_v).astype(BF)

    qr = rotated(0, q_gain, 0)
    kr = rotated(1, k_gain, 1)
    value = proj[2]
    low = jnp.finfo(F32).min

    q_pre, k_pre, v_pre = qr[:PRE], kr[:PRE], value[:PRE]
    rows = context.reshape(2 * SLOTS, HEAD_DIM)[...]
    column = iota((PRE, 2 * SLOTS), 1)
    seen = ((column & 1) == 0) & (column < 2 * numbers[0])
    s_old = jnp.where(seen, dot(q_pre, rows, 1, 1) * factor, low)
    causal = iota((PRE, PRE), 1) <= iota((PRE, PRE), 0)
    s_new = jnp.where(causal, dot(q_pre, k_pre, 1, 1) * factor, low)
    top = jnp.maximum(
        jnp.max(s_old, axis=1, keepdims=True), jnp.max(s_new, axis=1, keepdims=True)
    )
    e_old = jnp.where(seen, jnp.exp(s_old - top), 0.0)
    e_new = jnp.where(causal, jnp.exp(s_new - top), 0.0)
    share = 1.0 / (
        jnp.sum(e_old, axis=1, keepdims=True) + jnp.sum(e_new, axis=1, keepdims=True)
    )
    p_old = pltpu.roll(e_old * share, 1, 1).astype(BF)
    p_new = (e_new * share).astype(BF)
    mixed_pre = (dot(p_old, rows) + dot(p_new, v_pre)).astype(BF)

    q_dec, k_dec, v_dec = qr[PRE:], kr[PRE:], value[PRE:]
    keys = cache.reshape(DEC * 2 * SLOTS, HEAD_DIM)[...]
    row = iota((DEC, DEC * 2 * SLOTS), 0)
    column = iota((DEC, DEC * 2 * SLOTS), 1)
    length = jnp.where(
        row == 0,
        numbers[1],
        jnp.where(row == 1, numbers[2], jnp.where(row == 2, numbers[3], numbers[4])),
    )
    place = column - row * (2 * SLOTS)
    seen = ((column & 1) == 0) & (place >= 0) & (place < 2 * length)
    s_old = jnp.where(seen, dot(q_dec, keys, 1, 1) * factor, low)
    s_own = (
        jnp.sum(q_dec.astype(F32) * k_dec.astype(F32), axis=1, keepdims=True) * factor
    )
    top = jnp.maximum(jnp.max(s_old, axis=1, keepdims=True), s_own)
    e_old = jnp.where(seen, jnp.exp(s_old - top), 0.0)
    e_own = jnp.exp(s_own - top)
    share = 1.0 / (jnp.sum(e_old, axis=1, keepdims=True) + e_own)
    p_old = pltpu.roll(e_old * share, 1, 1).astype(BF)
    p_own = (e_own * share).astype(BF).astype(F32)
    mixed_dec = (dot(p_old, keys) + p_own * v_dec.astype(F32)).astype(BF)

    w = weight[...]
    out_pre = dot(mixed_pre, w)
    out_dec = dot(mixed_dec, w)

    @pl.when(head == 0)
    def _():
        for block in range(TP):
            span = slice(block * COLS, (block + 1) * COLS)
            total[block, :PRE] = out_pre[:, span]
            total[block, PRE:] = out_dec[:, span]

    @pl.when(head > 0)
    def _():
        for block in range(TP):
            span = slice(block * COLS, (block + 1) * COLS)
            total[block, :PRE] += out_pre[:, span]
            total[block, PRE:] += out_dec[:, span]

    @pl.when(head == HEADS_HERE - 1)
    def _():
        own[...] = total[numbers[5]]
        for step in range(1, TP):
            sends[step - 1][...] = total[(numbers[5] + step) % TP].astype(BF)


def attention(numbers, proj, inv, cosine, sine, q_gain, k_gain, context, cache, weight):
    whole = lambda *shape: pl.BlockSpec(shape, lambda h: (0,) * len(shape))
    return pl.pallas_call(
        attention_kernel,
        grid=(HEADS_HERE,),
        in_specs=[
            SM,
            pl.BlockSpec((3, ROWS, HEAD_DIM), lambda h: (0, 0, h)),
            whole(ROWS, 2),
            whole(ROWS, HEAD_DIM),
            whole(ROWS, HEAD_DIM),
            pl.BlockSpec((1, HEAD_DIM), lambda h: (0, h)),
            pl.BlockSpec((1, HEAD_DIM), lambda h: (0, h)),
            pl.BlockSpec((1, SLOTS, 2, HEAD_DIM), lambda h: (0, 0, 0, h)),
            pl.BlockSpec((DEC, SLOTS, 2, HEAD_DIM), lambda h: (0, 0, 0, h)),
            pl.BlockSpec((HEAD_DIM, FULL), lambda h: (h, 0)),
        ],
        out_specs=[whole(ROWS, COLS)] * TP,
        out_shape=[jax.ShapeDtypeStruct((ROWS, COLS), F32)]
        + [jax.ShapeDtypeStruct((ROWS, COLS), BF)] * (TP - 1),
        scratch_shapes=[pltpu.VMEM((TP, ROWS, COLS), F32)],
        compiler_params=pltpu.CompilerParams(vmem_limit_bytes=VMEM_LIMIT),
        cost_estimate=pl.CostEstimate(
            flops=2_000_000_000, bytes_accessed=10_000_000, transcendentals=1_000_000
        ),
        name="attention",
    )(numbers, proj, inv, cosine, sine, q_gain, k_gain, context, cache, weight)


def slot_part(code):
    wide = code.astype(F32)
    return jnp.where(wide > 64.0, wide - 64.0, wide)


def pair_onehot(code, plane, second):
    place = iota((EXPERTS, PAIR_LANES), 1)
    device = place >> 4
    x, c, y = device & 3, (device >> 2) & 1, device >> 3
    expert = plane * PLANES + y * 2 + (x >> 1)
    spread = (iota((EXPERTS, PAIR_LANES), 0) == expert).astype(F32).astype(BF)
    slot = dot(slot_part(code).astype(BF), spread)
    place = iota((1, PAIR_LANES), 1)
    device = place >> 4
    quarter = (device & 1) * 2 + ((device >> 2) & 1)
    wanted = quarter * QUARTER + (place & 7) + 1
    wanted = jnp.where(((place >> 3) & 1) == second, wanted, -1).astype(F32)
    return (slot == wanted).astype(F32).astype(BF)


def expand_kernel(numbers, code, *refs):
    held, out = refs[:-1], refs[-1]
    plane = numbers[0]
    for pair in range(PLANES // 2):
        filled = None
        for second in range(2):
            position = 2 * pair + second
            hits = pair_onehot(
                code[(plane + NEAR[position] + PLANES) % PLANES], plane, second
            )
            if position < PLANES - 1:
                rows = held[position][...]
            else:
                rows = jnp.concatenate(
                    [held[PLANES - 1][...], held[PLANES][...]], axis=0
                )
            part = dot(hits, rows, 0, 0)
            filled = part if filled is None else filled + part
        out[:, 16 * pair : 16 * pair + 16, :] = filled.astype(BF).reshape(32, 16, COLS)


def expand(numbers, code, held):
    return pl.pallas_call(
        expand_kernel,
        in_specs=[SM, VM] + [VM] * len(held),
        out_specs=VM,
        out_shape=jax.ShapeDtypeStruct((32, 64, COLS), BF),
        compiler_params=pltpu.CompilerParams(vmem_limit_bytes=VMEM_LIMIT),
        cost_estimate=pl.CostEstimate(
            flops=700_000_000, bytes_accessed=4_000_000, transcendentals=0
        ),
        name="expand",
    )(numbers, code, *held)


def combine_kernel(numbers, order, code, answers, out):
    plane = numbers[0]
    pair = pl.program_id(0)
    rows = answers[...].reshape(PAIR_LANES, COLS)
    for second in range(2):
        group = order[2 * pair + second]
        hits = pair_onehot(code[group], plane, second)
        out[second] = dot(hits, rows).astype(BF)


def combine(numbers, order, code, answers):
    return pl.pallas_call(
        combine_kernel,
        grid=(PLANES // 2,),
        in_specs=[
            SM,
            SM,
            pl.BlockSpec((EXPERTS, ROWS, EXPERTS), lambda p: (0, 0, 0)),
            pl.BlockSpec((32, 16, COLS), lambda p: (0, p, 0)),
        ],
        out_specs=pl.BlockSpec((2, ROWS, COLS), lambda p: (p, 0, 0)),
        out_shape=jax.ShapeDtypeStruct((PLANES, ROWS, COLS), BF),
        compiler_params=pltpu.CompilerParams(vmem_limit_bytes=VMEM_LIMIT),
        cost_estimate=pl.CostEstimate(
            flops=700_000_000, bytes_accessed=4_000_000, transcendentals=0
        ),
        name="combine",
    )(numbers, order, code, answers)


def chosen_kernel(numbers, code, out):
    plane, expert, quarter = numbers[0], numbers[1], numbers[2]
    is_expert = iota((ROWS, EXPERTS), 1) == expert
    place = iota((1, 64), 1)
    wanted = quarter * QUARTER + (place & 7) + 1

    def one(column, carry):
        filled = jnp.zeros((64, EXPERTS), F32)
        for position in range(PLANES):
            z = (plane + NEAR[position] + PLANES) % PLANES
            rows = code[column * PLANES + z]
            slot = jnp.sum(
                jnp.where(is_expert, slot_part(rows), 0.0), axis=1, keepdims=True
            )
            aim = jnp.where((place >> 3) == position, wanted, -1).astype(F32)
            hits = (slot == aim).astype(F32).astype(BF)
            filled = filled + dot(hits, rows, 0, 0)
        out[column] = filled
        return carry

    lax.fori_loop(0, PLANES, one, 0)


def chosen_rows(numbers, code):
    return pl.pallas_call(
        chosen_kernel,
        in_specs=[SM, VM],
        out_specs=VM,
        out_shape=jax.ShapeDtypeStruct((PLANES, 64, EXPERTS), F32),
        compiler_params=pltpu.CompilerParams(vmem_limit_bytes=VMEM_LIMIT),
        cost_estimate=pl.CostEstimate(
            flops=200_000_000, bytes_accessed=2_000_000, transcendentals=0
        ),
        name="chosen_rows",
    )(numbers, code)


def expert_kernel(numbers, arrived, codes, origin, gain, router, *refs):
    parts, out = refs[:18], refs[18]
    weights, sems = refs[19:22], refs[22]
    at_home = numbers[3]
    for kind in range(3):
        own, first, other_own, second, other_first, other_second = parts[
            6 * kind : 6 * kind + 6
        ]

        @pl.when(at_home == 1)
        def _():
            pltpu.make_async_copy(own, weights[kind].at[0], sems.at[kind, 0]).start()
            pltpu.make_async_copy(
                other_second, weights[kind].at[3], sems.at[kind, 3]
            ).start()

        @pl.when(at_home == 0)
        def _():
            pltpu.make_async_copy(
                other_own, weights[kind].at[0], sems.at[kind, 0]
            ).start()
            pltpu.make_async_copy(second, weights[kind].at[3], sems.at[kind, 3]).start()

        pltpu.make_async_copy(first, weights[kind].at[1], sems.at[kind, 1]).start()
        pltpu.make_async_copy(
            other_first, weights[kind].at[2], sems.at[kind, 2]
        ).start()

    wide = []
    squares = jnp.zeros((512, 1), F32)
    for x in range(TP):
        part = arrived[:, x].reshape(512, COLS).astype(F32)
        squares = squares + jnp.sum(part * part, axis=1, keepdims=True)
    scale = lax.rsqrt(squares / FULL + 1e-05)
    logits = jnp.zeros((512, EXPERTS), F32)
    for x in range(TP):
        span = slice(x * COLS, (x + 1) * COLS)
        part = arrived[:, x].reshape(512, COLS).astype(F32)
        normed = (part * scale * gain[:, span]).astype(BF)
        wide.append(normed)
        logits = logits + dot(normed, router[:, span], 1, 1)
    code = codes[...].reshape(512, EXPERTS)
    chosen = code > 0.0
    is_expert = iota((512, EXPERTS), 1) == numbers[1]
    top = jnp.max(jnp.where(chosen, logits, jnp.finfo(F32).min), axis=1, keepdims=True)
    raised = jnp.where(chosen, jnp.exp(jnp.minimum(logits - top, 0.0)), 0.0)
    bottom = jnp.sum(raised, axis=1, keepdims=True)
    share = jnp.sum(jnp.where(is_expert, raised, 0.0), axis=1, keepdims=True)
    gate = jnp.where(bottom > 0.0, share / jnp.where(bottom > 0.0, bottom, 1.0), 0.0)
    mark = jnp.sum(jnp.where(is_expert, code, 0.0), axis=1, keepdims=True)
    first_choice = (mark > 64.0).astype(F32)

    total = None
    for quarter in range(4):
        for kind in range(3):
            source = parts[6 * kind + 1]
            pltpu.make_async_copy(
                source, weights[kind].at[quarter], sems.at[kind, quarter]
            ).wait()
        gate_pre = jnp.zeros((512, 256), F32)
        up_pre = jnp.zeros((512, 256), F32)
        for x in range(TP):
            span = slice(x * COLS, (x + 1) * COLS)
            gate_pre = gate_pre + dot(wide[x], weights[0][quarter, span, :])
            up_pre = up_pre + dot(wide[x], weights[1][quarter, span, :])
        hidden = (gate_pre / (1.0 + jnp.exp(-gate_pre)) * up_pre).astype(BF)
        term = dot(hidden, weights[2][quarter])
        total = term if total is None else total + term
    result = total.astype(BF).astype(F32) * gate
    move = (origin[...] == iota((512, 512), 1)).astype(F32).astype(BF)
    for x in range(TP):
        span = slice(x * COLS, (x + 1) * COLS)
        part = arrived[:, x].reshape(512, COLS).astype(F32)
        piece = (result[:, span] + first_choice * part).astype(BF)
        out[:, x] = dot(move, piece).astype(BF).reshape(PLANES, 64, COLS)


def expert(numbers, arrived, codes, origin, gain, router, parts):
    return pl.pallas_call(
        expert_kernel,
        in_specs=[SM] + [VM] * 5 + [HB] * 18,
        out_specs=VM,
        out_shape=jax.ShapeDtypeStruct((PLANES, TP, 64, COLS), BF),
        scratch_shapes=[
            pltpu.VMEM((4, FULL, 256), BF),
            pltpu.VMEM((4, FULL, 256), BF),
            pltpu.VMEM((4, 256, FULL), BF),
            pltpu.SemaphoreType.DMA((3, 4)),
        ],
        compiler_params=pltpu.CompilerParams(vmem_limit_bytes=VMEM_LIMIT),
        cost_estimate=pl.CostEstimate(
            flops=6_500_000_000, bytes_accessed=20_000_000, transcendentals=500_000
        ),
        name="expert",
    )(numbers, arrived, codes, origin, gain, router, *parts)


def pair_moves():
    at = lambda core, x: core * TP + x
    over = lambda d: (d + TP) % (2 * TP)
    first = [
        (at(0, 0), at(0, 1)),
        (at(0, 1), at(0, 0)),
        (at(0, 2), at(1, 1)),
        (at(0, 3), at(1, 0)),
        (at(1, 2), at(1, 3)),
        (at(1, 3), at(1, 2)),
        (at(1, 1), at(0, 2)),
        (at(1, 0), at(0, 3)),
    ]
    second = [
        (at(1, 0), at(1, 1)),
        (at(1, 1), at(1, 0)),
        (at(0, 2), at(0, 3)),
        (at(0, 3), at(0, 2)),
    ]
    home = [at(0, 0), at(0, 1), at(1, 2), at(1, 3)]
    return (
        first,
        second,
        [(d, over(d)) for d in home],
        [(d, over(d)) for d in range(2 * TP)],
        [(over(d), d) for d in home],
    )


def gathered_weight(own):
    first_move, second_move, out_of_home, both, to_home = pair_moves()
    axes = ("c", "tp")
    first = lax.ppermute(own, axes, first_move)
    other_own = lax.ppermute(own, axes, out_of_home)
    second = lax.ppermute(first, axes, second_move)
    other_first = lax.ppermute(first, axes, both)
    other_second = lax.ppermute(second, axes, to_home)
    return [own, first, other_own, second, other_first, other_second]


def around(value, axis, step):
    count = lax.axis_size(axis)
    return lax.ppermute(value, axis, [(i, (i + step) % count) for i in range(count)])


def gather_column(value):
    up = [value]
    down = [value]
    for _ in range(3):
        up.append(around(up[-1], "z", 1))
        down.append(around(down[-1], "z", -1))
    return [
        value,
        up[1],
        down[1],
        up[2],
        down[2],
        up[3],
        down[3],
        around(up[3][:64], "z", 1),
        around(down[3][64:], "z", -1),
    ]


def per_device(
    projected,
    residual,
    query_gain,
    key_gain,
    context_cache,
    decode_cache,
    offsets,
    lengths,
    group_order,
    expert_ids,
    out_weight,
    post_gain,
    router,
    gate_weight,
    up_weight,
    down_weight,
):
    z, y, c, tp = (lax.axis_index(name) for name in ("z", "y", "c", "tp"))
    column = y * 2 + c

    every = jnp.arange(EXPERTS, dtype=jnp.int32)
    chosen = jnp.zeros((ROWS, EXPERTS), jnp.bool_)
    for k in range(expert_ids.shape[1]):
        chosen = chosen | (expert_ids[:, k : k + 1] == every[None, :])
    below = jnp.arange(ROWS)[:, None] >= jnp.arange(ROWS)[None, :]
    slot = dot(below.astype(BF), chosen.astype(BF))
    first_choice = expert_ids[:, :1] == every[None, :]
    code = jnp.where(chosen, slot + 64.0 * first_choice, 0.0).astype(BF)
    code_column = lax.all_gather(code, "z", axis=0)
    code_all = lax.all_gather(code_column, ("y", "c"), axis=0).reshape(
        EXPERTS, ROWS, EXPERTS
    )

    parts = (
        gathered_weight(gate_weight[0])
        + gathered_weight(up_weight[0])
        + gathered_weight(down_weight[0])
    )

    proj = jnp.transpose(projected, (1, 0, 2))
    raw = proj[:2].astype(F32)
    squares = lax.psum(jnp.sum(raw * raw, axis=2), "tp")
    inv = lax.rsqrt(squares / FULL + 1e-05).T
    spot = jnp.arange(ROWS, dtype=jnp.int32)
    positions = offsets[0] + spot
    for i in range(DEC):
        positions = jnp.where(spot == PRE + i, lengths[i], positions)
    half = HEAD_DIM // 2
    frequency = 10000.0 ** (-2.0 * jnp.arange(half, dtype=F32) / HEAD_DIM)
    angles = positions.astype(F32)[:, None] * frequency[None, :]
    cosine, sine = jnp.cos(angles), jnp.sin(angles)
    cosine = jnp.concatenate([cosine, cosine], axis=1)
    sine = jnp.concatenate([-sine, sine], axis=1)
    numbers = jnp.concatenate([offsets, lengths, tp[None].astype(jnp.int32)])
    own, *sends = attention(
        numbers,
        proj,
        inv,
        cosine,
        sine,
        query_gain[None],
        key_gain[None],
        context_cache,
        decode_cache,
        out_weight,
    )
    state = own
    for step in range(1, TP):
        state = state + around(sends[step - 1], "tp", step).astype(F32)
    residual_here = lax.dynamic_slice_in_dim(residual, tp * COLS, COLS, 1)
    state = (residual_here.astype(F32) + state).astype(BF)

    serves = y * 2 + tp // 2
    quarter = (tp % 2) * 2 + c
    at_home = (tp // 2 == c).astype(jnp.int32)
    numbers = jnp.stack([z, z * PLANES + serves, quarter, at_home]).astype(jnp.int32)
    codes = chosen_rows(numbers, code_all)
    outgoing = expand(numbers, code_column, gather_column(state))
    plane = ("y", "c", "tp")
    arrived = lax.all_to_all(outgoing, plane, split_axis=0, concat_axis=0, tiled=True)

    groups = jnp.arange(EXPERTS, dtype=jnp.int32)
    inverse = jnp.sum(
        jnp.where(group_order[None, :] == groups[:, None], groups[None, :], 0), axis=1
    )
    source = inverse.reshape(PLANES, PLANES).T
    source_z, source_column = source // PLANES, source % PLANES
    distance = (source_z - z + PLANES) % PLANES
    position = jnp.zeros_like(distance)
    for spot_here, near in enumerate(NEAR):
        position = jnp.where(distance == near % PLANES, spot_here, position)
    origin = (source_column * PLANES + position)[:, :, None] * QUARTER + jnp.arange(
        QUARTER, dtype=jnp.int32
    )
    result = expert(
        numbers,
        arrived.reshape(PLANES, TP, 64, COLS),
        codes,
        origin.reshape(512, 1),
        post_gain[None],
        router.T,
        parts,
    )
    answers = lax.all_to_all(
        result.reshape(32, 64, COLS), plane, split_axis=0, concat_axis=0, tiled=True
    )
    mine = lax.dynamic_index_in_dim(source, column, 0, keepdims=False)
    rows_in_code = (mine % PLANES) * PLANES + mine // PLANES
    sums = combine(numbers, rows_in_code, code_all, answers)
    return lax.psum_scatter(sums, "z", scatter_dimension=0)


def solution(mesh):
    split = Mesh(mesh.devices.reshape(PLANES, 4, 2, TP), ("z", "y", "c", "tp"))
    req = ("z", "y", "c")
    return jax.shard_map(
        per_device,
        mesh=split,
        in_specs=(
            P(req, None, "tp"),
            P(req, None),
            P("tp"),
            P("tp"),
            P(req, None, None, "tp"),
            P(req, None, None, "tp"),
            P(req),
            P(req),
            P(),
            P(req, None),
            P("tp", None),
            P(),
            P(),
            P(req, None, "tp"),
            P(req, None, "tp"),
            P(req, "tp", None),
        ),
        out_specs=P(req, "tp"),
        check_vma=False,
    )
```

time: 691 us -> 290 us (0.42)
  blocking collectives: 206 us -> 45.9 us
  local copies, waits for them, and re-layouts: 152 us -> 10.6 us
  waiting for transfers between devices: 239 us -> 106 us
  Pallas kernels: 0 us -> 48.6 us
  starting transfers between devices: 10.7 us -> 53.4 us
  matrix products: 29.3 us -> 0.19 us
  other arithmetic: 35 us -> 8.94 us
    all_to_all x1 -> x0, blocking collectives: 196 us -> none  [per_device(): lax.all_to_all(outgoing, 'req', split_axis=0, concat_axis=0, tiled=True)]
    unnamed x47 -> x32, local copies, waits for them, and re-layouts: 75.1 us -> 2.67 us
    all_gather x1, waiting for transfers between devices: 77.7 us -> 27.7 us  [per_device(): lax.all_gather(code_column, ('y', 'c'), axis=0)]
    pallas_call x0 -> x5, Pallas kernels: none -> 48.6 us  [the longest x1 20.4 us: expert(): pl.pallas_call(expert_kernel, in_specs=[SM] + [VM] * 5 + [HB] * 18, out_s...]
    concatenate x4 -> x0, local copies, waits for them, and re-layouts: 44.5 us -> none  [the longest x1 40.4 us: per_device(): padded = jnp.concatenate([border, segment, border], axis=0)]
    reduce_scatter x1, waiting for transfers between devices: 79.9 us -> 37.4 us  [per_device(): return lax.psum_scatter(sums, 'z', scatter_dimension=0)]
    ppermute x0 -> x26, starting transfers between devices: none -> 38.4 us  [the longest x11 17.5 us: around(): lax.ppermute(value, axis, [(i, (i + step) % count) for i in range(count)])]
    psum x1 -> x0, waiting for transfers between devices: 31.9 us -> none  [per_device(): total_out = lax.psum(partial_out, 'tp')]
  transfers between devices with their start and end apart: 4 -> 30, of which waited for: 4 -> 11; matrix products, arithmetic and copies ran while one was open for 3% -> 3% of each run, Pallas kernels for 0% -> 4%
where the time goes in v1:
time: 290 us; the launch traced here: 288 us
  waiting for transfers between devices  106 us (37%)
  starting transfers between devices  53.4 us (18%)
  Pallas kernels  48.6 us (17%)
  blocking collectives  45.9 us (16%)
  between operations  14.4 us (5%)
  local copies, waits for them, and re-layouts  10.6 us (4%)
  other arithmetic  8.94 us (3%)
    reduce_scatter x1, waiting for transfers between devices, per_device(): return lax.psum_scatter(sums, 'z', scatter_dimension=0)  37.4 us
    all_gather x1, blocking collectives, per_device(): code_column = lax.all_gather(code, 'z', axis=0)  28.1 us
    all_gather x1, waiting for transfers between devices, per_device(): lax.all_gather(code_column, ('y', 'c'), axis=0)  27.7 us
    all_to_all x1, waiting for transfers between devices, per_device(): lax.all_to_all(result.reshape(32, 64, COLS), plane, split_axis=0, concat_...  26.7 us
    pallas_call x1, Pallas kernels, expert(): pl.pallas_call(expert_kernel, in_specs=[SM] + [VM] * 5 + [HB] * 18, out_s...  20.4 us
    psum x1, blocking collectives, per_device(): squares = lax.psum(jnp.sum(raw * raw, axis=2), 'tp')  17.8 us
    ppermute x11, starting transfers between devices, around(): lax.ppermute(value, axis, [(i, (i + step) % count) for i in range(count)])  17.5 us
    ppermute x11, waiting for transfers between devices, around(): lax.ppermute(value, axis, [(i, (i + step) % count) for i in range(count)])  13.4 us
  transfers between devices with their start and end apart: 30, of which 11 were waited for; matrix products, arithmetic and copies ran while one was open for 3% of the time, Pallas kernels for 4%

profile of v1, /device:TPU:32, one launch (start us, length us, event | category | flops | bytes accessed | tf_op | source)
XLA Modules:
  0.0 287.9 jit_solution(3541727453228830721)
XLA Ops:
  7.2 1.1 multiply_reduce_fusion
  8.3 1.5 fusion.33
  9.8 0.1 copy.34
  9.9 17.8 %psum.7 = f32[2,132]{0,1:T(8,128)S(1)} all-reduce(f32[2,132]{0,1:T(8,128)S(1)} %copy.34), channel_id=1, replica_groups=mesh['z'=8,'y'=4,'c'=2,'tp'=4] {'tp'}, use_global_device_ids=true, to_apply=%region_2.3 | all-reduce | flops 264 | bytes 2112 | tf_op jit(solution)/shard_map/psum | solution.py:482
  27.7 0.6 rsqrt_bitcast_fusion.inv
  28.3 1.3 pad_add_fusion.1.numbers
  29.6 2.4 fusion.29
  32.0 0.3 fusion.19
  32.3 0.8 pad_maximum_fusion
  33.1 11.6 %attention.1 = (f32[132,512]{1,0:T(8,128)}, bf16[132,512]{1,0:T(8,128)(2,1)}, bf16[132,512]{1,0:T(8,128)(2,1)}, bf16[132,512]{1,0:T(8,128)(2,1)}) custom-call(s32[6]{0:T(128)} %pad_add_fusion.1.numbers, bf16[3,132,512]{2,1,0:T(8,128)(2,1)} %bitcast.55, f32[132,2]{1,0:T(8,128)} %rsqrt_bitcast_fusion.inv, f32[132,128]{1,0:T(8,128)} %get-tuple-element.28.cosine, ...), custom_call_target="tpu_custom_call" | custom-call | flops 2000000000 | bytes 10000000 | tf_op jit(solution)/shard_map/attention/pallas_call | solution.py:130
  44.8 1.5 collective-permute-start.1
  46.3 2.5 collective-permute-start.2
  48.8 4.0 %collective-permute-done = bf16[132,512]{1,0:T(8,128)(2,1)S(1)} collective-permute-done((bf16[132,512]{1,0:T(8,128)(2,1)}, bf16[132,512]{1,0:T(8,128)(2,1)S(1)}, u32[]{:S(2)}, u32[]{:S(2)}) %collective-permute-start) | collective-permute-done | bytes 135200 | tf_op jit(solution)/shard_map/ppermute | solution.py:418
  52.8 0.9 collective-permute-done.2
  53.6 1.1 add_convert_fusion.refs_0_
  54.7 0.2 collective-permute-start.4
  54.9 1.9 collective-permute-start.3
  56.8 3.0 %collective-permute-done.4.refs_2_ = bf16[132,512]{1,0:T(8,128)(2,1)S(1)} collective-permute-done((bf16[132,512]{1,0:T(8,128)(2,1)S(1)}, bf16[132,512]{1,0:T(8,128)(2,1)S(1)}, u32[]{:S(2)}, u32[]{:S(2)}) %collective-permute-start.4) | collective-permute-done | bytes 135200 | tf_op jit(solution)/shard_map/ppermute | solution.py:418
  59.9 3.8 %collective-permute-start.6 = (bf16[132,512]{1,0:T(8,128)(2,1)S(1)}, bf16[132,512]{1,0:T(8,128)(2,1)S(1)}, u32[]{:S(2)}, u32[]{:S(2)}) collective-permute-start(bf16[132,512]{1,0:T(8,128)(2,1)S(1)} %collective-permute-done.4.refs_2_), channel_id=1, source_target_pairs={{0,224},{32,0},{64,32},{96,64},{128,96},{160,128},{192,160},{224,1... | collective-permute-start | bytes 405512 | tf_op jit(solution)/shard_map/ppermute | solution.py:418
  63.6 0.5 collective-permute-done.3.refs_1_
  64.1 2.1 collective-permute-done.6.refs_4_
  66.2 3.7 %collective-permute-start.8 = (bf16[132,512]{1,0:T(8,128)(2,1)S(1)}, bf16[132,512]{1,0:T(8,128)(2,1)S(1)}, u32[]{:S(2)}, u32[]{:S(2)}) collective-permute-start(bf16[132,512]{1,0:T(8,128)(2,1)S(1)} %collective-permute-done.6.refs_4_), channel_id=1, source_target_pairs={{0,224},{32,0},{64,32},{96,64},{128,96},{160,128},{192,160},{224,1... | collective-permute-start | bytes 405512 | tf_op jit(solution)/shard_map/ppermute | solution.py:418
  69.9 0.4 collective-permute-done.5.refs_3_
  70.4 2.2 collective-permute-done.8.refs_6_
  72.5 3.7 %collective-permute-start.10 = (bf16[68,512]{1,0:T(8,128)(2,1)S(1)}, bf16[68,512]{1,0:T(8,128)(2,1)S(1)}, u32[]{:S(2)}, u32[]{:S(2)}) collective-permute-start(bf16[68,512]{1,0:T(8,128)(2,1)S(1)} %slice.63), channel_id=1, source_target_pairs={{0,224},{32,0},{64,32},{96,64},{128,96},{160,128},{192,160},{224,1... | collective-permute-start | bytes 208904 | tf_op jit(solution)/shard_map/ppermute | solution.py:418
  76.3 0.4 collective-permute-done.7.refs_5_
  76.6 0.1 collective-permute-start.9
  76.7 2.3 collective-permute-start.12
  79.1 1.1 collective-permute-start.11
  80.2 3.8 %collective-permute-start.17 = (bf16[2048,256]{1,0:T(8,128)(2,1)}, bf16[2048,256]{1,0:T(8,128)(2,1)}, u32[]{:S(2)}, u32[]{:S(2)}) collective-permute-start(bf16[2048,256]{1,0:T(8,128)(2,1)} %bitcast.28.refs_6_), channel_id=1, source_target_pairs={{0,4},{1,5},{6,2},{7,3},{8,12},{9,13},{14,10},{15,11},{16,20},{17,... | collective-permute-start | bytes 3145736 | tf_op jit(solution)/shard_map/ppermute | solution.py:409
  84.0 2.0 collective-permute-start.21
  86.0 0.2 fusion.2
  86.2 28.1 %all-gather.2 = bf16[8,132,64]{1,2,0:T(8,128)(2,1)S(1)} all-gather(bf16[1,132,64]{1,2,0:T(8,128)(2,1)S(1)} %fusion.2), channel_id=2, replica_groups=mesh['z'=8,'y'=4,'c'=2,'tp'=4] {'z'}, dimensions={0}, use_global_device_ids=true | all-gather | bytes 152064 | tf_op jit(solution)/shard_map/all_gather | solution.py:469
  114.3 0.9 copy.36.code
  115.2 0.6 pad_add_fusion.numbers
  115.8 2.3 collective-permute-start.22
  118.0 1.7 collective-permute-start.13
  119.8 1.6 collective-permute-start.18
  121.4 1.7 collective-permute-start.23
  123.1 5.1 %expand.1 = bf16[32,64,512]{2,1,0:T(8,128)(2,1)} custom-call(s32[4]{0:T(128)} %pad_add_fusion.numbers, bf16[8,132,64]{2,1,0:T(8,128)(2,1)} %copy.36.code, bf16[132,512]{1,0:T(8,128)(2,1)} %copy-done.3, bf16[132,512]{1,0:T(8,128)(2,1)} %copy-done.7, bf16[132,512]{1,0:T(8,128)(2,1)} %copy-done.6, bf16[132,512]{1,0:T(8,128)(2,1)} %copy-done.9, ...), custom_call_target="tpu_custom_call" | custom-call | flops 700000000 | bytes 4000000 | tf_op jit(solution)/shard_map/expand/pallas_call | solution.py:199
  128.3 9.3 %all-to-all-start = ((bf16[32,64,512]{2,1,0:T(8,128)(2,1)}), bf16[32,64,512]{2,1,0:T(8,128)(2,1)S(1)}, u32[]{:S(2)}, u32[]{:S(2)}) async-start(bf16[32,64,512]{2,1,0:T(8,128)(2,1)} %expand.1), calls=%async_computation | async-start | bytes 4194304 | tf_op jit(solution)/shard_map/all_to_all | solution.py:520
  137.6 0.7 all-gather.5.cloned.1.call-update
  138.3 0.4 collective-permute-start.19
  138.7 0.2 collective-permute-start.24
  138.9 1.3 collective-permute-start.15
  140.2 1.3 collective-permute-start.20
  141.5 1.3 collective-permute-start.25
  142.8 0.1 select_reduce_fusion
  142.9 0.1 reshape.62
  143.1 0.1 copy.38
  143.1 0.1 iota_add_fusion
  143.2 0.8 add.135.origin
  144.1 27.7 %all-gather.5.cloned.1.call-done = bf16[64,132,64]{1,2,0:T(8,128)(2,1)} async-done(((bf16[8,132,64]{1,2,0:T(8,128)(2,1)}), bf16[64,132,64]{1,2,0:T(8,128)(2,1)}) %all-gather.5.cloned.1.call-update) | async-done | bytes 1081360 | tf_op jit(solution)/shard_map/all_gather | solution.py:470
  171.8 4.3 %copy.40.code = bf16[64,132,64]{2,1,0:T(8,128)(2,1)} copy(bf16[64,132,64]{1,2,0:T(8,128)(2,1)} %all-gather.5.cloned.1.call-done) | data formatting | bytes 2162688 | tf_op jit(solution)/shard_map/all_gather | solution.py:470
  176.1 6.1 %chosen_rows.1.codes = f32[8,64,64]{2,1,0:T(8,128)} custom-call(s32[4]{0:T(128)} %pad_add_fusion.numbers, bf16[64,132,64]{2,1,0:T(8,128)(2,1)} %copy.40.code), custom_call_target="tpu_custom_call" | custom-call | flops 200000000 | bytes 2000000 | tf_op jit(solution)/shard_map/chosen_rows/pallas_call | solution.py:266
  182.2 1.3 copy-done.2
  183.5 20.4 %expert.1 = bf16[8,4,64,512]{3,2,1,0:T(8,128)(2,1)} custom-call(s32[4]{0:T(128)} %pad_add_fusion.numbers, bf16[8,4,64,512]{3,2,1,0:T(8,128)(2,1)} %bitcast.52, f32[8,64,64]{2,1,0:T(8,128)} %chosen_rows.1.codes, s32[512,1]{1,0:T(8,128)} %add.135.origin, f32[1,2048]{1,0:T(1,128)} %bitcast.70, bf16[64,2048]{1,0:T(8,128)(2,1)} %bitcast.69, ...), custom_call_target="tpu_custom_call" | custom-call | flops 6499999744 | bytes 20000000 | tf_op jit(solution)/shard_map/expert/pallas_call | solution.py:357
  203.9 5.5 %all-to-all-start.1 = ((bf16[32,64,512]{2,1,0:T(8,128)(2,1)}), bf16[32,64,512]{2,1,0:T(8,128)(2,1)S(1)}, u32[]{:S(2)}, u32[]{:S(2)}) async-start(bf16[32,64,512]{2,1,0:T(8,128)(2,1)} %bitcast.53), calls=%async_computation.1 | async-start | bytes 4194304 | tf_op jit(solution)/shard_map/all_to_all | solution.py:544
  209.5 0.2 dynamic-slice_reduce_fusion
  209.6 0.5 fusion.31.order
  210.2 26.7 %all-to-all-done.1.answers = bf16[32,64,512]{2,1,0:T(8,128)(2,1)S(1)} async-done(((bf16[32,64,512]{2,1,0:T(8,128)(2,1)}), bf16[32,64,512]{2,1,0:T(8,128)(2,1)S(1)}, u32[]{:S(2)}, u32[]{:S(2)}) %all-to-all-start.1) | async-done | bytes 2097184 | tf_op jit(solution)/shard_map/all_to_all | solution.py:544
  236.9 1.3 copy-done
  238.2 5.4 %combine.1 = bf16[8,132,512]{2,1,0:T(8,128)(2,1)} custom-call(s32[4]{0:T(128)} %pad_add_fusion.numbers, s32[8]{0:T(128)} %fusion.31.order, bf16[64,132,64]{2,1,0:T(8,128)(2,1)} %copy.40.code, bf16[32,64,512]{2,1,0:T(8,128)(2,1)} %copy-done), custom_call_target="tpu_custom_call" | custom-call | flops 700000000 | bytes 4000000 | tf_op jit(solution)/shard_map/combine/pallas_call | solution.py:223
  243.7 37.4 %reduce-scatter.2.cloned.1.call-done = bf16[1,132,512]{2,1,0:T(8,128)(2,1)} async-done(((bf16[8,132,512]{2,1,0:T(8,128)(2,1)}), bf16[1,132,512]{2,1,0:T(8,128)(2,1)}) %reduce-scatter.2.cloned.1.call-update) | async-done | bytes 135184 | tf_op jit(solution)/shard_map/reduce_scatter | solution.py:550
  (62 shorter events, 0.3 us)
Async XLA Ops:
  33.1 43.6 %copy-start.13 = (bf16[1,2048,256]{2,1,0:T(8,128)(2,1)S(1)}, bf16[1,2048,256]{2,1,0:T(8,128)(2,1)}, u32[]{:S(2)}) copy-start(bf16[1,2048,256]{2,1,0:T(8,128)(2,1)} %param.29) | copy-start | bytes 3145732
  33.1 52.9 %copy-start.12 = (s32[132,8]{0,1:T(8,128)S(1)}, s32[132,8]{0,1:T(8,128)}, u32[]{:S(2)}) copy-start(s32[132,8]{0,1:T(8,128)} %param.25) | copy-start | bytes 12676
  44.7 8.0 %collective-permute-start = (bf16[132,512]{1,0:T(8,128)(2,1)}, bf16[132,512]{1,0:T(8,128)(2,1)S(1)}, u32[]{:S(2)}, u32[]{:S(2)}) collective-permute-start(bf16[132,512]{1,0:T(8,128)(2,1)} %get-tuple-element.10), channel_id=1, source_target_pairs={{0,1},{1,2},{2,3},{3,0},{4,5},{5,6},{6,7},{7,4},{8,9},{9,10},{10,1... | collective-permute-start | bytes 405512 | tf_op jit(solution)/shard_map/ppermute | solution.py:418
  44.8 8.0 %collective-permute-start.1 = (bf16[132,512]{1,0:T(8,128)(2,1)}, bf16[132,512]{1,0:T(8,128)(2,1)S(1)}, u32[]{:S(2)}, u32[]{:S(2)}) collective-permute-start(bf16[132,512]{1,0:T(8,128)(2,1)} %get-tuple-element.11), channel_id=1, source_target_pairs={{0,2},{1,3},{2,0},{3,1},{4,6},{5,7},{6,4},{7,5},{8,10},{9,11},{10,... | collective-permute-start | bytes 405512 | tf_op jit(solution)/shard_map/ppermute | solution.py:418
  46.3 7.3 %collective-permute-start.2 = (bf16[132,512]{1,0:T(8,128)(2,1)}, bf16[132,512]{1,0:T(8,128)(2,1)S(1)}, u32[]{:S(2)}, u32[]{:S(2)}) collective-permute-start(bf16[132,512]{1,0:T(8,128)(2,1)} %get-tuple-element.12), channel_id=1, source_target_pairs={{0,3},{1,0},{2,1},{3,2},{4,7},{5,4},{6,5},{7,6},{8,11},{9,8},{10,9... | collective-permute-start | bytes 405512 | tf_op jit(solution)/shard_map/ppermute | solution.py:418
  54.7 68.4 %copy-start.3 = (bf16[132,512]{1,0:T(8,128)(2,1)}, bf16[132,512]{1,0:T(8,128)(2,1)S(1)}, u32[]{:S(2)}) copy-start(bf16[132,512]{1,0:T(8,128)(2,1)S(1)} %add_convert_fusion.refs_0_) | copy-start | bytes 405508
  54.7 5.1 %collective-permute-start.4 = (bf16[132,512]{1,0:T(8,128)(2,1)S(1)}, bf16[132,512]{1,0:T(8,128)(2,1)S(1)}, u32[]{:S(2)}, u32[]{:S(2)}) collective-permute-start(bf16[132,512]{1,0:T(8,128)(2,1)S(1)} %add_convert_fusion.refs_0_), channel_id=1, source_target_pairs={{0,224},{32,0},{64,32},{96,64},{128,96},{160,128},{192,160},{224,1... | collective-permute-start | bytes 405512 | tf_op jit(solution)/shard_map/ppermute | solution.py:418
  54.9 9.2 %collective-permute-start.3 = (bf16[132,512]{1,0:T(8,128)(2,1)S(1)}, bf16[132,512]{1,0:T(8,128)(2,1)S(1)}, u32[]{:S(2)}, u32[]{:S(2)}) collective-permute-start(bf16[132,512]{1,0:T(8,128)(2,1)S(1)} %add_convert_fusion.refs_0_), channel_id=1, source_target_pairs={{0,32},{32,64},{64,96},{96,128},{128,160},{160,192},{192,224},{224... | collective-permute-start | bytes 405512 | tf_op jit(solution)/shard_map/ppermute | solution.py:418
  59.9 63.2 %copy-start.6 = (bf16[132,512]{1,0:T(8,128)(2,1)}, bf16[132,512]{1,0:T(8,128)(2,1)S(1)}, u32[]{:S(2)}) copy-start(bf16[132,512]{1,0:T(8,128)(2,1)S(1)} %collective-permute-done.4.refs_2_) | copy-start | bytes 405508
  59.9 6.4 %collective-permute-start.6 = (bf16[132,512]{1,0:T(8,128)(2,1)S(1)}, bf16[132,512]{1,0:T(8,128)(2,1)S(1)}, u32[]{:S(2)}, u32[]{:S(2)}) collective-permute-start(bf16[132,512]{1,0:T(8,128)(2,1)S(1)} %collective-permute-done.4.refs_2_), channel_id=1, source_target_pairs={{0,224},{32,0},{64,32},{96,64},{128,96},{160,128},{192,160},{224,1... | collective-permute-start | bytes 405512 | tf_op jit(solution)/shard_map/ppermute | solution.py:418
  64.1 59.0 %copy-start.7 = (bf16[132,512]{1,0:T(8,128)(2,1)}, bf16[132,512]{1,0:T(8,128)(2,1)S(1)}, u32[]{:S(2)}) copy-start(bf16[132,512]{1,0:T(8,128)(2,1)S(1)} %collective-permute-done.3.refs_1_) | copy-start | bytes 405508
  64.1 6.3 %collective-permute-start.5 = (bf16[132,512]{1,0:T(8,128)(2,1)S(1)}, bf16[132,512]{1,0:T(8,128)(2,1)S(1)}, u32[]{:S(2)}, u32[]{:S(2)}) collective-permute-start(bf16[132,512]{1,0:T(8,128)(2,1)S(1)} %collective-permute-done.3.refs_1_), channel_id=1, source_target_pairs={{0,32},{32,64},{64,96},{96,128},{128,160},{160,192},{192,224},{224... | collective-permute-start | bytes 405512 | tf_op jit(solution)/shard_map/ppermute | solution.py:418
  66.2 56.8 %copy-start.8 = (bf16[132,512]{1,0:T(8,128)(2,1)}, bf16[132,512]{1,0:T(8,128)(2,1)S(1)}, u32[]{:S(2)}) copy-start(bf16[132,512]{1,0:T(8,128)(2,1)S(1)} %collective-permute-done.6.refs_4_) | copy-start | bytes 405508
  66.2 6.3 %collective-permute-start.8 = (bf16[132,512]{1,0:T(8,128)(2,1)S(1)}, bf16[132,512]{1,0:T(8,128)(2,1)S(1)}, u32[]{:S(2)}, u32[]{:S(2)}) collective-permute-start(bf16[132,512]{1,0:T(8,128)(2,1)S(1)} %collective-permute-done.6.refs_4_), channel_id=1, source_target_pairs={{0,224},{32,0},{64,32},{96,64},{128,96},{160,128},{192,160},{224,1... | collective-permute-start | bytes 405512 | tf_op jit(solution)/shard_map/ppermute | solution.py:418
  70.4 52.7 %copy-start.9 = (bf16[132,512]{1,0:T(8,128)(2,1)}, bf16[132,512]{1,0:T(8,128)(2,1)S(1)}, u32[]{:S(2)}) copy-start(bf16[132,512]{1,0:T(8,128)(2,1)S(1)} %collective-permute-done.5.refs_3_) | copy-start | bytes 405508
  70.4 6.3 %collective-permute-start.7 = (bf16[132,512]{1,0:T(8,128)(2,1)S(1)}, bf16[132,512]{1,0:T(8,128)(2,1)S(1)}, u32[]{:S(2)}, u32[]{:S(2)}) collective-permute-start(bf16[132,512]{1,0:T(8,128)(2,1)S(1)} %collective-permute-done.5.refs_3_), channel_id=1, source_target_pairs={{0,32},{32,64},{64,96},{96,128},{128,160},{160,192},{192,224},{224... | collective-permute-start | bytes 405512 | tf_op jit(solution)/shard_map/ppermute | solution.py:418
  72.5 50.6 %copy-start.4 = (bf16[132,512]{1,0:T(8,128)(2,1)}, bf16[132,512]{1,0:T(8,128)(2,1)S(1)}, u32[]{:S(2)}) copy-start(bf16[132,512]{1,0:T(8,128)(2,1)S(1)} %collective-permute-done.8.refs_6_) | copy-start | bytes 405508
  72.5 11.4 %collective-permute-start.10 = (bf16[68,512]{1,0:T(8,128)(2,1)S(1)}, bf16[68,512]{1,0:T(8,128)(2,1)S(1)}, u32[]{:S(2)}, u32[]{:S(2)}) collective-permute-start(bf16[68,512]{1,0:T(8,128)(2,1)S(1)} %slice.63), channel_id=1, source_target_pairs={{0,224},{32,0},{64,32},{96,64},{128,96},{160,128},{192,160},{224,1... | collective-permute-start | bytes 208904 | tf_op jit(solution)/shard_map/ppermute | solution.py:418
  76.6 46.5 %copy-start.5 = (bf16[132,512]{1,0:T(8,128)(2,1)}, bf16[132,512]{1,0:T(8,128)(2,1)S(1)}, u32[]{:S(2)}) copy-start(bf16[132,512]{1,0:T(8,128)(2,1)S(1)} %collective-permute-done.7.refs_5_) | copy-start | bytes 405508
  76.6 7.3 %collective-permute-start.9 = (bf16[64,512]{1,0:T(8,128)(2,1)S(1)}, bf16[64,512]{1,0:T(8,128)(2,1)S(1)}, u32[]{:S(2)}, u32[]{:S(2)}) collective-permute-start(bf16[64,512]{1,0:T(8,128)(2,1)S(1)} %slice.62), channel_id=1, source_target_pairs={{0,32},{32,64},{64,96},{96,128},{128,160},{160,192},{192,224},{224... | collective-permute-start | bytes 196616 | tf_op jit(solution)/shard_map/ppermute | solution.py:418
  76.7 39.0 %collective-permute-start.12 = (bf16[2048,256]{1,0:T(8,128)(2,1)S(1)}, bf16[2048,256]{1,0:T(8,128)(2,1)}, u32[]{:S(2)}, u32[]{:S(2)}) collective-permute-start(bf16[2048,256]{1,0:T(8,128)(2,1)S(1)} %bitcast.67), channel_id=1, source_target_pairs={{0,4},{1,5},{6,2},{7,3},{8,12},{9,13},{14,10},{15,11},{16,20},{17,... | collective-permute-start | bytes 3145736 | tf_op jit(solution)/shard_map/ppermute | solution.py:409
  79.1 38.9 %collective-permute-start.11 = (bf16[2048,256]{1,0:T(8,128)(2,1)S(1)}, bf16[2048,256]{1,0:T(8,128)(2,1)}, u32[]{:S(2)}, u32[]{:S(2)}) collective-permute-start(bf16[2048,256]{1,0:T(8,128)(2,1)S(1)} %bitcast.68), channel_id=1, source_target_pairs={{0,1},{1,0},{2,5},{3,4},{6,7},{7,6},{5,2},{4,3},{8,9},{9,8},{10,13... | collective-permute-start | bytes 3145736 | tf_op jit(solution)/shard_map/ppermute | solution.py:408
  80.2 37.9 %collective-permute-start.17 = (bf16[2048,256]{1,0:T(8,128)(2,1)}, bf16[2048,256]{1,0:T(8,128)(2,1)}, u32[]{:S(2)}, u32[]{:S(2)}) collective-permute-start(bf16[2048,256]{1,0:T(8,128)(2,1)} %bitcast.28.refs_6_), channel_id=1, source_target_pairs={{0,4},{1,5},{6,2},{7,3},{8,12},{9,13},{14,10},{15,11},{16,20},{17,... | collective-permute-start | bytes 3145736 | tf_op jit(solution)/shard_map/ppermute | solution.py:409
  84.0 39.1 %copy-start.11 = (bf16[64,512]{1,0:T(8,128)(2,1)}, bf16[64,512]{1,0:T(8,128)(2,1)S(1)}, u32[]{:S(2)}) copy-start(bf16[64,512]{1,0:T(8,128)(2,1)S(1)} %collective-permute-done.9.refs_7_) | copy-start | bytes 196612
  84.0 35.8 %collective-permute-start.16 = (bf16[2048,256]{1,0:T(8,128)(2,1)}, bf16[2048,256]{1,0:T(8,128)(2,1)}, u32[]{:S(2)}, u32[]{:S(2)}) collective-permute-start(bf16[2048,256]{1,0:T(8,128)(2,1)} %bitcast.28.refs_6_), channel_id=1, source_target_pairs={{0,1},{1,0},{2,5},{3,4},{6,7},{7,6},{5,2},{4,3},{8,9},{9,8},{10,13... | collective-permute-start | bytes 3145736 | tf_op jit(solution)/shard_map/ppermute | solution.py:408
  84.0 39.1 %copy-start.10 = (bf16[68,512]{1,0:T(8,128)(2,1)}, bf16[68,512]{1,0:T(8,128)(2,1)S(1)}, u32[]{:S(2)}) copy-start(bf16[68,512]{1,0:T(8,128)(2,1)S(1)} %collective-permute-done.10.refs_8_) | copy-start | bytes 208900
  84.0 37.4 %collective-permute-start.21 = (bf16[256,2048]{1,0:T(8,128)(2,1)}, bf16[256,2048]{1,0:T(8,128)(2,1)}, u32[]{:S(2)}, u32[]{:S(2)}) collective-permute-start(bf16[256,2048]{1,0:T(8,128)(2,1)} %bitcast.29.refs_12_), channel_id=1, source_target_pairs={{0,1},{1,0},{2,5},{3,4},{6,7},{7,6},{5,2},{4,3},{8,9},{9,8},{10,13... | collective-permute-start | bytes 3145736 | tf_op jit(solution)/shard_map/ppermute | solution.py:408
  114.3 14.0 %copy-start.1 = (bf16[8,132,64]{1,2,0:T(8,128)(2,1)}, bf16[8,132,64]{1,2,0:T(8,128)(2,1)S(1)}, u32[]{:S(2)}) copy-start(bf16[8,132,64]{1,2,0:T(8,128)(2,1)S(1)} %all-gather.2) | copy-start | bytes 405508
  115.8 22.5 %collective-permute-start.22 = (bf16[256,2048]{1,0:T(8,128)(2,1)}, bf16[256,2048]{1,0:T(8,128)(2,1)}, u32[]{:S(2)}, u32[]{:S(2)}) collective-permute-start(bf16[256,2048]{1,0:T(8,128)(2,1)} %bitcast.29.refs_12_), channel_id=1, source_target_pairs={{0,4},{1,5},{6,2},{7,3},{8,12},{9,13},{14,10},{15,11},{16,20},{17,... | collective-permute-start | bytes 3145736 | tf_op jit(solution)/shard_map/ppermute | solution.py:409
  118.0 20.7 %collective-permute-start.14 = (bf16[2048,256]{1,0:T(8,128)(2,1)}, bf16[2048,256]{1,0:T(8,128)(2,1)S(1)}, u32[]{:S(2)}, u32[]{:S(2)}) collective-permute-start(bf16[2048,256]{1,0:T(8,128)(2,1)} %collective-permute-done.11.refs_1_), channel_id=1, source_target_pairs={{0,4},{1,5},{2,6},{3,7},{4,0},{5,1},{6,2},{7,3},{8,12},{9,13},{10,... | collective-permute-start | bytes 3145736 | tf_op jit(solution)/shard_map/ppermute | solution.py:411
  118.0 20.9 %collective-permute-start.13 = (bf16[2048,256]{1,0:T(8,128)(2,1)}, bf16[2048,256]{1,0:T(8,128)(2,1)}, u32[]{:S(2)}, u32[]{:S(2)}) collective-permute-start(bf16[2048,256]{1,0:T(8,128)(2,1)} %collective-permute-done.11.refs_1_), channel_id=1, source_target_pairs={{4,5},{5,4},{2,3},{3,2},{12,13},{13,12},{10,11},{11,10},{20,21},{2... | collective-permute-start | bytes 3145736 | tf_op jit(solution)/shard_map/ppermute | solution.py:410
  119.8 20.5 %collective-permute-start.18 = (bf16[2048,256]{1,0:T(8,128)(2,1)}, bf16[2048,256]{1,0:T(8,128)(2,1)}, u32[]{:S(2)}, u32[]{:S(2)}) collective-permute-start(bf16[2048,256]{1,0:T(8,128)(2,1)} %collective-permute-done.16.refs_7_), channel_id=1, source_target_pairs={{4,5},{5,4},{2,3},{3,2},{12,13},{13,12},{10,11},{11,10},{20,21},{2... | collective-permute-start | bytes 3145736 | tf_op jit(solution)/shard_map/ppermute | solution.py:410
  121.4 20.1 %collective-permute-start.23 = (bf16[256,2048]{1,0:T(8,128)(2,1)}, bf16[256,2048]{1,0:T(8,128)(2,1)}, u32[]{:S(2)}, u32[]{:S(2)}) collective-permute-start(bf16[256,2048]{1,0:T(8,128)(2,1)} %collective-permute-done.21.refs_13_), channel_id=1, source_target_pairs={{4,5},{5,4},{2,3},{3,2},{12,13},{13,12},{10,11},{11,10},{20,21},{2... | collective-permute-start | bytes 3145736 | tf_op jit(solution)/shard_map/ppermute | solution.py:410
  128.3 14.6 %copy-start.15 = (s32[64]{0:T(128)S(1)}, s32[64]{0:T(128)}, u32[]{:S(2)}) copy-start(s32[64]{0:T(128)} %param.24) | copy-start | bytes 772
  128.3 53.9 %all-to-all-start = ((bf16[32,64,512]{2,1,0:T(8,128)(2,1)}), bf16[32,64,512]{2,1,0:T(8,128)(2,1)S(1)}, u32[]{:S(2)}, u32[]{:S(2)}) async-start(bf16[32,64,512]{2,1,0:T(8,128)(2,1)} %expand.1), calls=%async_computation | async-start | bytes 4194304 | tf_op jit(solution)/shard_map/all_to_all | solution.py:520
  137.6 34.2 %all-gather.5.cloned.1.call-start = ((), (), s32[]{:S(2)}) async-start(), calls=%async_computation.4 | async-start | bytes 2359296 | tf_op jit(solution)/shard_map/all_gather | solution.py:470
  138.3 43.9 %collective-permute-start.19 = (bf16[2048,256]{1,0:T(8,128)(2,1)}, bf16[2048,256]{1,0:T(8,128)(2,1)}, u32[]{:S(2)}, u32[]{:S(2)}) collective-permute-start(bf16[2048,256]{1,0:T(8,128)(2,1)} %collective-permute-done.16.refs_7_), channel_id=1, source_target_pairs={{0,4},{1,5},{2,6},{3,7},{4,0},{5,1},{6,2},{7,3},{8,12},{9,13},{10,... | collective-permute-start | bytes 3145736 | tf_op jit(solution)/shard_map/ppermute | solution.py:411
  138.7 37.4 %copy-start.14 = (bf16[2048,256]{1,0:T(8,128)(2,1)}, bf16[2048,256]{1,0:T(8,128)(2,1)S(1)}, u32[]{:S(2)}) copy-start(bf16[2048,256]{1,0:T(8,128)(2,1)S(1)} %collective-permute-done.14.refs_4_) | copy-start | bytes 3145732
  138.7 43.5 %collective-permute-start.24 = (bf16[256,2048]{1,0:T(8,128)(2,1)}, bf16[256,2048]{1,0:T(8,128)(2,1)}, u32[]{:S(2)}, u32[]{:S(2)}) collective-permute-start(bf16[256,2048]{1,0:T(8,128)(2,1)} %collective-permute-done.21.refs_13_), channel_id=1, source_target_pairs={{0,4},{1,5},{2,6},{3,7},{4,0},{5,1},{6,2},{7,3},{8,12},{9,13},{10,... | collective-permute-start | bytes 3145736 | tf_op jit(solution)/shard_map/ppermute | solution.py:411
  138.9 43.3 %collective-permute-start.15 = (bf16[2048,256]{1,0:T(8,128)(2,1)}, bf16[2048,256]{1,0:T(8,128)(2,1)}, u32[]{:S(2)}, u32[]{:S(2)}) collective-permute-start(bf16[2048,256]{1,0:T(8,128)(2,1)} %collective-permute-done.13.refs_3_), channel_id=1, source_target_pairs={{4,0},{5,1},{2,6},{3,7},{12,8},{13,9},{10,14},{11,15},{20,16},{21,... | collective-permute-start | bytes 3145736 | tf_op jit(solution)/shard_map/ppermute | solution.py:412
  140.2 42.0 %collective-permute-start.20 = (bf16[2048,256]{1,0:T(8,128)(2,1)}, bf16[2048,256]{1,0:T(8,128)(2,1)}, u32[]{:S(2)}, u32[]{:S(2)}) collective-permute-start(bf16[2048,256]{1,0:T(8,128)(2,1)} %collective-permute-done.18.refs_9_), channel_id=1, source_target_pairs={{4,0},{5,1},{2,6},{3,7},{12,8},{13,9},{10,14},{11,15},{20,16},{21,... | collective-permute-start | bytes 3145736 | tf_op jit(solution)/shard_map/ppermute | solution.py:412
  141.5 40.7 %collective-permute-start.25 = (bf16[256,2048]{1,0:T(8,128)(2,1)}, bf16[256,2048]{1,0:T(8,128)(2,1)}, u32[]{:S(2)}, u32[]{:S(2)}) collective-permute-start(bf16[256,2048]{1,0:T(8,128)(2,1)} %collective-permute-done.23.refs_15_), channel_id=1, source_target_pairs={{4,0},{5,1},{2,6},{3,7},{12,8},{13,9},{10,14},{11,15},{20,16},{21,... | collective-permute-start | bytes 3145736 | tf_op jit(solution)/shard_map/ppermute | solution.py:412
  182.2 1.3 copy-start.2
  203.9 33.0 %all-to-all-start.1 = ((bf16[32,64,512]{2,1,0:T(8,128)(2,1)}), bf16[32,64,512]{2,1,0:T(8,128)(2,1)S(1)}, u32[]{:S(2)}, u32[]{:S(2)}) async-start(bf16[32,64,512]{2,1,0:T(8,128)(2,1)} %bitcast.53), calls=%async_computation.1 | async-start | bytes 4194304 | tf_op jit(solution)/shard_map/all_to_all | solution.py:544
  209.4 71.7 %reduce-scatter.2.cloned.1.call-start = ((), (), s32[]{:S(2)}) async-start(), calls=%async_computation.3 | async-start | bytes 1253376 | tf_op jit(solution)/shard_map/reduce_scatter | solution.py:550
  236.9 1.3 copy-start
Sparse Core Ops, SparseCore 0:
  140.3 31.4 all-gather.4
  243.8 37.2 reduce-scatter.1

commit v2 on v1

--- a/solution.py
+++ b/solution.py
@@ -17,6 +17,7 @@
 COLS = 512
 FULL = 2048
 EXPERTS = 64
+LANES = 128
 CAP = 32
 PLANES = 8
 TP = 4
@@ -160,11 +161,11 @@
 
 
 def pair_onehot(code, plane, second):
-    place = iota((EXPERTS, PAIR_LANES), 1)
+    place = iota((LANES, PAIR_LANES), 1)
     device = place >> 4
     x, c, y = device & 3, (device >> 2) & 1, device >> 3
     expert = plane * PLANES + y * 2 + (x >> 1)
-    spread = (iota((EXPERTS, PAIR_LANES), 0) == expert).astype(F32).astype(BF)
+    spread = (iota((LANES, PAIR_LANES), 0) == expert).astype(F32).astype(BF)
     slot = dot(slot_part(code).astype(BF), spread)
     place = iota((1, PAIR_LANES), 1)
     device = place >> 4
@@ -226,7 +227,7 @@
         in_specs=[
             SM,
             SM,
-            pl.BlockSpec((EXPERTS, ROWS, EXPERTS), lambda p: (0, 0, 0)),
+            pl.BlockSpec((EXPERTS, ROWS, LANES), lambda p: (0, 0, 0)),
             pl.BlockSpec((32, 16, COLS), lambda p: (0, p, 0)),
         ],
         out_specs=pl.BlockSpec((2, ROWS, COLS), lambda p: (p, 0, 0)),
@@ -241,12 +242,12 @@
 
 def chosen_kernel(numbers, code, out):
     plane, expert, quarter = numbers[0], numbers[1], numbers[2]
-    is_expert = iota((ROWS, EXPERTS), 1) == expert
+    is_expert = iota((ROWS, LANES), 1) == expert
     place = iota((1, 64), 1)
     wanted = quarter * QUARTER + (place & 7) + 1
 
     def one(column, carry):
-        filled = jnp.zeros((64, EXPERTS), F32)
+        filled = jnp.zeros((64, LANES), F32)
         for position in range(PLANES):
             z = (plane + NEAR[position] + PLANES) % PLANES
             rows = code[column * PLANES + z]
@@ -267,7 +268,7 @@
         chosen_kernel,
         in_specs=[SM, VM],
         out_specs=VM,
-        out_shape=jax.ShapeDtypeStruct((PLANES, 64, EXPERTS), F32),
+        out_shape=jax.ShapeDtypeStruct((PLANES, 64, LANES), F32),
         compiler_params=pltpu.CompilerParams(vmem_limit_bytes=VMEM_LIMIT),
         cost_estimate=pl.CostEstimate(
             flops=200_000_000, bytes_accessed=2_000_000, transcendentals=0
@@ -278,8 +279,24 @@
 
 def expert_kernel(numbers, arrived, codes, origin, gain, router, *refs):
     parts, out = refs[:18], refs[18]
-    weights, sems = refs[19:22], refs[22]
+    weights, normed, hidden, sems = refs[19:22], refs[22], refs[23], refs[24]
     at_home = numbers[3]
+
+    def place(kind, quarter):
+        if kind < 2:
+            return weights[kind].at[quarter]
+        return weights[2].at[quarter * 256 : (quarter + 1) * 256]
+
+    def bring(source, kind, quarter):
+        pltpu.make_async_copy(
+            source, place(kind, quarter), sems.at[kind, quarter]
+        ).start()
+
+    def arrival(kind, quarter):
+        return pltpu.make_async_copy(
+            parts[6 * kind + 1], place(kind, quarter), sems.at[kind, quarter]
+        )
+
     for kind in range(3):
         own, first, other_own, second, other_first, other_second = parts[
             6 * kind : 6 * kind + 6
@@ -287,37 +304,28 @@
 
         @pl.when(at_home == 1)
         def _():
-            pltpu.make_async_copy(own, weights[kind].at[0], sems.at[kind, 0]).start()
-            pltpu.make_async_copy(
-                other_second, weights[kind].at[3], sems.at[kind, 3]
-            ).start()
+            bring(own, kind, 0)
+            bring(other_second, kind, 3)
 
         @pl.when(at_home == 0)
         def _():
-            pltpu.make_async_copy(
-                other_own, weights[kind].at[0], sems.at[kind, 0]
-            ).start()
-            pltpu.make_async_copy(second, weights[kind].at[3], sems.at[kind, 3]).start()
-
-        pltpu.make_async_copy(first, weights[kind].at[1], sems.at[kind, 1]).start()
-        pltpu.make_async_copy(
-            other_first, weights[kind].at[2], sems.at[kind, 2]
-        ).start()
-
-    wide = []
+            bring(other_own, kind, 0)
+            bring(second, kind, 3)
+
+        bring(first, kind, 1)
+        bring(other_first, kind, 2)
+
     squares = jnp.zeros((512, 1), F32)
     for x in range(TP):
         part = arrived[:, x].reshape(512, COLS).astype(F32)
         squares = squares + jnp.sum(part * part, axis=1, keepdims=True)
     scale = lax.rsqrt(squares / FULL + 1e-05)
-    logits = jnp.zeros((512, EXPERTS), F32)
     for x in range(TP):
         span = slice(x * COLS, (x + 1) * COLS)
         part = arrived[:, x].reshape(512, COLS).astype(F32)
-        normed = (part * scale * gain[:, span]).astype(BF)
-        wide.append(normed)
-        logits = logits + dot(normed, router[:, span], 1, 1)
-    code = codes[...].reshape(512, EXPERTS)
+        normed[:, span] = (part * scale * gain[:, span]).astype(BF)
+    logits = dot(normed[...], router[...], 1, 1)
+    code = codes[...].reshape(512, LANES)[:, :EXPERTS]
     chosen = code > 0.0
     is_expert = iota((512, EXPERTS), 1) == numbers[1]
     top = jnp.max(jnp.where(chosen, logits, jnp.finfo(F32).min), axis=1, keepdims=True)
@@ -328,28 +336,22 @@
     mark = jnp.sum(jnp.where(is_expert, code, 0.0), axis=1, keepdims=True)
     first_choice = (mark > 64.0).astype(F32)
 
-    total = None
     for quarter in range(4):
-        for kind in range(3):
-            source = parts[6 * kind + 1]
-            pltpu.make_async_copy(
-                source, weights[kind].at[quarter], sems.at[kind, quarter]
-            ).wait()
-        gate_pre = jnp.zeros((512, 256), F32)
-        up_pre = jnp.zeros((512, 256), F32)
-        for x in range(TP):
-            span = slice(x * COLS, (x + 1) * COLS)
-            gate_pre = gate_pre + dot(wide[x], weights[0][quarter, span, :])
-            up_pre = up_pre + dot(wide[x], weights[1][quarter, span, :])
-        hidden = (gate_pre / (1.0 + jnp.exp(-gate_pre)) * up_pre).astype(BF)
-        term = dot(hidden, weights[2][quarter])
-        total = term if total is None else total + term
-    result = total.astype(BF).astype(F32) * gate
+        for kind in range(2):
+            arrival(kind, quarter).wait()
+        gate_pre = dot(normed[...], weights[0][quarter])
+        up_pre = dot(normed[...], weights[1][quarter])
+        hidden[:, quarter * 256 : (quarter + 1) * 256] = (
+            gate_pre / (1.0 + jnp.exp(-gate_pre)) * up_pre
+        ).astype(BF)
+    for quarter in range(4):
+        arrival(2, quarter).wait()
     move = (origin[...] == iota((512, 512), 1)).astype(F32).astype(BF)
     for x in range(TP):
         span = slice(x * COLS, (x + 1) * COLS)
         part = arrived[:, x].reshape(512, COLS).astype(F32)
-        piece = (result[:, span] + first_choice * part).astype(BF)
+        result = dot(hidden[...], weights[2][:, span]).astype(BF).astype(F32) * gate
+        piece = (result + first_choice * part).astype(BF)
         out[:, x] = dot(move, piece).astype(BF).reshape(PLANES, 64, COLS)
 
 
@@ -362,7 +364,9 @@
         scratch_shapes=[
             pltpu.VMEM((4, FULL, 256), BF),
             pltpu.VMEM((4, FULL, 256), BF),
-            pltpu.VMEM((4, 256, FULL), BF),
+            pltpu.VMEM((1024, FULL), BF),
+            pltpu.VMEM((512, FULL), BF),
+            pltpu.VMEM((512, 1024), BF),
             pltpu.SemaphoreType.DMA((3, 4)),
         ],
         compiler_params=pltpu.CompilerParams(vmem_limit_bytes=VMEM_LIMIT),
@@ -402,15 +406,11 @@
     )
 
 
-def gathered_weight(own):
-    first_move, second_move, out_of_home, both, to_home = pair_moves()
-    axes = ("c", "tp")
-    first = lax.ppermute(own, axes, first_move)
-    other_own = lax.ppermute(own, axes, out_of_home)
-    second = lax.ppermute(first, axes, second_move)
-    other_first = lax.ppermute(first, axes, both)
-    other_second = lax.ppermute(second, axes, to_home)
-    return [own, first, other_own, second, other_first, other_second]
+PAIR = ("c", "tp")
+
+
+def tied(*values):
+    return lax.optimization_barrier(values)
 
 
 def around(value, axis, step):
@@ -418,12 +418,14 @@
     return lax.ppermute(value, axis, [(i, (i + step) % count) for i in range(count)])
 
 
-def gather_column(value):
+def gather_column(value, code):
     up = [value]
     down = [value]
-    for _ in range(3):
+    for step in range(3):
         up.append(around(up[-1], "z", 1))
         down.append(around(down[-1], "z", -1))
+        if step == 1:
+            up[2], down[2], code = tied(up[2], down[2], code)
     return [
         value,
         up[1],
@@ -434,7 +436,7 @@
         down[3],
         around(up[3][:64], "z", 1),
         around(down[3][64:], "z", -1),
-    ]
+    ], code
 
 
 def per_device(
@@ -458,28 +460,27 @@
     z, y, c, tp = (lax.axis_index(name) for name in ("z", "y", "c", "tp"))
     column = y * 2 + c
 
-    every = jnp.arange(EXPERTS, dtype=jnp.int32)
-    chosen = jnp.zeros((ROWS, EXPERTS), jnp.bool_)
+    every = jnp.arange(LANES, dtype=jnp.int32)
+    chosen = jnp.zeros((ROWS, LANES), jnp.bool_)
     for k in range(expert_ids.shape[1]):
         chosen = chosen | (expert_ids[:, k : k + 1] == every[None, :])
     below = jnp.arange(ROWS)[:, None] >= jnp.arange(ROWS)[None, :]
     slot = dot(below.astype(BF), chosen.astype(BF))
     first_choice = expert_ids[:, :1] == every[None, :]
     code = jnp.where(chosen, slot + 64.0 * first_choice, 0.0).astype(BF)
-    code_column = lax.all_gather(code, "z", axis=0)
-    code_all = lax.all_gather(code_column, ("y", "c"), axis=0).reshape(
-        EXPERTS, ROWS, EXPERTS
-    )
-
-    parts = (
-        gathered_weight(gate_weight[0])
-        + gathered_weight(up_weight[0])
-        + gathered_weight(down_weight[0])
-    )
+    widened = jnp.concatenate([code] + [jnp.zeros_like(code)] * 3, axis=1)
+    code_column = lax.all_gather(widened, "z", axis=0)
+
+    first_move, second_move, out_of_home, both, to_home = pair_moves()
+    owns = [gate_weight[0], up_weight[0], down_weight[0]]
+    firsts = [lax.ppermute(own, PAIR, first_move) for own in owns]
 
     proj = jnp.transpose(projected, (1, 0, 2))
     raw = proj[:2].astype(F32)
-    squares = lax.psum(jnp.sum(raw * raw, axis=2), "tp")
+    squares = jnp.sum(raw * raw, axis=2)
+    shared = [around(squares, "tp", step) for step in range(1, TP)]
+    squares = squares + shared[0] + shared[1] + shared[2]
+    squares, firsts[0] = tied(squares, firsts[0])
     inv = lax.rsqrt(squares / FULL + 1e-05).T
     spot = jnp.arange(ROWS, dtype=jnp.int32)
     positions = offsets[0] + spot
@@ -504,18 +505,36 @@
         decode_cache,
         out_weight,
     )
+    *sends, firsts[1], firsts[2] = tied(*sends, firsts[1], firsts[2])
+    seconds = [lax.ppermute(first, PAIR, second_move) for first in firsts]
     state = own
     for step in range(1, TP):
         state = state + around(sends[step - 1], "tp", step).astype(F32)
     residual_here = lax.dynamic_slice_in_dim(residual, tp * COLS, COLS, 1)
     state = (residual_here.astype(F32) + state).astype(BF)
+    column_states, code_column = gather_column(state, code_column)
+    code_column = code_column[:, :, :LANES]
+    code_all = lax.all_gather(code_column, ("y", "c"), axis=0).reshape(
+        EXPERTS, ROWS, LANES
+    )
 
     serves = y * 2 + tp // 2
     quarter = (tp % 2) * 2 + c
     at_home = (tp // 2 == c).astype(jnp.int32)
     numbers = jnp.stack([z, z * PLANES + serves, quarter, at_home]).astype(jnp.int32)
     codes = chosen_rows(numbers, code_all)
-    outgoing = expand(numbers, code_column, gather_column(state))
+    outgoing = expand(numbers, code_column, column_states)
+    outgoing, *seconds = tied(outgoing, *seconds)
+    parts = []
+    for own, first, second in zip(owns, firsts, seconds, strict=True):
+        parts += [
+            own,
+            first,
+            lax.ppermute(own, PAIR, out_of_home),
+            second,
+            lax.ppermute(first, PAIR, both),
+            lax.ppermute(second, PAIR, to_home),
+        ]
     plane = ("y", "c", "tp")
     arrived = lax.all_to_all(outgoing, plane, split_axis=0, concat_axis=0, tiled=True)
 
@@ -547,7 +566,9 @@
     mine = lax.dynamic_index_in_dim(source, column, 0, keepdims=False)
     rows_in_code = (mine % PLANES) * PLANES + mine // PLANES
     sums = combine(numbers, rows_in_code, code_all, answers)
-    return lax.psum_scatter(sums, "z", scatter_dimension=0)
+    return lax.psum_scatter(
+        sums.reshape(PLANES * ROWS, COLS), "z", scatter_dimension=0, tiled=True
+    )
 
 
 def solution(mesh):

time: 290 us -> 260 us (0.90)
  blocking collectives: 45.9 us -> 25 us
  waiting for transfers between devices: 106 us -> 88.3 us
  starting transfers between devices: 53.4 us -> 61.2 us
  local copies, waits for them, and re-layouts: 10.6 us -> 16.4 us
  Pallas kernels: 48.6 us -> 43.4 us
    reduce_scatter x1 -> x0, waiting for transfers between devices: 37.4 us -> none  [per_device(): return lax.psum_scatter(sums, 'z', scatter_dimension=0)]
    ppermute x11 -> x14, waiting for transfers between devices: 13.4 us -> 47.9 us  [around(): lax.ppermute(value, axis, [(i, (i + step) % count) for i in range(count)])]
    all_gather x1 -> x0, blocking collectives: 28.1 us -> none  [per_device(): code_column = lax.all_gather(code, 'z', axis=0)]
    all_gather x1, waiting for transfers between devices: 27.7 us -> 0.01 us  [per_device(): lax.all_gather(code_column, ('y', 'c'), axis=0)]
    unnamed x0 -> x1, blocking collectives: none -> 25 us
    psum x1 -> x0, blocking collectives: 17.8 us -> none  [per_device(): squares = lax.psum(jnp.sum(raw * raw, axis=2), 'tp')]
    all_to_all x1, waiting for transfers between devices: 0.01 us -> 11 us  [per_device(): lax.all_to_all(outgoing, plane, split_axis=0, concat_axis=0, tiled=True)]
    pallas_call x1, Pallas kernels: 20.4 us -> 15 us  [expert(): pl.pallas_call(expert_kernel, in_specs=[SM] + [VM] * 5 + [HB] * 18, out_s...]
  transfers between devices with their start and end apart: 30 -> 34, of which waited for: 11 -> 14; matrix products, arithmetic and copies ran while one was open for 3% -> 7% of each run, Pallas kernels for 4% -> 9%
where the time goes in v2:
time: 260 us; the launch traced here: 259 us
  waiting for transfers between devices  88.3 us (34%)
  starting transfers between devices  61.2 us (24%)
  Pallas kernels  43.4 us (17%)
  blocking collectives  25 us (10%)
  local copies, waits for them, and re-layouts  16.4 us (6%)
  between operations  15.1 us (6%)
  other arithmetic  9.19 us (4%)
    ppermute x14, waiting for transfers between devices, around(): lax.ppermute(value, axis, [(i, (i + step) % count) for i in range(count)])  47.9 us
    all_to_all x1, waiting for transfers between devices, per_device(): lax.all_to_all(result.reshape(32, 64, COLS), plane, split_axis=0, concat_...  26.8 us
    unnamed x1, blocking collectives  25 us
    ppermute x14, starting transfers between devices, around(): lax.ppermute(value, axis, [(i, (i + step) % count) for i in range(count)])  19 us
    pallas_call x1, Pallas kernels, expert(): pl.pallas_call(expert_kernel, in_specs=[SM] + [VM] * 5 + [HB] * 18, out_s...  15 us
    all_to_all x1, starting transfers between devices, per_device(): lax.all_to_all(outgoing, plane, split_axis=0, concat_axis=0, tiled=True)  14.4 us
    pallas_call x1, Pallas kernels, attention(): pl.pallas_call(attention_kernel, grid=(HEADS_HERE,), in_specs=[SM, pl.Blo...  11.6 us
    all_to_all x1, waiting for transfers between devices, per_device(): lax.all_to_all(outgoing, plane, split_axis=0, concat_axis=0, tiled=True)  11 us
  transfers between devices with their start and end apart: 34, of which 14 were waited for; matrix products, arithmetic and copies ran while one was open for 7% of the time, Pallas kernels for 9%

profile of v2, /device:TPU:32, one launch (start us, length us, event | category | flops | bytes accessed | tf_op | source)
XLA Modules:
  0.0 259.1 jit_solution(15588400447026694736)
XLA Ops:
  6.5 1.1 multiply_reduce_fusion
  7.8 2.8 %collective-permute-start.2 = (f32[2,132]{0,1:T(8,128)S(1)}, f32[2,132]{0,1:T(8,128)S(1)}, u32[]{:S(2)}, u32[]{:S(2)}) collective-permute-start(f32[2,132]{0,1:T(8,128)S(1)} %copy.30), channel_id=1, source_target_pairs={{0,3},{1,0},{2,1},{3,2},{4,7},{5,4},{6,5},{7,6},{8,11},{9,8},{10,9... | collective-permute-start | bytes 3176 | tf_op jit(solution)/shard_map/ppermute | solution.py:418
  10.6 0.8 collective-permute-start.1
  11.4 0.9 collective-permute-start.3
  12.3 1.1 collective-permute-start.4
  13.4 0.9 collective-permute-start.5
  14.3 1.1 fusion.32
  15.8 0.7 pad_bitcast_fusion
  16.6 1.5 fusion.33
  18.7 2.5 fusion.29
  21.5 0.8 pad_maximum_fusion
  22.3 1.1 collective-permute-start
  23.5 1.3 pad_add_fusion.1.numbers
  24.7 26.5 %collective-permute-done = f32[2,132]{0,1:T(8,128)S(1)} collective-permute-done((f32[2,132]{0,1:T(8,128)S(1)}, f32[2,132]{0,1:T(8,128)S(1)}, u32[]{:S(2)}, u32[]{:S(2)}) %collective-permute-start) | collective-permute-done | bytes 1088 | tf_op jit(solution)/shard_map/ppermute | solution.py:418
  51.2 0.7 rsqrt_bitcast_fusion.inv
  52.0 11.6 %attention.1 = (f32[132,512]{1,0:T(8,128)}, bf16[132,512]{1,0:T(8,128)(2,1)}, bf16[132,512]{1,0:T(8,128)(2,1)}, bf16[132,512]{1,0:T(8,128)(2,1)}) custom-call(s32[6]{0:T(128)} %pad_add_fusion.1.numbers, bf16[3,132,512]{2,1,0:T(8,128)(2,1)} %bitcast.57, f32[132,2]{1,0:T(8,128)} %rsqrt_bitcast_fusion.inv, f32[132,128]{1,0:T(8,128)} %get-tuple-element.56.cosine, ...), custom_call_target="tpu_custom_call" | custom-call | flops 2000000000 | bytes 10000000 | tf_op jit(solution)/shard_map/attention/pallas_call | solution.py:131
  63.7 2.1 collective-permute-start.7
  65.8 4.3 %collective-permute-done.8 = bf16[132,512]{1,0:T(8,128)(2,1)S(1)} collective-permute-done((bf16[132,512]{1,0:T(8,128)(2,1)}, bf16[132,512]{1,0:T(8,128)(2,1)S(1)}, u32[]{:S(2)}, u32[]{:S(2)}) %collective-permute-start.8) | collective-permute-done | bytes 135200 | tf_op jit(solution)/shard_map/ppermute | solution.py:418
  70.1 1.9 collective-permute-done.7
  72.0 2.1 collective-permute-done.6
  74.2 1.1 add_convert_fusion.refs_0_
  75.3 1.6 collective-permute-start.9
  76.9 0.5 collective-permute-start.11
  77.4 3.5 %collective-permute-done.9.refs_1_ = bf16[132,512]{1,0:T(8,128)(2,1)S(1)} collective-permute-done((bf16[132,512]{1,0:T(8,128)(2,1)S(1)}, bf16[132,512]{1,0:T(8,128)(2,1)S(1)}, u32[]{:S(2)}, u32[]{:S(2)}) %collective-permute-start.9) | collective-permute-done | bytes 135200 | tf_op jit(solution)/shard_map/ppermute | solution.py:418
  80.8 1.4 collective-permute-start.10
  82.7 2.7 %collective-permute-start.12 = (bf16[132,512]{1,0:T(8,128)(2,1)S(1)}, bf16[132,512]{1,0:T(8,128)(2,1)S(1)}, u32[]{:S(2)}, u32[]{:S(2)}) collective-permute-start(bf16[132,512]{1,0:T(8,128)(2,1)S(1)} %collective-permute-done.11.refs_2_), channel_id=1, source_target_pairs={{0,224},{32,0},{64,32},{96,64},{128,96},{160,128},{192,160},{224,1... | collective-permute-start | bytes 405512 | tf_op jit(solution)/shard_map/ppermute | solution.py:418
  85.3 2.9 %collective-permute-done.10.refs_3_ = bf16[132,512]{1,0:T(8,128)(2,1)S(1)} collective-permute-done((bf16[132,512]{1,0:T(8,128)(2,1)S(1)}, bf16[132,512]{1,0:T(8,128)(2,1)S(1)}, u32[]{:S(2)}, u32[]{:S(2)}) %collective-permute-start.10) | collective-permute-done | bytes 135200 | tf_op jit(solution)/shard_map/ppermute | solution.py:418
  88.3 0.5 collective-permute-done.12.refs_4_
  88.8 1.0 slice.62.code
  89.9 0.8 copy.33
  90.7 1.7 collective-permute-start.17
  92.4 1.6 collective-permute-start.18
  94.0 1.7 collective-permute-start.19
  95.7 3.2 %collective-permute-start.13 = (bf16[132,512]{1,0:T(8,128)(2,1)S(1)}, bf16[132,512]{1,0:T(8,128)(2,1)S(1)}, u32[]{:S(2)}, u32[]{:S(2)}) collective-permute-start(bf16[132,512]{1,0:T(8,128)(2,1)S(1)} %collective-permute-done.10.refs_3_), channel_id=1, source_target_pairs={{0,32},{32,64},{64,96},{96,128},{128,160},{160,192},{192,224},{224... | collective-permute-start | bytes 405512 | tf_op jit(solution)/shard_map/ppermute | solution.py:418
  98.9 3.7 %collective-permute-done.13.refs_5_ = bf16[132,512]{1,0:T(8,128)(2,1)S(1)} collective-permute-done((bf16[132,512]{1,0:T(8,128)(2,1)S(1)}, bf16[132,512]{1,0:T(8,128)(2,1)S(1)}, u32[]{:S(2)}, u32[]{:S(2)}) %collective-permute-start.13) | collective-permute-done | bytes 135200 | tf_op jit(solution)/shard_map/ppermute | solution.py:418
  102.7 2.6 collective-permute-start.15
  105.8 0.6 pad_add_fusion.numbers
  106.5 1.5 collective-permute-done.15.refs_7_
  107.9 2.3 collective-permute-start.20
  110.2 2.3 collective-permute-start.23
  112.5 2.3 collective-permute-start.26
  114.8 1.5 collective-permute-start.21
  116.4 5.2 %expand.1 = bf16[32,64,512]{2,1,0:T(8,128)(2,1)} custom-call(s32[4]{0:T(128)} %pad_add_fusion.numbers, bf16[8,132,128]{2,1,0:T(8,128)(2,1)} %copy-done.1, bf16[132,512]{1,0:T(8,128)(2,1)} %copy-done.3, bf16[132,512]{1,0:T(8,128)(2,1)} %copy-done.6, bf16[132,512]{1,0:T(8,128)(2,1)} %copy-done.7, bf16[132,512]{1,0:T(8,128)(2,1)} %copy-done.8, ...), custom_call_target="tpu_custom_call" | custom-call | flops 700000000 | bytes 4000000 | tf_op jit(solution)/shard_map/expand/pallas_call | solution.py:200
  121.6 14.4 %all-to-all-start = ((bf16[32,64,512]{2,1,0:T(8,128)(2,1)}), bf16[32,64,512]{2,1,0:T(8,128)(2,1)S(1)}, u32[]{:S(2)}, u32[]{:S(2)}) async-start(bf16[32,64,512]{2,1,0:T(8,128)(2,1)} %expand.1), calls=%async_computation | async-start | bytes 4194304 | tf_op jit(solution)/shard_map/all_to_all | solution.py:539
  136.6 1.3 collective-permute-start.22
  137.9 1.3 collective-permute-start.25
  139.2 1.5 collective-permute-start.28
  141.1 0.8 add.147.origin
  142.0 4.4 %copy.37.code = bf16[64,132,128]{2,1,0:T(8,128)(2,1)} copy(bf16[64,132,128]{2,0,1:T(8,128)(2,1)} %all-gather.6.cloned.1.call-done) | data formatting | bytes 4325376 | tf_op jit(solution)/shard_map/all_gather | solution.py:517
  146.3 6.1 %chosen_rows.1.codes = f32[8,64,128]{2,1,0:T(8,128)} custom-call(s32[4]{0:T(128)} %pad_add_fusion.numbers, bf16[64,132,128]{2,1,0:T(8,128)(2,1)} %copy.37.code), custom_call_target="tpu_custom_call" | custom-call | flops 200000000 | bytes 2000000 | tf_op jit(solution)/shard_map/chosen_rows/pallas_call | solution.py:267
  152.5 11.0 %all-to-all-done = bf16[32,64,512]{2,1,0:T(8,128)(2,1)S(1)} async-done(((bf16[32,64,512]{2,1,0:T(8,128)(2,1)}), bf16[32,64,512]{2,1,0:T(8,128)(2,1)S(1)}, u32[]{:S(2)}, u32[]{:S(2)}) %all-to-all-start) | async-done | bytes 2097184 | tf_op jit(solution)/shard_map/all_to_all | solution.py:539
  163.5 1.4 copy-done.2
  164.8 15.0 %expert.1 = bf16[8,4,64,512]{3,2,1,0:T(8,128)(2,1)} custom-call(s32[4]{0:T(128)} %pad_add_fusion.numbers, bf16[8,4,64,512]{3,2,1,0:T(8,128)(2,1)} %bitcast.54, f32[8,64,128]{2,1,0:T(8,128)} %chosen_rows.1.codes, s32[512,1]{1,0:T(8,128)} %add.147.origin, f32[1,2048]{1,0:T(1,128)} %bitcast.78, bf16[64,2048]{1,0:T(8,128)(2,1)} %bitcast.77, ...), custom_call_target="tpu_custom_call" | custom-call | flops 6499999744 | bytes 20000000 | tf_op jit(solution)/shard_map/expert/pallas_call | solution.py:359
  179.8 4.9 %all-to-all-start.1 = ((bf16[32,64,512]{2,1,0:T(8,128)(2,1)}), bf16[32,64,512]{2,1,0:T(8,128)(2,1)S(1)}, u32[]{:S(2)}, u32[]{:S(2)}) async-start(bf16[32,64,512]{2,1,0:T(8,128)(2,1)} %bitcast.55), calls=%async_computation.1 | async-start | bytes 4194304 | tf_op jit(solution)/shard_map/all_to_all | solution.py:563
  184.9 0.5 fusion.31.order
  185.5 26.8 %all-to-all-done.1.answers = bf16[32,64,512]{2,1,0:T(8,128)(2,1)S(1)} async-done(((bf16[32,64,512]{2,1,0:T(8,128)(2,1)}), bf16[32,64,512]{2,1,0:T(8,128)(2,1)S(1)}, u32[]{:S(2)}, u32[]{:S(2)}) %all-to-all-start.1) | async-done | bytes 2097184 | tf_op jit(solution)/shard_map/all_to_all | solution.py:563
  212.2 1.4 copy-done
  213.6 5.5 %combine.1 = bf16[8,132,512]{2,1,0:T(8,128)(2,1)} custom-call(s32[4]{0:T(128)} %pad_add_fusion.numbers, s32[8]{0:T(128)} %fusion.31.order, bf16[64,132,128]{2,1,0:T(8,128)(2,1)} %copy.37.code, bf16[32,64,512]{2,1,0:T(8,128)(2,1)} %copy-done), custom_call_target="tpu_custom_call" | custom-call | flops 700000000 | bytes 4000000 | tf_op jit(solution)/shard_map/combine/pallas_call | solution.py:224
  219.1 1.3 reshape.69
  220.5 25.0 %fusion = bf16[136,512]{1,0:T(8,128)(2,1)S(1)} fusion(bf16[1056,512]{1,0:T(8,128)(2,1)S(1)} %reshape.69), kind=kCustom, calls=%all-reduce-scatter | all-reduce-scatter fusion | flops 557057 | bytes 1221632
  245.5 1.9 collective-permute-start.29
  247.4 0.6 dynamic-slice.8
  248.7 2.6 %collective-permute-done.29 = bf16[28,512]{1,0:T(8,128)(2,1)S(1)} collective-permute-done((bf16[28,512]{1,0:T(8,128)(2,1)S(1)}, bf16[28,512]{1,0:T(8,128)(2,1)S(1)}, u32[]{:S(2)}, u32[]{:S(2)}) %collective-permute-start.29) | collective-permute-done | bytes 28704
  251.5 0.7 constant_dynamic-slice_fusion
  (79 shorter events, 3.5 us)
Async XLA Ops:
  6.5 82.3 %all-gather.8.cloned.1.call-start = ((), (), s32[]{:S(2)}) async-start(), calls=%async_computation.3 | async-start | bytes 1253376 | tf_op jit(solution)/shard_map/all_gather | solution.py:472
  7.8 14.6 %collective-permute-start.2 = (f32[2,132]{0,1:T(8,128)S(1)}, f32[2,132]{0,1:T(8,128)S(1)}, u32[]{:S(2)}, u32[]{:S(2)}) collective-permute-start(f32[2,132]{0,1:T(8,128)S(1)} %copy.30), channel_id=1, source_target_pairs={{0,3},{1,0},{2,1},{3,2},{4,7},{5,4},{6,5},{7,6},{8,11},{9,8},{10,9... | collective-permute-start | bytes 3176 | tf_op jit(solution)/shard_map/ppermute | solution.py:418
  10.6 14.1 %collective-permute-start.1 = (f32[2,132]{0,1:T(8,128)S(1)}, f32[2,132]{0,1:T(8,128)S(1)}, u32[]{:S(2)}, u32[]{:S(2)}) collective-permute-start(f32[2,132]{0,1:T(8,128)S(1)} %copy.30), channel_id=1, source_target_pairs={{0,2},{1,3},{2,0},{3,1},{4,6},{5,7},{6,4},{7,5},{8,10},{9,11},{10,... | collective-permute-start | bytes 3176 | tf_op jit(solution)/shard_map/ppermute | solution.py:418
  11.4 39.8 %collective-permute-start.3 = (bf16[2048,256]{1,0:T(8,128)(2,1)}, bf16[2048,256]{1,0:T(8,128)(2,1)S(1)}, u32[]{:S(2)}, u32[]{:S(2)}) collective-permute-start(bf16[2048,256]{1,0:T(8,128)(2,1)} %bitcast.68), channel_id=1, source_target_pairs={{0,1},{1,0},{2,5},{3,4},{6,7},{7,6},{5,2},{4,3},{8,9},{9,8},{10,13... | collective-permute-start | bytes 3145736 | tf_op jit(solution)/shard_map/ppermute | solution.py:476
  12.3 51.3 %collective-permute-start.4 = (bf16[2048,256]{1,0:T(8,128)(2,1)}, bf16[2048,256]{1,0:T(8,128)(2,1)}, u32[]{:S(2)}, u32[]{:S(2)}) collective-permute-start(bf16[2048,256]{1,0:T(8,128)(2,1)} %bitcast.71), channel_id=1, source_target_pairs={{0,1},{1,0},{2,5},{3,4},{6,7},{7,6},{5,2},{4,3},{8,9},{9,8},{10,13... | collective-permute-start | bytes 3145736 | tf_op jit(solution)/shard_map/ppermute | solution.py:476
  13.4 50.2 %collective-permute-start.5 = (bf16[256,2048]{1,0:T(8,128)(2,1)}, bf16[256,2048]{1,0:T(8,128)(2,1)}, u32[]{:S(2)}, u32[]{:S(2)}) collective-permute-start(bf16[256,2048]{1,0:T(8,128)(2,1)} %bitcast.74), channel_id=1, source_target_pairs={{0,1},{1,0},{2,5},{3,4},{6,7},{7,6},{5,2},{4,3},{8,9},{9,8},{10,13... | collective-permute-start | bytes 3145736 | tf_op jit(solution)/shard_map/ppermute | solution.py:476
  16.5 125.4 %all-gather.6.cloned.1.call-start = ((), (), s32[]{:S(2)}) async-start(), calls=%async_computation.2 | async-start | bytes 2433024 | tf_op jit(solution)/shard_map/all_gather | solution.py:517
  22.3 28.9 %collective-permute-start = (f32[2,132]{0,1:T(8,128)S(1)}, f32[2,132]{0,1:T(8,128)S(1)}, u32[]{:S(2)}, u32[]{:S(2)}) collective-permute-start(f32[2,132]{0,1:T(8,128)S(1)} %copy.30), channel_id=1, source_target_pairs={{0,1},{1,2},{2,3},{3,0},{4,5},{5,6},{6,7},{7,4},{8,9},{9,10},{10,1... | collective-permute-start | bytes 3176 | tf_op jit(solution)/shard_map/ppermute | solution.py:418
  51.2 12.3 %copy-start.14 = (bf16[2048,256]{1,0:T(8,128)(2,1)}, bf16[2048,256]{1,0:T(8,128)(2,1)S(1)}, u32[]{:S(2)}) copy-start(bf16[2048,256]{1,0:T(8,128)(2,1)S(1)} %collective-permute-done.3.refs_1_) | copy-start | bytes 3145732
  63.6 44.4 %copy-start.13 = (bf16[1,2048,256]{2,1,0:T(8,128)(2,1)S(1)}, bf16[1,2048,256]{2,1,0:T(8,128)(2,1)}, u32[]{:S(2)}) copy-start(bf16[1,2048,256]{2,1,0:T(8,128)(2,1)} %param.29) | copy-start | bytes 3145732
  63.6 6.5 %collective-permute-start.8 = (bf16[132,512]{1,0:T(8,128)(2,1)}, bf16[132,512]{1,0:T(8,128)(2,1)S(1)}, u32[]{:S(2)}, u32[]{:S(2)}) collective-permute-start(bf16[132,512]{1,0:T(8,128)(2,1)} %get-tuple-element.30), channel_id=1, source_target_pairs={{0,3},{1,0},{2,1},{3,2},{4,7},{5,4},{6,5},{7,6},{8,11},{9,8},{10,9... | collective-permute-start | bytes 405512 | tf_op jit(solution)/shard_map/ppermute | solution.py:418
  63.7 8.3 %collective-permute-start.7 = (bf16[132,512]{1,0:T(8,128)(2,1)}, bf16[132,512]{1,0:T(8,128)(2,1)S(1)}, u32[]{:S(2)}, u32[]{:S(2)}) collective-permute-start(bf16[132,512]{1,0:T(8,128)(2,1)} %get-tuple-element.29), channel_id=1, source_target_pairs={{0,2},{1,3},{2,0},{3,1},{4,6},{5,7},{6,4},{7,5},{8,10},{9,11},{10,... | collective-permute-start | bytes 405512 | tf_op jit(solution)/shard_map/ppermute | solution.py:418
  65.8 8.4 %collective-permute-start.6 = (bf16[132,512]{1,0:T(8,128)(2,1)}, bf16[132,512]{1,0:T(8,128)(2,1)S(1)}, u32[]{:S(2)}, u32[]{:S(2)}) collective-permute-start(bf16[132,512]{1,0:T(8,128)(2,1)} %get-tuple-element.28), channel_id=1, source_target_pairs={{0,1},{1,2},{2,3},{3,0},{4,5},{5,6},{6,7},{7,4},{8,9},{9,10},{10,1... | collective-permute-start | bytes 405512 | tf_op jit(solution)/shard_map/ppermute | solution.py:418
  75.3 41.0 %copy-start.3 = (bf16[132,512]{1,0:T(8,128)(2,1)}, bf16[132,512]{1,0:T(8,128)(2,1)S(1)}, u32[]{:S(2)}) copy-start(bf16[132,512]{1,0:T(8,128)(2,1)S(1)} %add_convert_fusion.refs_0_) | copy-start | bytes 405508
  75.3 5.6 %collective-permute-start.9 = (bf16[132,512]{1,0:T(8,128)(2,1)S(1)}, bf16[132,512]{1,0:T(8,128)(2,1)S(1)}, u32[]{:S(2)}, u32[]{:S(2)}) collective-permute-start(bf16[132,512]{1,0:T(8,128)(2,1)S(1)} %add_convert_fusion.refs_0_), channel_id=1, source_target_pairs={{0,32},{32,64},{64,96},{96,128},{128,160},{160,192},{192,224},{224... | collective-permute-start | bytes 405512 | tf_op jit(solution)/shard_map/ppermute | solution.py:418
  76.9 5.8 %collective-permute-start.11 = (bf16[132,512]{1,0:T(8,128)(2,1)S(1)}, bf16[132,512]{1,0:T(8,128)(2,1)S(1)}, u32[]{:S(2)}, u32[]{:S(2)}) collective-permute-start(bf16[132,512]{1,0:T(8,128)(2,1)S(1)} %add_convert_fusion.refs_0_), channel_id=1, source_target_pairs={{0,224},{32,0},{64,32},{96,64},{128,96},{160,128},{192,160},{224,1... | collective-permute-start | bytes 405512 | tf_op jit(solution)/shard_map/ppermute | solution.py:418
  80.8 35.5 %copy-start.6 = (bf16[132,512]{1,0:T(8,128)(2,1)}, bf16[132,512]{1,0:T(8,128)(2,1)S(1)}, u32[]{:S(2)}) copy-start(bf16[132,512]{1,0:T(8,128)(2,1)S(1)} %collective-permute-done.9.refs_1_) | copy-start | bytes 405508
  80.8 7.4 %collective-permute-start.10 = (bf16[132,512]{1,0:T(8,128)(2,1)S(1)}, bf16[132,512]{1,0:T(8,128)(2,1)S(1)}, u32[]{:S(2)}, u32[]{:S(2)}) collective-permute-start(bf16[132,512]{1,0:T(8,128)(2,1)S(1)} %collective-permute-done.9.refs_1_), channel_id=1, source_target_pairs={{0,32},{32,64},{64,96},{96,128},{128,160},{160,192},{192,224},{224... | collective-permute-start | bytes 405512 | tf_op jit(solution)/shard_map/ppermute | solution.py:418
  82.7 33.6 %copy-start.7 = (bf16[132,512]{1,0:T(8,128)(2,1)}, bf16[132,512]{1,0:T(8,128)(2,1)S(1)}, u32[]{:S(2)}) copy-start(bf16[132,512]{1,0:T(8,128)(2,1)S(1)} %collective-permute-done.11.refs_2_) | copy-start | bytes 405508
  82.7 6.2 %collective-permute-start.12 = (bf16[132,512]{1,0:T(8,128)(2,1)S(1)}, bf16[132,512]{1,0:T(8,128)(2,1)S(1)}, u32[]{:S(2)}, u32[]{:S(2)}) collective-permute-start(bf16[132,512]{1,0:T(8,128)(2,1)S(1)} %collective-permute-done.11.refs_2_), channel_id=1, source_target_pairs={{0,224},{32,0},{64,32},{96,64},{128,96},{160,128},{192,160},{224,1... | collective-permute-start | bytes 405512 | tf_op jit(solution)/shard_map/ppermute | solution.py:418
  88.3 28.0 %copy-start.8 = (bf16[132,512]{1,0:T(8,128)(2,1)}, bf16[132,512]{1,0:T(8,128)(2,1)S(1)}, u32[]{:S(2)}) copy-start(bf16[132,512]{1,0:T(8,128)(2,1)S(1)} %collective-permute-done.10.refs_3_) | copy-start | bytes 405508
  88.8 27.5 %copy-start.9 = (bf16[132,512]{1,0:T(8,128)(2,1)}, bf16[132,512]{1,0:T(8,128)(2,1)S(1)}, u32[]{:S(2)}) copy-start(bf16[132,512]{1,0:T(8,128)(2,1)S(1)} %collective-permute-done.12.refs_4_) | copy-start | bytes 405508
  89.9 26.4 %copy-start.1 = (bf16[8,132,128]{2,1,0:T(8,128)(2,1)}, bf16[8,132,128]{2,1,0:T(8,128)(2,1)S(1)}, u32[]{:S(2)}) copy-start(bf16[8,132,128]{2,1,0:T(8,128)(2,1)S(1)} %slice.62.code) | copy-start | bytes 811012
  90.7 21.8 %collective-permute-start.17 = (bf16[2048,256]{1,0:T(8,128)(2,1)}, bf16[2048,256]{1,0:T(8,128)(2,1)}, u32[]{:S(2)}, u32[]{:S(2)}) collective-permute-start(bf16[2048,256]{1,0:T(8,128)(2,1)} %copy-done.14), channel_id=1, source_target_pairs={{4,5},{5,4},{2,3},{3,2},{12,13},{13,12},{10,11},{11,10},{20,21},{2... | collective-permute-start | bytes 3145736 | tf_op jit(solution)/shard_map/ppermute | solution.py:509
  92.4 22.4 %collective-permute-start.18 = (bf16[2048,256]{1,0:T(8,128)(2,1)}, bf16[2048,256]{1,0:T(8,128)(2,1)}, u32[]{:S(2)}, u32[]{:S(2)}) collective-permute-start(bf16[2048,256]{1,0:T(8,128)(2,1)} %collective-permute-done.4.refs_7_), channel_id=1, source_target_pairs={{4,5},{5,4},{2,3},{3,2},{12,13},{13,12},{10,11},{11,10},{20,21},{2... | collective-permute-start | bytes 3145736 | tf_op jit(solution)/shard_map/ppermute | solution.py:509
  94.0 27.6 %collective-permute-start.19 = (bf16[256,2048]{1,0:T(8,128)(2,1)}, bf16[256,2048]{1,0:T(8,128)(2,1)}, u32[]{:S(2)}, u32[]{:S(2)}) collective-permute-start(bf16[256,2048]{1,0:T(8,128)(2,1)} %collective-permute-done.5.refs_13_), channel_id=1, source_target_pairs={{4,5},{5,4},{2,3},{3,2},{12,13},{13,12},{10,11},{11,10},{20,21},{2... | collective-permute-start | bytes 3145736 | tf_op jit(solution)/shard_map/ppermute | solution.py:509
  95.7 6.9 %collective-permute-start.13 = (bf16[132,512]{1,0:T(8,128)(2,1)S(1)}, bf16[132,512]{1,0:T(8,128)(2,1)S(1)}, u32[]{:S(2)}, u32[]{:S(2)}) collective-permute-start(bf16[132,512]{1,0:T(8,128)(2,1)S(1)} %collective-permute-done.10.refs_3_), channel_id=1, source_target_pairs={{0,32},{32,64},{64,96},{96,128},{128,160},{160,192},{192,224},{224... | collective-permute-start | bytes 405512 | tf_op jit(solution)/shard_map/ppermute | solution.py:418
  98.9 6.7 %collective-permute-start.14 = (bf16[132,512]{1,0:T(8,128)(2,1)S(1)}, bf16[132,512]{1,0:T(8,128)(2,1)S(1)}, u32[]{:S(2)}, u32[]{:S(2)}) collective-permute-start(bf16[132,512]{1,0:T(8,128)(2,1)S(1)} %collective-permute-done.12.refs_4_), channel_id=1, source_target_pairs={{0,224},{32,0},{64,32},{96,64},{128,96},{160,128},{192,160},{224,1... | collective-permute-start | bytes 405512 | tf_op jit(solution)/shard_map/ppermute | solution.py:418
  102.6 13.7 %copy-start.5 = (bf16[132,512]{1,0:T(8,128)(2,1)}, bf16[132,512]{1,0:T(8,128)(2,1)S(1)}, u32[]{:S(2)}) copy-start(bf16[132,512]{1,0:T(8,128)(2,1)S(1)} %collective-permute-done.13.refs_5_) | copy-start | bytes 405508
  102.7 5.3 %collective-permute-start.15 = (bf16[64,512]{1,0:T(8,128)(2,1)S(1)}, bf16[64,512]{1,0:T(8,128)(2,1)S(1)}, u32[]{:S(2)}, u32[]{:S(2)}) collective-permute-start(bf16[64,512]{1,0:T(8,128)(2,1)S(1)} %slice.66), channel_id=1, source_target_pairs={{0,32},{32,64},{64,96},{96,128},{128,160},{160,192},{192,224},{224... | collective-permute-start | bytes 196616 | tf_op jit(solution)/shard_map/ppermute | solution.py:418
  105.7 10.7 %copy-start.4 = (bf16[132,512]{1,0:T(8,128)(2,1)}, bf16[132,512]{1,0:T(8,128)(2,1)S(1)}, u32[]{:S(2)}) copy-start(bf16[132,512]{1,0:T(8,128)(2,1)S(1)} %collective-permute-done.14.refs_6_) | copy-start | bytes 405508
  105.7 4.5 %collective-permute-start.16 = (bf16[68,512]{1,0:T(8,128)(2,1)S(1)}, bf16[68,512]{1,0:T(8,128)(2,1)S(1)}, u32[]{:S(2)}, u32[]{:S(2)}) collective-permute-start(bf16[68,512]{1,0:T(8,128)(2,1)S(1)} %slice.67), channel_id=1, source_target_pairs={{0,224},{32,0},{64,32},{96,64},{128,96},{160,128},{192,160},{224,1... | collective-permute-start | bytes 208904 | tf_op jit(solution)/shard_map/ppermute | solution.py:418
  107.9 8.4 %copy-start.11 = (bf16[64,512]{1,0:T(8,128)(2,1)}, bf16[64,512]{1,0:T(8,128)(2,1)S(1)}, u32[]{:S(2)}) copy-start(bf16[64,512]{1,0:T(8,128)(2,1)S(1)} %collective-permute-done.15.refs_7_) | copy-start | bytes 196612
  107.9 28.4 %collective-permute-start.20 = (bf16[2048,256]{1,0:T(8,128)(2,1)S(1)}, bf16[2048,256]{1,0:T(8,128)(2,1)}, u32[]{:S(2)}, u32[]{:S(2)}) collective-permute-start(bf16[2048,256]{1,0:T(8,128)(2,1)S(1)} %bitcast.70), channel_id=1, source_target_pairs={{0,4},{1,5},{6,2},{7,3},{8,12},{9,13},{14,10},{15,11},{16,20},{17,... | collective-permute-start | bytes 3145736 | tf_op jit(solution)/shard_map/ppermute | solution.py:533
  110.2 6.1 %copy-start.10 = (bf16[68,512]{1,0:T(8,128)(2,1)}, bf16[68,512]{1,0:T(8,128)(2,1)S(1)}, u32[]{:S(2)}) copy-start(bf16[68,512]{1,0:T(8,128)(2,1)S(1)} %collective-permute-done.16.refs_8_) | copy-start | bytes 208900
  110.2 26.4 %collective-permute-start.23 = (bf16[2048,256]{1,0:T(8,128)(2,1)}, bf16[2048,256]{1,0:T(8,128)(2,1)}, u32[]{:S(2)}, u32[]{:S(2)}) collective-permute-start(bf16[2048,256]{1,0:T(8,128)(2,1)} %bitcast.72), channel_id=1, source_target_pairs={{0,4},{1,5},{6,2},{7,3},{8,12},{9,13},{14,10},{15,11},{16,20},{17,... | collective-permute-start | bytes 3145736 | tf_op jit(solution)/shard_map/ppermute | solution.py:533
  112.5 25.4 %collective-permute-start.26 = (bf16[256,2048]{1,0:T(8,128)(2,1)}, bf16[256,2048]{1,0:T(8,128)(2,1)}, u32[]{:S(2)}, u32[]{:S(2)}) collective-permute-start(bf16[256,2048]{1,0:T(8,128)(2,1)} %bitcast.75), channel_id=1, source_target_pairs={{0,4},{1,5},{6,2},{7,3},{8,12},{9,13},{14,10},{15,11},{16,20},{17,... | collective-permute-start | bytes 3145736 | tf_op jit(solution)/shard_map/ppermute | solution.py:533
  114.8 24.4 %collective-permute-start.21 = (bf16[2048,256]{1,0:T(8,128)(2,1)}, bf16[2048,256]{1,0:T(8,128)(2,1)}, u32[]{:S(2)}, u32[]{:S(2)}) collective-permute-start(bf16[2048,256]{1,0:T(8,128)(2,1)} %copy-done.14), channel_id=1, source_target_pairs={{0,4},{1,5},{2,6},{3,7},{4,0},{5,1},{6,2},{7,3},{8,12},{9,13},{10,... | collective-permute-start | bytes 3145736 | tf_op jit(solution)/shard_map/ppermute | solution.py:535
  121.6 19.2 %copy-start.16 = (s32[64]{0:T(128)S(1)}, s32[64]{0:T(128)}, u32[]{:S(2)}) copy-start(s32[64]{0:T(128)} %param.24) | copy-start | bytes 772
  121.6 41.9 %all-to-all-start = ((bf16[32,64,512]{2,1,0:T(8,128)(2,1)}), bf16[32,64,512]{2,1,0:T(8,128)(2,1)S(1)}, u32[]{:S(2)}, u32[]{:S(2)}) async-start(bf16[32,64,512]{2,1,0:T(8,128)(2,1)} %expand.1), calls=%async_computation | async-start | bytes 4194304 | tf_op jit(solution)/shard_map/all_to_all | solution.py:539
  136.0 16.5 %collective-permute-start.24 = (bf16[2048,256]{1,0:T(8,128)(2,1)}, bf16[2048,256]{1,0:T(8,128)(2,1)}, u32[]{:S(2)}, u32[]{:S(2)}) collective-permute-start(bf16[2048,256]{1,0:T(8,128)(2,1)} %collective-permute-done.4.refs_7_), channel_id=1, source_target_pairs={{0,4},{1,5},{2,6},{3,7},{4,0},{5,1},{6,2},{7,3},{8,12},{9,13},{10,... | collective-permute-start | bytes 3145736 | tf_op jit(solution)/shard_map/ppermute | solution.py:535
  136.3 16.1 %collective-permute-start.27 = (bf16[256,2048]{1,0:T(8,128)(2,1)}, bf16[256,2048]{1,0:T(8,128)(2,1)S(1)}, u32[]{:S(2)}, u32[]{:S(2)}) collective-permute-start(bf16[256,2048]{1,0:T(8,128)(2,1)} %collective-permute-done.5.refs_13_), channel_id=1, source_target_pairs={{0,4},{1,5},{2,6},{3,7},{4,0},{5,1},{6,2},{7,3},{8,12},{9,13},{10,... | collective-permute-start | bytes 3145736 | tf_op jit(solution)/shard_map/ppermute | solution.py:535
  136.6 15.9 %collective-permute-start.22 = (bf16[2048,256]{1,0:T(8,128)(2,1)}, bf16[2048,256]{1,0:T(8,128)(2,1)}, u32[]{:S(2)}, u32[]{:S(2)}) collective-permute-start(bf16[2048,256]{1,0:T(8,128)(2,1)} %collective-permute-done.17.refs_3_), channel_id=1, source_target_pairs={{4,0},{5,1},{2,6},{3,7},{12,8},{13,9},{10,14},{11,15},{20,16},{21,... | collective-permute-start | bytes 3145736 | tf_op jit(solution)/shard_map/ppermute | solution.py:536
  137.9 14.6 %collective-permute-start.25 = (bf16[2048,256]{1,0:T(8,128)(2,1)}, bf16[2048,256]{1,0:T(8,128)(2,1)}, u32[]{:S(2)}, u32[]{:S(2)}) collective-permute-start(bf16[2048,256]{1,0:T(8,128)(2,1)} %collective-permute-done.18.refs_9_), channel_id=1, source_target_pairs={{4,0},{5,1},{2,6},{3,7},{12,8},{13,9},{10,14},{11,15},{20,16},{21,... | collective-permute-start | bytes 3145736 | tf_op jit(solution)/shard_map/ppermute | solution.py:536
  139.2 13.3 %collective-permute-start.28 = (bf16[256,2048]{1,0:T(8,128)(2,1)}, bf16[256,2048]{1,0:T(8,128)(2,1)}, u32[]{:S(2)}, u32[]{:S(2)}) collective-permute-start(bf16[256,2048]{1,0:T(8,128)(2,1)} %collective-permute-done.19.refs_15_), channel_id=1, source_target_pairs={{4,0},{5,1},{2,6},{3,7},{12,8},{13,9},{10,14},{11,15},{20,16},{21,... | collective-permute-start | bytes 3145736 | tf_op jit(solution)/shard_map/ppermute | solution.py:536
  152.4 11.0 %copy-start.15 = (bf16[256,2048]{1,0:T(8,128)(2,1)}, bf16[256,2048]{1,0:T(8,128)(2,1)S(1)}, u32[]{:S(2)}) copy-start(bf16[256,2048]{1,0:T(8,128)(2,1)S(1)} %collective-permute-done.27.refs_16_) | copy-start | bytes 3145732
  163.4 1.4 copy-start.2
  179.8 32.4 %all-to-all-start.1 = ((bf16[32,64,512]{2,1,0:T(8,128)(2,1)}), bf16[32,64,512]{2,1,0:T(8,128)(2,1)S(1)}, u32[]{:S(2)}, u32[]{:S(2)}) async-start(bf16[32,64,512]{2,1,0:T(8,128)(2,1)} %bitcast.55), calls=%async_computation.1 | async-start | bytes 4194304 | tf_op jit(solution)/shard_map/all_to_all | solution.py:563
  212.2 1.4 copy-start
  219.1 28.3 %copy-start.12 = (u32[256]{0:T(256)S(1)}, u32[256]{0:T(256)}, u32[]{:S(2)}) copy-start(u32[256]{0:T(256)} %constant.160) | copy-start | bytes 3076
  245.5 5.8 %collective-permute-start.29 = (bf16[28,512]{1,0:T(8,128)(2,1)S(1)}, bf16[28,512]{1,0:T(8,128)(2,1)S(1)}, u32[]{:S(2)}, u32[]{:S(2)}) collective-permute-start(bf16[28,512]{1,0:T(8,128)(2,1)S(1)} %slice.68), channel_id=1, source_target_pairs={{0,32},{32,64},{64,96},{96,128},{128,160},{160,192},{192,224},{1,3... | collective-permute-start | bytes 86024
Sparse Core Ops, SparseCore 0:
  16.6 40.0 all-gather.7
  90.8 31.2 all-gather.5

commit v3 on v2

--- a/solution.py
+++ b/solution.py
@@ -13,6 +13,7 @@
 PRE = 128
 DEC = 4
 ROWS = PRE + DEC
+PADDED = 136
 SLOTS = 512
 COLS = 512
 FULL = 2048
@@ -175,31 +176,48 @@
     return (slot == wanted).astype(F32).astype(BF)
 
 
-def expand_kernel(numbers, code, *refs):
+def hits_kernel(numbers, order, code, out):
+    for position in range(PLANES):
+        out[position] = pair_onehot(
+            code[order[position]][:ROWS], numbers[0], position & 1
+        )
+
+
+def pair_hits(numbers, order, code):
+    return pl.pallas_call(
+        hits_kernel,
+        in_specs=[SM, SM, VM],
+        out_specs=VM,
+        out_shape=jax.ShapeDtypeStruct((PLANES, ROWS, PAIR_LANES), BF),
+        compiler_params=pltpu.CompilerParams(vmem_limit_bytes=VMEM_LIMIT),
+        cost_estimate=pl.CostEstimate(
+            flops=700_000_000, bytes_accessed=4_000_000, transcendentals=0
+        ),
+        name="pair_hits",
+    )(numbers, order, code)
+
+
+def expand_kernel(hits, *refs):
     held, out = refs[:-1], refs[-1]
-    plane = numbers[0]
     for pair in range(PLANES // 2):
         filled = None
         for second in range(2):
             position = 2 * pair + second
-            hits = pair_onehot(
-                code[(plane + NEAR[position] + PLANES) % PLANES], plane, second
-            )
             if position < PLANES - 1:
                 rows = held[position][...]
             else:
                 rows = jnp.concatenate(
-                    [held[PLANES - 1][...], held[PLANES][...]], axis=0
+                    [held[position][...], held[position + 1][...]], axis=0
                 )
-            part = dot(hits, rows, 0, 0)
+            part = dot(hits[position], rows, 0, 0)
             filled = part if filled is None else filled + part
         out[:, 16 * pair : 16 * pair + 16, :] = filled.astype(BF).reshape(32, 16, COLS)
 
 
-def expand(numbers, code, held):
+def expand(hits, held):
     return pl.pallas_call(
         expand_kernel,
-        in_specs=[SM, VM] + [VM] * len(held),
+        in_specs=[VM] * (1 + len(held)),
         out_specs=VM,
         out_shape=jax.ShapeDtypeStruct((32, 64, COLS), BF),
         compiler_params=pltpu.CompilerParams(vmem_limit_bytes=VMEM_LIMIT),
@@ -207,37 +225,31 @@
             flops=700_000_000, bytes_accessed=4_000_000, transcendentals=0
         ),
         name="expand",
-    )(numbers, code, *held)
-
-
-def combine_kernel(numbers, order, code, answers, out):
-    plane = numbers[0]
-    pair = pl.program_id(0)
+    )(hits, *held)
+
+
+def combine_kernel(hits, answers, out):
     rows = answers[...].reshape(PAIR_LANES, COLS)
     for second in range(2):
-        group = order[2 * pair + second]
-        hits = pair_onehot(code[group], plane, second)
-        out[second] = dot(hits, rows).astype(BF)
-
-
-def combine(numbers, order, code, answers):
+        out[second] = dot(hits[second], rows).astype(BF)
+
+
+def combine(hits, answers):
     return pl.pallas_call(
         combine_kernel,
         grid=(PLANES // 2,),
         in_specs=[
-            SM,
-            SM,
-            pl.BlockSpec((EXPERTS, ROWS, LANES), lambda p: (0, 0, 0)),
+            pl.BlockSpec((2, ROWS, PAIR_LANES), lambda p: (p, 0, 0)),
             pl.BlockSpec((32, 16, COLS), lambda p: (0, p, 0)),
         ],
         out_specs=pl.BlockSpec((2, ROWS, COLS), lambda p: (p, 0, 0)),
         out_shape=jax.ShapeDtypeStruct((PLANES, ROWS, COLS), BF),
         compiler_params=pltpu.CompilerParams(vmem_limit_bytes=VMEM_LIMIT),
         cost_estimate=pl.CostEstimate(
-            flops=700_000_000, bytes_accessed=4_000_000, transcendentals=0
+            flops=600_000_000, bytes_accessed=4_000_000, transcendentals=0
         ),
         name="combine",
-    )(numbers, order, code, answers)
+    )(hits, answers)
 
 
 def chosen_kernel(numbers, code, out):
@@ -250,7 +262,7 @@
         filled = jnp.zeros((64, LANES), F32)
         for position in range(PLANES):
             z = (plane + NEAR[position] + PLANES) % PLANES
-            rows = code[column * PLANES + z]
+            rows = code[column * PLANES + z][:ROWS]
             slot = jnp.sum(
                 jnp.where(is_expert, slot_part(rows), 0.0), axis=1, keepdims=True
             )
@@ -277,43 +289,44 @@
     )(numbers, code)
 
 
+def weight_copies(parts, target, sems, at_home, begin):
+    own, first, other_own, second, other_first, other_second = parts
+    if not begin:
+        for quarter in range(4):
+            pltpu.make_async_copy(
+                target(first), target(None, quarter), sems.at[quarter]
+            ).wait()
+        return
+
+    def bring(source, quarter):
+        pltpu.make_async_copy(
+            target(source), target(None, quarter), sems.at[quarter]
+        ).start()
+
+    @pl.when(at_home == 1)
+    def _():
+        bring(own, 0)
+        bring(other_second, 3)
+
+    @pl.when(at_home == 0)
+    def _():
+        bring(other_own, 0)
+        bring(second, 3)
+
+    bring(first, 1)
+    bring(other_first, 2)
+
+
 def expert_kernel(numbers, arrived, codes, origin, gain, router, *refs):
-    parts, out = refs[:18], refs[18]
-    weights, normed, hidden, sems = refs[19:22], refs[22], refs[23], refs[24]
+    wide_parts, down_parts, out = refs[:6], refs[6:12], refs[12]
+    wide, down, normed, hidden, sems = refs[13:18]
     at_home = numbers[3]
-
-    def place(kind, quarter):
-        if kind < 2:
-            return weights[kind].at[quarter]
-        return weights[2].at[quarter * 256 : (quarter + 1) * 256]
-
-    def bring(source, kind, quarter):
-        pltpu.make_async_copy(
-            source, place(kind, quarter), sems.at[kind, quarter]
-        ).start()
-
-    def arrival(kind, quarter):
-        return pltpu.make_async_copy(
-            parts[6 * kind + 1], place(kind, quarter), sems.at[kind, quarter]
-        )
-
-    for kind in range(3):
-        own, first, other_own, second, other_first, other_second = parts[
-            6 * kind : 6 * kind + 6
-        ]
-
-        @pl.when(at_home == 1)
-        def _():
-            bring(own, kind, 0)
-            bring(other_second, kind, 3)
-
-        @pl.when(at_home == 0)
-        def _():
-            bring(other_own, kind, 0)
-            bring(second, kind, 3)
-
-        bring(first, kind, 1)
-        bring(other_first, kind, 2)
+    to_wide = lambda source, quarter=None: wide.at[quarter] if source is None else source
+    to_down = lambda source, quarter=None: (
+        down.at[quarter * 256 : (quarter + 1) * 256] if source is None else source
+    )
+    weight_copies(wide_parts, to_wide, sems.at[0], at_home, True)
+    weight_copies(down_parts, to_down, sems.at[1], at_home, True)
 
     squares = jnp.zeros((512, 1), F32)
     for x in range(TP):
@@ -322,8 +335,7 @@
     scale = lax.rsqrt(squares / FULL + 1e-05)
     for x in range(TP):
         span = slice(x * COLS, (x + 1) * COLS)
-        part = arrived[:, x].reshape(512, COLS).astype(F32)
-        normed[:, span] = (part * scale * gain[:, span]).astype(BF)
+        normed[:, span] = (arrived[:, x].reshape(512, COLS).astype(F32) * scale * gain[:, span]).astype(BF)
     logits = dot(normed[...], router[...], 1, 1)
     code = codes[...].reshape(512, LANES)[:, :EXPERTS]
     chosen = code > 0.0
@@ -336,45 +348,42 @@
     mark = jnp.sum(jnp.where(is_expert, code, 0.0), axis=1, keepdims=True)
     first_choice = (mark > 64.0).astype(F32)
 
+    weight_copies(wide_parts, to_wide, sems.at[0], at_home, False)
     for quarter in range(4):
-        for kind in range(2):
-            arrival(kind, quarter).wait()
-        gate_pre = dot(normed[...], weights[0][quarter])
-        up_pre = dot(normed[...], weights[1][quarter])
+        gate_pre = dot(normed[...], wide[quarter, :FULL])
+        up_pre = dot(normed[...], wide[quarter, FULL:])
         hidden[:, quarter * 256 : (quarter + 1) * 256] = (
             gate_pre / (1.0 + jnp.exp(-gate_pre)) * up_pre
         ).astype(BF)
-    for quarter in range(4):
-        arrival(2, quarter).wait()
+    weight_copies(down_parts, to_down, sems.at[1], at_home, False)
     move = (origin[...] == iota((512, 512), 1)).astype(F32).astype(BF)
     for x in range(TP):
         span = slice(x * COLS, (x + 1) * COLS)
         part = arrived[:, x].reshape(512, COLS).astype(F32)
-        result = dot(hidden[...], weights[2][:, span]).astype(BF).astype(F32) * gate
+        result = dot(hidden[...], down[:, span]).astype(BF).astype(F32) * gate
         piece = (result + first_choice * part).astype(BF)
         out[:, x] = dot(move, piece).astype(BF).reshape(PLANES, 64, COLS)
 
 
-def expert(numbers, arrived, codes, origin, gain, router, parts):
+def expert(numbers, arrived, codes, origin, gain, router, wide_parts, down_parts):
     return pl.pallas_call(
         expert_kernel,
-        in_specs=[SM] + [VM] * 5 + [HB] * 18,
+        in_specs=[SM] + [VM] * 5 + [HB] * 12,
         out_specs=VM,
         out_shape=jax.ShapeDtypeStruct((PLANES, TP, 64, COLS), BF),
         scratch_shapes=[
-            pltpu.VMEM((4, FULL, 256), BF),
-            pltpu.VMEM((4, FULL, 256), BF),
+            pltpu.VMEM((4, 2 * FULL, 256), BF),
             pltpu.VMEM((1024, FULL), BF),
             pltpu.VMEM((512, FULL), BF),
             pltpu.VMEM((512, 1024), BF),
-            pltpu.SemaphoreType.DMA((3, 4)),
+            pltpu.SemaphoreType.DMA((2, 4)),
         ],
         compiler_params=pltpu.CompilerParams(vmem_limit_bytes=VMEM_LIMIT),
         cost_estimate=pl.CostEstimate(
-            flops=6_500_000_000, bytes_accessed=20_000_000, transcendentals=500_000
+            flops=8_000_000_000, bytes_accessed=20_000_000, transcendentals=500_000
         ),
         name="expert",
-    )(numbers, arrived, codes, origin, gain, router, *parts)
+    )(numbers, arrived, codes, origin, gain, router, *wide_parts, *down_parts)
 
 
 def pair_moves():
@@ -418,27 +427,6 @@
     return lax.ppermute(value, axis, [(i, (i + step) % count) for i in range(count)])
 
 
-def gather_column(value, code):
-    up = [value]
-    down = [value]
-    for step in range(3):
-        up.append(around(up[-1], "z", 1))
-        down.append(around(down[-1], "z", -1))
-        if step == 1:
-            up[2], down[2], code = tied(up[2], down[2], code)
-    return [
-        value,
-        up[1],
-        down[1],
-        up[2],
-        down[2],
-        up[3],
-        down[3],
-        around(up[3][:64], "z", 1),
-        around(down[3][64:], "z", -1),
-    ], code
-
-
 def per_device(
     projected,
     residual,
@@ -468,19 +456,20 @@
     slot = dot(below.astype(BF), chosen.astype(BF))
     first_choice = expert_ids[:, :1] == every[None, :]
     code = jnp.where(chosen, slot + 64.0 * first_choice, 0.0).astype(BF)
-    widened = jnp.concatenate([code] + [jnp.zeros_like(code)] * 3, axis=1)
+    widened = jnp.pad(code, ((0, PADDED - ROWS), (0, COLS - LANES)))
     code_column = lax.all_gather(widened, "z", axis=0)
 
     first_move, second_move, out_of_home, both, to_home = pair_moves()
-    owns = [gate_weight[0], up_weight[0], down_weight[0]]
-    firsts = [lax.ppermute(own, PAIR, first_move) for own in owns]
+    wide = jnp.concatenate([gate_weight[0], up_weight[0]], axis=0)
+    down = down_weight[0]
 
     proj = jnp.transpose(projected, (1, 0, 2))
     raw = proj[:2].astype(F32)
     squares = jnp.sum(raw * raw, axis=2)
     shared = [around(squares, "tp", step) for step in range(1, TP)]
     squares = squares + shared[0] + shared[1] + shared[2]
-    squares, firsts[0] = tied(squares, firsts[0])
+    squares, wide = tied(squares, wide)
+    wide_first = lax.ppermute(wide, PAIR, first_move)
     inv = lax.rsqrt(squares / FULL + 1e-05).T
     spot = jnp.arange(ROWS, dtype=jnp.int32)
     positions = offsets[0] + spot
@@ -505,38 +494,43 @@
         decode_cache,
         out_weight,
     )
-    *sends, firsts[1], firsts[2] = tied(*sends, firsts[1], firsts[2])
-    seconds = [lax.ppermute(first, PAIR, second_move) for first in firsts]
+    *sends, wide_first = tied(*sends, wide_first)
     state = own
     for step in range(1, TP):
         state = state + around(sends[step - 1], "tp", step).astype(F32)
     residual_here = lax.dynamic_slice_in_dim(residual, tp * COLS, COLS, 1)
     state = (residual_here.astype(F32) + state).astype(BF)
-    column_states, code_column = gather_column(state, code_column)
-    code_column = code_column[:, :, :LANES]
-    code_all = lax.all_gather(code_column, ("y", "c"), axis=0).reshape(
-        EXPERTS, ROWS, LANES
-    )
-
     serves = y * 2 + tp // 2
     quarter = (tp % 2) * 2 + c
     at_home = (tp // 2 == c).astype(jnp.int32)
     numbers = jnp.stack([z, z * PLANES + serves, quarter, at_home]).astype(jnp.int32)
+
+    state, wide_first, down = tied(state, wide_first, down)
+    down_first = lax.ppermute(down, PAIR, first_move)
+    wide_second = lax.ppermute(wide_first, PAIR, second_move)
+
+    up_1, down_1 = around(state, "z", 1), around(state, "z", -1)
+    up_2, down_2 = around(up_1, "z", 1), around(down_1, "z", -1)
+    up_2, down_2, code_column = tied(up_2, down_2, code_column)
+    code_column = code_column[:, :, :LANES]
+    code_all = lax.all_gather(code_column, ("y", "c"), axis=0).reshape(
+        EXPERTS, PADDED, LANES
+    )
+    near = (z + jnp.array(NEAR, jnp.int32) + PLANES) % PLANES
+    out_hits = pair_hits(numbers, near.astype(jnp.int32), code_column)
+    plane = ("y", "c", "tp")
+
+    def exchanged(blocks):
+        return lax.all_to_all(blocks, plane, split_axis=0, concat_axis=0, tiled=True)
+
+    up_3, down_3 = around(up_2, "z", 1), around(down_2, "z", -1)
+    far = [around(up_3[:64], "z", 1), around(down_3[64:], "z", -1)]
+    *far, down_first = tied(*far, down_first)
+    down_second = lax.ppermute(down_first, PAIR, second_move)
+    outgoing = expand(out_hits, [state, up_1, down_1, up_2, down_2, up_3, down_3, *far])
+    outgoing, wide_second = tied(outgoing, wide_second)
+    arrived = exchanged(outgoing)
     codes = chosen_rows(numbers, code_all)
-    outgoing = expand(numbers, code_column, column_states)
-    outgoing, *seconds = tied(outgoing, *seconds)
-    parts = []
-    for own, first, second in zip(owns, firsts, seconds, strict=True):
-        parts += [
-            own,
-            first,
-            lax.ppermute(own, PAIR, out_of_home),
-            second,
-            lax.ppermute(first, PAIR, both),
-            lax.ppermute(second, PAIR, to_home),
-        ]
-    plane = ("y", "c", "tp")
-    arrived = lax.all_to_all(outgoing, plane, split_axis=0, concat_axis=0, tiled=True)
 
     groups = jnp.arange(EXPERTS, dtype=jnp.int32)
     inverse = jnp.sum(
@@ -551,6 +545,23 @@
     origin = (source_column * PLANES + position)[:, :, None] * QUARTER + jnp.arange(
         QUARTER, dtype=jnp.int32
     )
+    mine = lax.dynamic_index_in_dim(source, column, 0, keepdims=False)
+    back_hits = pair_hits(numbers, (mine % PLANES) * PLANES + mine // PLANES, code_all)
+    codes, back_hits = tied(codes, back_hits)
+    wide_parts, down_parts = (
+        [
+            own,
+            first,
+            lax.ppermute(own, PAIR, out_of_home),
+            second,
+            lax.ppermute(first, PAIR, both),
+            lax.ppermute(second, PAIR, to_home),
+        ]
+        for own, first, second in (
+            (wide, wide_first, wide_second),
+            (down, down_first, down_second),
+        )
+    )
     result = expert(
         numbers,
         arrived.reshape(PLANES, TP, 64, COLS),
@@ -558,17 +569,12 @@
         origin.reshape(512, 1),
         post_gain[None],
         router.T,
-        parts,
-    )
-    answers = lax.all_to_all(
-        result.reshape(32, 64, COLS), plane, split_axis=0, concat_axis=0, tiled=True
-    )
-    mine = lax.dynamic_index_in_dim(source, column, 0, keepdims=False)
-    rows_in_code = (mine % PLANES) * PLANES + mine // PLANES
-    sums = combine(numbers, rows_in_code, code_all, answers)
-    return lax.psum_scatter(
-        sums.reshape(PLANES * ROWS, COLS), "z", scatter_dimension=0, tiled=True
-    )
+        wide_parts,
+        down_parts,
+    )
+    answers = exchanged(result.reshape(32, 64, COLS))
+    sums = combine(back_hits, answers).reshape(PLANES * ROWS, COLS)
+    return lax.psum_scatter(sums, "z", scatter_dimension=0, tiled=True)
 
 
 def solution(mesh):

time: 260 us -> 229 us (0.88)
  waiting for transfers between devices: 88.3 us -> 44.3 us
  blocking collectives: 25 us -> 58 us
  starting transfers between devices: 61.2 us -> 44.5 us
  local copies, waits for them, and re-layouts: 16.4 us -> 7.35 us
  Pallas kernels: 43.4 us -> 47.7 us
    all_to_all x0 -> x1, blocking collectives: none -> 33.3 us  [exchanged(): lax.all_to_all(blocks, plane, split_axis=0, concat_axis=0, tiled=True)]
    all_to_all x2 -> x1, waiting for transfers between devices: 37.7 us -> 11.4 us  [exchanged(): lax.all_to_all(blocks, plane, split_axis=0, concat_axis=0, tiled=True)]
    ppermute x14, waiting for transfers between devices: 47.9 us -> 21.7 us  [around(): lax.ppermute(value, axis, [(i, (i + step) % count) for i in range(count)])]
    all_to_all x2 -> x1, starting transfers between devices: 19.3 us -> 8.7 us  [exchanged(): lax.all_to_all(blocks, plane, split_axis=0, concat_axis=0, tiled=True)]
    ppermute x6 -> x4, waiting for transfers between devices: 0.02 us -> 10.1 us  [the longest x1 7.33 us: per_device(): wide_first = lax.ppermute(wide, PAIR, first_move)]
    all_gather x1 -> x0, local copies, waits for them, and re-layouts: 4.39 us -> none  [per_device(): lax.all_gather(code_column, ('y', 'c'), axis=0)]
    pallas_call x3 -> x5, Pallas kernels: 25.7 us -> 30 us  [the longest x1 15.4 us: expert(): pl.pallas_call(expert_kernel, in_specs=[SM] + [VM] * 5 + [HB] * 12, out_s...]
    ppermute x6 -> x4, starting transfers between devices: 7.91 us -> 3.99 us  [the longest x1 2.04 us: per_device(): wide_second = lax.ppermute(wide_first, PAIR, second_move)]
  transfers between devices with their start and end apart: 34 -> 28, of which waited for: 14 -> 13; matrix products, arithmetic and copies ran while one was open for 7% -> 6% of each run, Pallas kernels for 9% -> 12%
where the time goes in v3:
time: 229 us; the launch traced here: 228 us
  blocking collectives  58 us (25%)
  Pallas kernels  47.7 us (21%)
  starting transfers between devices  44.5 us (19%)
  waiting for transfers between devices  44.3 us (19%)
  between operations  15.1 us (7%)
  other arithmetic  10.5 us (5%)
  local copies, waits for them, and re-layouts  7.35 us (3%)
    all_to_all x1, blocking collectives, exchanged(): lax.all_to_all(blocks, plane, split_axis=0, concat_axis=0, tiled=True)  33.3 us
    unnamed x1, blocking collectives  24.7 us
    ppermute x14, waiting for transfers between devices, around(): lax.ppermute(value, axis, [(i, (i + step) % count) for i in range(count)])  21.7 us
    ppermute x14, starting transfers between devices, around(): lax.ppermute(value, axis, [(i, (i + step) % count) for i in range(count)])  18 us
    pallas_call x1, Pallas kernels, expert(): pl.pallas_call(expert_kernel, in_specs=[SM] + [VM] * 5 + [HB] * 12, out_s...  15.4 us
    pallas_call x1, Pallas kernels, attention(): pl.pallas_call(attention_kernel, grid=(HEADS_HERE,), in_specs=[SM, pl.Blo...  11.6 us
    all_to_all x1, waiting for transfers between devices, exchanged(): lax.all_to_all(blocks, plane, split_axis=0, concat_axis=0, tiled=True)  11.4 us
    all_to_all x1, starting transfers between devices, exchanged(): lax.all_to_all(blocks, plane, split_axis=0, concat_axis=0, tiled=True)  8.7 us
  transfers between devices with their start and end apart: 28, of which 13 were waited for; matrix products, arithmetic and copies ran while one was open for 6% of the time, Pallas kernels for 12%

profile of v3, /device:TPU:32, one launch (start us, length us, event | category | flops | bytes accessed | tf_op | source)
XLA Modules:
  0.0 227.9 jit_solution(12849555916371254351)
XLA Ops:
  6.5 1.1 multiply_reduce_fusion
  7.8 2.8 %collective-permute-start.2 = (f32[2,132]{0,1:T(8,128)S(1)}, f32[2,132]{0,1:T(8,128)S(1)}, u32[]{:S(2)}, u32[]{:S(2)}) collective-permute-start(f32[2,132]{0,1:T(8,128)S(1)} %copy.28), channel_id=1, source_target_pairs={{0,3},{1,0},{2,1},{3,2},{4,7},{5,4},{6,5},{7,6},{8,11},{9,8},{10,9... | collective-permute-start | bytes 3176 | tf_op jit(solution)/shard_map/ppermute | solution.py:427
  10.6 0.8 collective-permute-start.1
  11.4 0.9 collective-permute-start
  12.3 1.7 pad_maximum_fusion.refs_0_
  14.0 2.5 %collective-permute-done.1 = f32[2,132]{0,1:T(8,128)S(1)} collective-permute-done((f32[2,132]{0,1:T(8,128)S(1)}, f32[2,132]{0,1:T(8,128)S(1)}, u32[]{:S(2)}, u32[]{:S(2)}) %collective-permute-start.1) | collective-permute-done | bytes 1088 | tf_op jit(solution)/shard_map/ppermute | solution.py:427
  16.5 0.7 collective-permute-done
  17.4 0.4 fusion.2
  17.8 0.7 pad.4
  19.2 0.6 pad_add_fusion.1.numbers
  19.8 0.7 fusion.34
  20.4 2.4 %fusion.29 = f32[132]{0:T(256)S(1)} fusion(s32[]{:T(128)} %bitcast.52, s32[]{:T(128)} %bitcast.12, s32[]{:T(128)} %bitcast.11, s32[]{:T(128)} %bitcast.10, s32[]{:T(128)} %bitcast.9), kind=kLoop, calls=%fused_computation.73 | loop fusion | flops 1320 | bytes 548 | tf_op jit(solution)/shard_map/convert_element_type | solution.py:480
  22.8 0.3 fusion.19
  23.2 0.8 pad_maximum_fusion.1
  23.9 0.6 rsqrt_bitcast_fusion.inv
  24.6 11.6 %attention.1 = (f32[132,512]{1,0:T(8,128)}, bf16[132,512]{1,0:T(8,128)(2,1)}, bf16[132,512]{1,0:T(8,128)(2,1)}, bf16[132,512]{1,0:T(8,128)(2,1)}) custom-call(s32[6]{0:T(128)} %pad_add_fusion.1.numbers, bf16[3,132,512]{2,1,0:T(8,128)(2,1)} %bitcast.55, f32[132,2]{1,0:T(8,128)} %rsqrt_bitcast_fusion.inv, f32[132,128]{1,0:T(8,128)} %get-tuple-element.66.cosine, ...), custom_call_target="tpu_custom_call" | custom-call | flops 2000000000 | bytes 10000000 | tf_op jit(solution)/shard_map/attention/pallas_call | solution.py:132
  36.2 7.3 %collective-permute-done.3.refs_1_ = bf16[4096,256]{1,0:T(8,128)(2,1)} collective-permute-done((bf16[4096,256]{1,0:T(8,128)(2,1)S(1)}, bf16[4096,256]{1,0:T(8,128)(2,1)}, u32[]{:S(2)}, u32[]{:S(2)}) %collective-permute-start.3) | collective-permute-done | bytes 2097184 | tf_op jit(solution)/shard_map/ppermute | solution.py:472
  43.5 1.2 collective-permute-start.6
  44.7 0.9 collective-permute-start.5
  45.6 4.5 %collective-permute-done.6 = bf16[132,512]{1,0:T(8,128)(2,1)S(1)} collective-permute-done((bf16[132,512]{1,0:T(8,128)(2,1)}, bf16[132,512]{1,0:T(8,128)(2,1)S(1)}, u32[]{:S(2)}, u32[]{:S(2)}) %collective-permute-start.6) | collective-permute-done | bytes 135200 | tf_op jit(solution)/shard_map/ppermute | solution.py:427
  50.0 2.1 collective-permute-done.5
  52.2 1.0 collective-permute-done.4
  53.2 1.1 add_convert_fusion.refs_0_
  54.3 2.0 collective-permute-start.7
  56.3 0.1 collective-permute-start.9
  56.4 2.0 collective-permute-start.16
  58.5 1.1 collective-permute-done.7.refs_1_
  59.6 2.5 %collective-permute-start.8 = (bf16[132,512]{1,0:T(8,128)(2,1)S(1)}, bf16[132,512]{1,0:T(8,128)(2,1)S(1)}, u32[]{:S(2)}, u32[]{:S(2)}) collective-permute-start(bf16[132,512]{1,0:T(8,128)(2,1)S(1)} %collective-permute-done.7.refs_1_), channel_id=1, source_target_pairs={{0,32},{32,64},{64,96},{96,128},{128,160},{160,192},{192,224},{224... | collective-permute-start | bytes 405512 | tf_op jit(solution)/shard_map/ppermute | solution.py:427
  62.1 1.4 collective-permute-start.10
  63.5 2.9 %collective-permute-done.8.refs_3_ = bf16[132,512]{1,0:T(8,128)(2,1)S(1)} collective-permute-done((bf16[132,512]{1,0:T(8,128)(2,1)S(1)}, bf16[132,512]{1,0:T(8,128)(2,1)S(1)}, u32[]{:S(2)}, u32[]{:S(2)}) %collective-permute-start.8) | collective-permute-done | bytes 135200 | tf_op jit(solution)/shard_map/ppermute | solution.py:427
  66.4 1.0 collective-permute-done.10.refs_4_
  67.4 1.8 slice.62.code
  69.2 0.2 collective-permute-start.15
  69.4 4.3 %collective-permute-start.17 = (bf16[4096,256]{1,0:T(8,128)(2,1)S(1)}, bf16[4096,256]{1,0:T(8,128)(2,1)}, u32[]{:S(2)}, u32[]{:S(2)}) collective-permute-start(bf16[4096,256]{1,0:T(8,128)(2,1)S(1)} %pad_maximum_fusion.refs_0_), channel_id=1, source_target_pairs={{0,4},{1,5},{6,2},{7,3},{8,12},{9,13},{14,10},{15,11},{16,20},{17,... | collective-permute-start | bytes 6291464 | tf_op jit(solution)/shard_map/ppermute | solution.py:555
  73.7 3.2 %collective-permute-start.11 = (bf16[132,512]{1,0:T(8,128)(2,1)S(1)}, bf16[132,512]{1,0:T(8,128)(2,1)S(1)}, u32[]{:S(2)}, u32[]{:S(2)}) collective-permute-start(bf16[132,512]{1,0:T(8,128)(2,1)S(1)} %collective-permute-done.8.refs_3_), channel_id=1, source_target_pairs={{0,32},{32,64},{64,96},{96,128},{128,160},{160,192},{192,224},{224... | collective-permute-start | bytes 405512 | tf_op jit(solution)/shard_map/ppermute | solution.py:427
  77.0 0.6 and_select_fusion.order
  77.5 5.7 %collective-permute-done.12.refs_6_ = bf16[132,512]{1,0:T(8,128)(2,1)S(1)} collective-permute-done((bf16[132,512]{1,0:T(8,128)(2,1)S(1)}, bf16[132,512]{1,0:T(8,128)(2,1)S(1)}, u32[]{:S(2)}, u32[]{:S(2)}) %collective-permute-start.12) | collective-permute-done | bytes 135200 | tf_op jit(solution)/shard_map/ppermute | solution.py:427
  83.3 0.6 pad_add_fusion.numbers
  83.9 2.1 collective-permute-start.13
  86.0 2.6 %pair_hits.3.hits = bf16[8,132,512]{2,1,0:T(8,128)(2,1)} custom-call(s32[4]{0:T(128)} %pad_add_fusion.numbers, s32[8]{0:T(128)} %and_select_fusion.order, bf16[8,136,128]{2,1,0:T(8,128)(2,1)} %slice.62.code), custom_call_target="tpu_custom_call" | custom-call | flops 700000000 | bytes 4000000 | tf_op jit(solution)/shard_map/pair_hits/pallas_call | solution.py:187
  88.7 2.8 %collective-permute-done.15.refs_7_ = bf16[256,2048]{1,0:T(8,128)(2,1)} collective-permute-done((bf16[256,2048]{1,0:T(8,128)(2,1)}, bf16[256,2048]{1,0:T(8,128)(2,1)}, u32[]{:S(2)}, u32[]{:S(2)}) %collective-permute-start.15) | collective-permute-done | bytes 1048608 | tf_op jit(solution)/shard_map/ppermute | solution.py:509
  91.5 1.6 collective-permute-start.21
  93.2 4.3 %expand.1 = bf16[32,64,512]{2,1,0:T(8,128)(2,1)} custom-call(bf16[8,132,512]{2,1,0:T(8,128)(2,1)} %pair_hits.3.hits, bf16[132,512]{1,0:T(8,128)(2,1)} %copy-done.1, bf16[132,512]{1,0:T(8,128)(2,1)} %copy-done.4, bf16[132,512]{1,0:T(8,128)(2,1)} %copy-done.5, bf16[132,512]{1,0:T(8,128)(2,1)} %copy-done.6, bf16[132,512]{1,0:T(8,128)(2,1)} %copy-done.7, ...), custom_call_target="tpu_custom_call" | custom-call | flops 700000000 | bytes 4000000 | tf_op jit(solution)/shard_map/expand/pallas_call | solution.py:218
  97.5 1.4 collective-permute-start.19
  98.9 8.7 %all-to-all-start = ((bf16[32,64,512]{2,1,0:T(8,128)(2,1)}), bf16[32,64,512]{2,1,0:T(8,128)(2,1)}, u32[]{:S(2)}, u32[]{:S(2)}) async-start(bf16[32,64,512]{2,1,0:T(8,128)(2,1)} %expand.1), calls=%async_computation | async-start | bytes 4194304 | tf_op jit(solution)/shard_map/all_to_all | solution.py:524
  107.7 3.1 %collective-permute-start.20 = (bf16[256,2048]{1,0:T(8,128)(2,1)S(1)}, bf16[256,2048]{1,0:T(8,128)(2,1)}, u32[]{:S(2)}, u32[]{:S(2)}) collective-permute-start(bf16[256,2048]{1,0:T(8,128)(2,1)S(1)} %bitcast.71), channel_id=1, source_target_pairs={{0,4},{1,5},{6,2},{7,3},{8,12},{9,13},{14,10},{15,11},{16,20},{17,... | collective-permute-start | bytes 3145736 | tf_op jit(solution)/shard_map/ppermute | solution.py:555
  110.8 1.5 collective-permute-start.23
  112.3 0.1 select_reduce_fusion
  112.5 0.2 dynamic-slice_reduce_fusion
  112.9 0.9 add.164.origin
  113.8 0.5 fusion.31.order
  114.3 6.1 %chosen_rows.1.codes = f32[8,64,128]{2,1,0:T(8,128)} custom-call(s32[4]{0:T(128)} %pad_add_fusion.numbers, bf16[64,136,128]{2,1,0:T(8,128)(2,1)} %all-gather.7.cloned.1.call-done.code), custom_call_target="tpu_custom_call" | custom-call | flops 200000000 | bytes 2000000 | tf_op jit(solution)/shard_map/chosen_rows/pallas_call | solution.py:279
  120.4 3.3 %pair_hits.2.hits = bf16[8,132,512]{2,1,0:T(8,128)(2,1)} custom-call(s32[4]{0:T(128)} %pad_add_fusion.numbers, s32[8]{0:T(128)} %fusion.31.order, bf16[64,136,128]{2,1,0:T(8,128)(2,1)} %all-gather.7.cloned.1.call-done.code), custom_call_target="tpu_custom_call" | custom-call | flops 700000000 | bytes 4000000 | tf_op jit(solution)/shard_map/pair_hits/pallas_call | solution.py:187
  123.7 11.4 %all-to-all-done = bf16[32,64,512]{2,1,0:T(8,128)(2,1)} async-done(((bf16[32,64,512]{2,1,0:T(8,128)(2,1)}), bf16[32,64,512]{2,1,0:T(8,128)(2,1)}, u32[]{:S(2)}, u32[]{:S(2)}) %all-to-all-start) | async-done | bytes 2097184 | tf_op jit(solution)/shard_map/all_to_all | solution.py:524
  135.1 15.4 %expert.1 = bf16[8,4,64,512]{3,2,1,0:T(8,128)(2,1)} custom-call(s32[4]{0:T(128)} %pad_add_fusion.numbers, bf16[8,4,64,512]{3,2,1,0:T(8,128)(2,1)} %bitcast.26.arrived, f32[8,64,128]{2,1,0:T(8,128)} %chosen_rows.1.codes, s32[512,1]{1,0:T(8,128)} %add.164.origin, f32[1,2048]{1,0:T(1,128)} %bitcast.73, bf16[64,2048]{1,0:T(8,128)(2,1)} %bitcast.72, ...), custom_call_target="tpu_custom_call" | custom-call | flops 8000000000 | bytes 20000000 | tf_op jit(solution)/shard_map/expert/pallas_call | solution.py:369
  150.5 33.3 %all_to_all.10.answers = bf16[32,64,512]{2,1,0:T(8,128)(2,1)} all-to-all(bf16[32,64,512]{2,1,0:T(8,128)(2,1)} %bitcast.53), channel_id=1, replica_groups=mesh['z'=8,'y'=4,'c'=2,'tp'=4] {'y','c','tp'}, dimensions={0} | all-to-all | bytes 4194304 | tf_op jit(solution)/shard_map/all_to_all | solution.py:524
  183.8 4.4 %combine.1 = bf16[8,132,512]{2,1,0:T(8,128)(2,1)} custom-call(bf16[8,132,512]{2,1,0:T(8,128)(2,1)} %pair_hits.2.hits, bf16[32,64,512]{2,1,0:T(8,128)(2,1)} %all_to_all.10.answers), custom_call_target="tpu_custom_call" | custom-call | flops 600000000 | bytes 4000000 | tf_op jit(solution)/shard_map/combine/pallas_call | solution.py:238
  188.2 1.3 reshape.69
  189.5 24.7 %fusion = bf16[136,512]{1,0:T(8,128)(2,1)S(1)} fusion(bf16[1056,512]{1,0:T(8,128)(2,1)S(1)} %reshape.69), kind=kCustom, calls=%all-reduce-scatter | all-reduce-scatter fusion | flops 557057 | bytes 1221632
  214.3 3.5 %collective-permute-start.24 = (bf16[28,512]{1,0:T(8,128)(2,1)S(1)}, bf16[28,512]{1,0:T(8,128)(2,1)S(1)}, u32[]{:S(2)}, u32[]{:S(2)}) collective-permute-start(bf16[28,512]{1,0:T(8,128)(2,1)S(1)} %slice.68), channel_id=1, source_target_pairs={{0,32},{32,64},{64,96},{96,128},{128,160},{160,192},{192,224},{1,3... | collective-permute-start | bytes 86024
  217.7 0.6 dynamic-slice.8
  219.0 1.1 collective-permute-done.24
  220.1 0.2 concatenate.16
  220.3 0.7 constant_dynamic-slice_fusion
  (70 shorter events, 0.8 us)
Async XLA Ops:
  6.5 57.0 %all-gather.5.cloned.1.call-start = ((), (), s32[]{:S(2)}) async-start(), calls=%async_computation.2 | async-start | bytes 1253376 | tf_op jit(solution)/shard_map/all_gather | solution.py:460
  7.8 6.2 %collective-permute-start.2 = (f32[2,132]{0,1:T(8,128)S(1)}, f32[2,132]{0,1:T(8,128)S(1)}, u32[]{:S(2)}, u32[]{:S(2)}) collective-permute-start(f32[2,132]{0,1:T(8,128)S(1)} %copy.28), channel_id=1, source_target_pairs={{0,3},{1,0},{2,1},{3,2},{4,7},{5,4},{6,5},{7,6},{8,11},{9,8},{10,9... | collective-permute-start | bytes 3176 | tf_op jit(solution)/shard_map/ppermute | solution.py:427
  10.6 5.9 %collective-permute-start.1 = (f32[2,132]{0,1:T(8,128)S(1)}, f32[2,132]{0,1:T(8,128)S(1)}, u32[]{:S(2)}, u32[]{:S(2)}) collective-permute-start(f32[2,132]{0,1:T(8,128)S(1)} %copy.28), channel_id=1, source_target_pairs={{0,2},{1,3},{2,0},{3,1},{4,6},{5,7},{6,4},{7,5},{8,10},{9,11},{10,... | collective-permute-start | bytes 3176 | tf_op jit(solution)/shard_map/ppermute | solution.py:427
  11.4 5.8 %collective-permute-start = (f32[2,132]{0,1:T(8,128)S(1)}, f32[2,132]{0,1:T(8,128)S(1)}, u32[]{:S(2)}, u32[]{:S(2)}) collective-permute-start(f32[2,132]{0,1:T(8,128)S(1)} %copy.28), channel_id=1, source_target_pairs={{0,1},{1,2},{2,3},{3,0},{4,5},{5,6},{6,7},{7,4},{8,9},{9,10},{10,1... | collective-permute-start | bytes 3176 | tf_op jit(solution)/shard_map/ppermute | solution.py:427
  12.3 5.1 %copy-start.11 = (s32[132,8]{0,1:T(8,128)S(1)}, s32[132,8]{0,1:T(8,128)}, u32[]{:S(2)}) copy-start(s32[132,8]{0,1:T(8,128)} %param.26) | copy-start | bytes 12676
  12.3 6.9 %copy-start.10 = (s32[4]{0:T(128)S(1)}, s32[4]{0:T(128)}, u32[]{:S(2)}) copy-start(s32[4]{0:T(128)} %param.24) | copy-start | bytes 52
  14.0 55.4 %copy-start = (bf16[4096,256]{1,0:T(8,128)(2,1)}, bf16[4096,256]{1,0:T(8,128)(2,1)S(1)}, u32[]{:S(2)}) copy-start(bf16[4096,256]{1,0:T(8,128)(2,1)S(1)} %pad_maximum_fusion.refs_0_) | copy-start | bytes 6291460
  17.3 26.2 %collective-permute-start.3 = (bf16[4096,256]{1,0:T(8,128)(2,1)S(1)}, bf16[4096,256]{1,0:T(8,128)(2,1)}, u32[]{:S(2)}, u32[]{:S(2)}) collective-permute-start(bf16[4096,256]{1,0:T(8,128)(2,1)S(1)} %pad_maximum_fusion.refs_0_), channel_id=1, source_target_pairs={{0,1},{1,0},{2,5},{3,4},{6,7},{7,6},{5,2},{4,3},{8,9},{9,8},{10,13... | collective-permute-start | bytes 6291464 | tf_op jit(solution)/shard_map/ppermute | solution.py:472
  18.5 95.8 %all-gather.7.cloned.1.call-start = ((), (), s32[]{:S(2)}) async-start(), calls=%async_computation.3 | async-start | bytes 2506752 | tf_op jit(solution)/shard_map/all_gather | solution.py:516
  24.6 52.4 %copy-start.16 = (s32[8]{0:T(128)S(1)}, s32[8]{0:T(128)}, u32[]{:S(2)}) copy-start(s32[8]{0:T(128)} %constant.153.clone) | copy-start | bytes 100
  43.5 6.6 %collective-permute-start.6 = (bf16[132,512]{1,0:T(8,128)(2,1)}, bf16[132,512]{1,0:T(8,128)(2,1)S(1)}, u32[]{:S(2)}, u32[]{:S(2)}) collective-permute-start(bf16[132,512]{1,0:T(8,128)(2,1)} %get-tuple-element.36), channel_id=1, source_target_pairs={{0,3},{1,0},{2,1},{3,2},{4,7},{5,4},{6,5},{7,6},{8,11},{9,8},{10,9... | collective-permute-start | bytes 405512 | tf_op jit(solution)/shard_map/ppermute | solution.py:427
  44.7 7.5 %collective-permute-start.5 = (bf16[132,512]{1,0:T(8,128)(2,1)}, bf16[132,512]{1,0:T(8,128)(2,1)S(1)}, u32[]{:S(2)}, u32[]{:S(2)}) collective-permute-start(bf16[132,512]{1,0:T(8,128)(2,1)} %get-tuple-element.35), channel_id=1, source_target_pairs={{0,2},{1,3},{2,0},{3,1},{4,6},{5,7},{6,4},{7,5},{8,10},{9,11},{10,... | collective-permute-start | bytes 405512 | tf_op jit(solution)/shard_map/ppermute | solution.py:427
  45.6 7.7 %collective-permute-start.4 = (bf16[132,512]{1,0:T(8,128)(2,1)}, bf16[132,512]{1,0:T(8,128)(2,1)S(1)}, u32[]{:S(2)}, u32[]{:S(2)}) collective-permute-start(bf16[132,512]{1,0:T(8,128)(2,1)} %get-tuple-element.34), channel_id=1, source_target_pairs={{0,1},{1,2},{2,3},{3,0},{4,5},{5,6},{6,7},{7,4},{8,9},{9,10},{10,1... | collective-permute-start | bytes 405512 | tf_op jit(solution)/shard_map/ppermute | solution.py:427
  54.3 38.8 %copy-start.1 = (bf16[132,512]{1,0:T(8,128)(2,1)}, bf16[132,512]{1,0:T(8,128)(2,1)S(1)}, u32[]{:S(2)}) copy-start(bf16[132,512]{1,0:T(8,128)(2,1)S(1)} %add_convert_fusion.refs_0_) | copy-start | bytes 405508
  54.3 5.3 %collective-permute-start.7 = (bf16[132,512]{1,0:T(8,128)(2,1)S(1)}, bf16[132,512]{1,0:T(8,128)(2,1)S(1)}, u32[]{:S(2)}, u32[]{:S(2)}) collective-permute-start(bf16[132,512]{1,0:T(8,128)(2,1)S(1)} %add_convert_fusion.refs_0_), channel_id=1, source_target_pairs={{0,32},{32,64},{64,96},{96,128},{128,160},{160,192},{192,224},{224... | collective-permute-start | bytes 405512 | tf_op jit(solution)/shard_map/ppermute | solution.py:427
  56.3 5.8 %collective-permute-start.9 = (bf16[132,512]{1,0:T(8,128)(2,1)S(1)}, bf16[132,512]{1,0:T(8,128)(2,1)S(1)}, u32[]{:S(2)}, u32[]{:S(2)}) collective-permute-start(bf16[132,512]{1,0:T(8,128)(2,1)S(1)} %add_convert_fusion.refs_0_), channel_id=1, source_target_pairs={{0,224},{32,0},{64,32},{96,64},{128,96},{160,128},{192,160},{224,1... | collective-permute-start | bytes 405512 | tf_op jit(solution)/shard_map/ppermute | solution.py:427
  56.4 41.1 %collective-permute-start.16 = (bf16[4096,256]{1,0:T(8,128)(2,1)}, bf16[4096,256]{1,0:T(8,128)(2,1)}, u32[]{:S(2)}, u32[]{:S(2)}) collective-permute-start(bf16[4096,256]{1,0:T(8,128)(2,1)} %collective-permute-done.3.refs_1_), channel_id=1, source_target_pairs={{4,5},{5,4},{2,3},{3,2},{12,13},{13,12},{10,11},{11,10},{20,21},{2... | collective-permute-start | bytes 6291464 | tf_op jit(solution)/shard_map/ppermute | solution.py:510
  59.6 33.5 %copy-start.4 = (bf16[132,512]{1,0:T(8,128)(2,1)}, bf16[132,512]{1,0:T(8,128)(2,1)S(1)}, u32[]{:S(2)}) copy-start(bf16[132,512]{1,0:T(8,128)(2,1)S(1)} %collective-permute-done.7.refs_1_) | copy-start | bytes 405508
  59.6 6.8 %collective-permute-start.8 = (bf16[132,512]{1,0:T(8,128)(2,1)S(1)}, bf16[132,512]{1,0:T(8,128)(2,1)S(1)}, u32[]{:S(2)}, u32[]{:S(2)}) collective-permute-start(bf16[132,512]{1,0:T(8,128)(2,1)S(1)} %collective-permute-done.7.refs_1_), channel_id=1, source_target_pairs={{0,32},{32,64},{64,96},{96,128},{128,160},{160,192},{192,224},{224... | collective-permute-start | bytes 405512 | tf_op jit(solution)/shard_map/ppermute | solution.py:427
  62.1 31.1 %copy-start.5 = (bf16[132,512]{1,0:T(8,128)(2,1)}, bf16[132,512]{1,0:T(8,128)(2,1)S(1)}, u32[]{:S(2)}) copy-start(bf16[132,512]{1,0:T(8,128)(2,1)S(1)} %collective-permute-done.9.refs_2_) | copy-start | bytes 405508
  62.1 5.3 %collective-permute-start.10 = (bf16[132,512]{1,0:T(8,128)(2,1)S(1)}, bf16[132,512]{1,0:T(8,128)(2,1)S(1)}, u32[]{:S(2)}, u32[]{:S(2)}) collective-permute-start(bf16[132,512]{1,0:T(8,128)(2,1)S(1)} %collective-permute-done.9.refs_2_), channel_id=1, source_target_pairs={{0,224},{32,0},{64,32},{96,64},{128,96},{160,128},{192,160},{224,1... | collective-permute-start | bytes 405512 | tf_op jit(solution)/shard_map/ppermute | solution.py:427
  66.4 26.7 %copy-start.6 = (bf16[132,512]{1,0:T(8,128)(2,1)}, bf16[132,512]{1,0:T(8,128)(2,1)S(1)}, u32[]{:S(2)}) copy-start(bf16[132,512]{1,0:T(8,128)(2,1)S(1)} %collective-permute-done.8.refs_3_) | copy-start | bytes 405508
  67.4 25.7 %copy-start.7 = (bf16[132,512]{1,0:T(8,128)(2,1)}, bf16[132,512]{1,0:T(8,128)(2,1)S(1)}, u32[]{:S(2)}) copy-start(bf16[132,512]{1,0:T(8,128)(2,1)S(1)} %collective-permute-done.10.refs_4_) | copy-start | bytes 405508
  69.2 22.3 %collective-permute-start.15 = (bf16[256,2048]{1,0:T(8,128)(2,1)}, bf16[256,2048]{1,0:T(8,128)(2,1)}, u32[]{:S(2)}, u32[]{:S(2)}) collective-permute-start(bf16[256,2048]{1,0:T(8,128)(2,1)} %bitcast.69), channel_id=1, source_target_pairs={{0,1},{1,0},{2,5},{3,4},{6,7},{7,6},{5,2},{4,3},{8,9},{9,8},{10,13... | collective-permute-start | bytes 3145736 | tf_op jit(solution)/shard_map/ppermute | solution.py:509
  69.4 41.3 %collective-permute-start.17 = (bf16[4096,256]{1,0:T(8,128)(2,1)S(1)}, bf16[4096,256]{1,0:T(8,128)(2,1)}, u32[]{:S(2)}, u32[]{:S(2)}) collective-permute-start(bf16[4096,256]{1,0:T(8,128)(2,1)S(1)} %pad_maximum_fusion.refs_0_), channel_id=1, source_target_pairs={{0,4},{1,5},{6,2},{7,3},{8,12},{9,13},{14,10},{15,11},{16,20},{17,... | collective-permute-start | bytes 6291464 | tf_op jit(solution)/shard_map/ppermute | solution.py:555
  73.7 10.2 %collective-permute-start.11 = (bf16[132,512]{1,0:T(8,128)(2,1)S(1)}, bf16[132,512]{1,0:T(8,128)(2,1)S(1)}, u32[]{:S(2)}, u32[]{:S(2)}) collective-permute-start(bf16[132,512]{1,0:T(8,128)(2,1)S(1)} %collective-permute-done.8.refs_3_), channel_id=1, source_target_pairs={{0,32},{32,64},{64,96},{96,128},{128,160},{160,192},{192,224},{224... | collective-permute-start | bytes 405512 | tf_op jit(solution)/shard_map/ppermute | solution.py:427
  77.0 6.3 %collective-permute-start.12 = (bf16[132,512]{1,0:T(8,128)(2,1)S(1)}, bf16[132,512]{1,0:T(8,128)(2,1)S(1)}, u32[]{:S(2)}, u32[]{:S(2)}) collective-permute-start(bf16[132,512]{1,0:T(8,128)(2,1)S(1)} %collective-permute-done.10.refs_4_), channel_id=1, source_target_pairs={{0,224},{32,0},{64,32},{96,64},{128,96},{160,128},{192,160},{224,1... | collective-permute-start | bytes 405512 | tf_op jit(solution)/shard_map/ppermute | solution.py:427
  83.2 9.9 %copy-start.2 = (bf16[132,512]{1,0:T(8,128)(2,1)}, bf16[132,512]{1,0:T(8,128)(2,1)S(1)}, u32[]{:S(2)}) copy-start(bf16[132,512]{1,0:T(8,128)(2,1)S(1)} %collective-permute-done.12.refs_6_) | copy-start | bytes 405508
  83.3 5.4 %collective-permute-start.14 = (bf16[68,512]{1,0:T(8,128)(2,1)S(1)}, bf16[68,512]{1,0:T(8,128)(2,1)S(1)}, u32[]{:S(2)}, u32[]{:S(2)}) collective-permute-start(bf16[68,512]{1,0:T(8,128)(2,1)S(1)} %slice.67), channel_id=1, source_target_pairs={{0,224},{32,0},{64,32},{96,64},{128,96},{160,128},{192,160},{224,1... | collective-permute-start | bytes 208904 | tf_op jit(solution)/shard_map/ppermute | solution.py:427
  83.9 9.2 %copy-start.3 = (bf16[132,512]{1,0:T(8,128)(2,1)}, bf16[132,512]{1,0:T(8,128)(2,1)S(1)}, u32[]{:S(2)}) copy-start(bf16[132,512]{1,0:T(8,128)(2,1)S(1)} %collective-permute-done.11.refs_5_) | copy-start | bytes 405508
  83.9 4.7 %collective-permute-start.13 = (bf16[64,512]{1,0:T(8,128)(2,1)S(1)}, bf16[64,512]{1,0:T(8,128)(2,1)S(1)}, u32[]{:S(2)}, u32[]{:S(2)}) collective-permute-start(bf16[64,512]{1,0:T(8,128)(2,1)S(1)} %slice.66), channel_id=1, source_target_pairs={{0,32},{32,64},{64,96},{96,128},{128,160},{160,192},{192,224},{224... | collective-permute-start | bytes 196616 | tf_op jit(solution)/shard_map/ppermute | solution.py:427
  88.7 4.5 %copy-start.9 = (bf16[64,512]{1,0:T(8,128)(2,1)}, bf16[64,512]{1,0:T(8,128)(2,1)S(1)}, u32[]{:S(2)}) copy-start(bf16[64,512]{1,0:T(8,128)(2,1)S(1)} %collective-permute-done.13.refs_7_) | copy-start | bytes 196612
  88.7 35.0 %collective-permute-start.18 = (bf16[4096,256]{1,0:T(8,128)(2,1)}, bf16[4096,256]{1,0:T(8,128)(2,1)}, u32[]{:S(2)}, u32[]{:S(2)}) collective-permute-start(bf16[4096,256]{1,0:T(8,128)(2,1)} %collective-permute-done.3.refs_1_), channel_id=1, source_target_pairs={{0,4},{1,5},{2,6},{3,7},{4,0},{5,1},{6,2},{7,3},{8,12},{9,13},{10,... | collective-permute-start | bytes 6291464 | tf_op jit(solution)/shard_map/ppermute | solution.py:557
  88.7 4.5 %copy-start.8 = (bf16[68,512]{1,0:T(8,128)(2,1)}, bf16[68,512]{1,0:T(8,128)(2,1)S(1)}, u32[]{:S(2)}) copy-start(bf16[68,512]{1,0:T(8,128)(2,1)S(1)} %collective-permute-done.14.refs_8_) | copy-start | bytes 208900
  91.5 19.3 %collective-permute-start.21 = (bf16[256,2048]{1,0:T(8,128)(2,1)}, bf16[256,2048]{1,0:T(8,128)(2,1)}, u32[]{:S(2)}, u32[]{:S(2)}) collective-permute-start(bf16[256,2048]{1,0:T(8,128)(2,1)} %collective-permute-done.15.refs_7_), channel_id=1, source_target_pairs={{4,5},{5,4},{2,3},{3,2},{12,13},{13,12},{10,11},{11,10},{20,21},{2... | collective-permute-start | bytes 3145736 | tf_op jit(solution)/shard_map/ppermute | solution.py:529
  97.5 10.1 %copy-start.13 = (bf16[1,256,2048]{2,1,0:T(8,128)(2,1)S(1)}, bf16[1,256,2048]{2,1,0:T(8,128)(2,1)}, u32[]{:S(2)}) copy-start(bf16[1,256,2048]{2,1,0:T(8,128)(2,1)} %param.32) | copy-start | bytes 3145732
  97.5 14.8 %copy-start.15 = (s32[64]{0:T(128)S(1)}, s32[64]{0:T(128)}, u32[]{:S(2)}) copy-start(s32[64]{0:T(128)} %param.25) | copy-start | bytes 772
  97.5 37.6 %collective-permute-start.19 = (bf16[4096,256]{1,0:T(8,128)(2,1)}, bf16[4096,256]{1,0:T(8,128)(2,1)}, u32[]{:S(2)}, u32[]{:S(2)}) collective-permute-start(bf16[4096,256]{1,0:T(8,128)(2,1)} %collective-permute-done.16.refs_3_), channel_id=1, source_target_pairs={{4,0},{5,1},{2,6},{3,7},{12,8},{13,9},{10,14},{11,15},{20,16},{21,... | collective-permute-start | bytes 6291464 | tf_op jit(solution)/shard_map/ppermute | solution.py:558
  98.9 36.1 %all-to-all-start = ((bf16[32,64,512]{2,1,0:T(8,128)(2,1)}), bf16[32,64,512]{2,1,0:T(8,128)(2,1)}, u32[]{:S(2)}, u32[]{:S(2)}) async-start(bf16[32,64,512]{2,1,0:T(8,128)(2,1)} %expand.1), calls=%async_computation | async-start | bytes 4194304 | tf_op jit(solution)/shard_map/all_to_all | solution.py:524
  107.7 16.0 %collective-permute-start.20 = (bf16[256,2048]{1,0:T(8,128)(2,1)S(1)}, bf16[256,2048]{1,0:T(8,128)(2,1)}, u32[]{:S(2)}, u32[]{:S(2)}) collective-permute-start(bf16[256,2048]{1,0:T(8,128)(2,1)S(1)} %bitcast.71), channel_id=1, source_target_pairs={{0,4},{1,5},{6,2},{7,3},{8,12},{9,13},{14,10},{15,11},{16,20},{17,... | collective-permute-start | bytes 3145736 | tf_op jit(solution)/shard_map/ppermute | solution.py:555
  110.8 12.9 %collective-permute-start.22 = (bf16[256,2048]{1,0:T(8,128)(2,1)}, bf16[256,2048]{1,0:T(8,128)(2,1)S(1)}, u32[]{:S(2)}, u32[]{:S(2)}) collective-permute-start(bf16[256,2048]{1,0:T(8,128)(2,1)} %collective-permute-done.15.refs_7_), channel_id=1, source_target_pairs={{0,4},{1,5},{2,6},{3,7},{4,0},{5,1},{6,2},{7,3},{8,12},{9,13},{10,... | collective-permute-start | bytes 3145736 | tf_op jit(solution)/shard_map/ppermute | solution.py:557
  110.8 12.9 %collective-permute-start.23 = (bf16[256,2048]{1,0:T(8,128)(2,1)}, bf16[256,2048]{1,0:T(8,128)(2,1)}, u32[]{:S(2)}, u32[]{:S(2)}) collective-permute-start(bf16[256,2048]{1,0:T(8,128)(2,1)} %collective-permute-done.21.refs_9_), channel_id=1, source_target_pairs={{4,0},{5,1},{2,6},{3,7},{12,8},{13,9},{10,14},{11,15},{20,16},{21,... | collective-permute-start | bytes 3145736 | tf_op jit(solution)/shard_map/ppermute | solution.py:558
  123.7 11.4 %copy-start.14 = (bf16[256,2048]{1,0:T(8,128)(2,1)}, bf16[256,2048]{1,0:T(8,128)(2,1)S(1)}, u32[]{:S(2)}) copy-start(bf16[256,2048]{1,0:T(8,128)(2,1)S(1)} %collective-permute-done.22.refs_10_) | copy-start | bytes 3145732
  188.2 29.6 %copy-start.12 = (u32[256]{0:T(256)S(1)}, u32[256]{0:T(256)}, u32[]{:S(2)}) copy-start(u32[256]{0:T(256)} %constant.168) | copy-start | bytes 3076
  214.3 5.8 %collective-permute-start.24 = (bf16[28,512]{1,0:T(8,128)(2,1)S(1)}, bf16[28,512]{1,0:T(8,128)(2,1)S(1)}, u32[]{:S(2)}, u32[]{:S(2)}) collective-permute-start(bf16[28,512]{1,0:T(8,128)(2,1)S(1)} %slice.68), channel_id=1, source_target_pairs={{0,32},{32,64},{64,96},{96,128},{128,160},{160,192},{192,224},{1,3... | collective-permute-start | bytes 86024
Sparse Core Ops, SparseCore 0:
  18.6 40.0 all-gather.4
  69.3 29.3 all-gather.6

commit v4 on v3

--- a/solution.py
+++ b/solution.py
@@ -289,15 +289,12 @@
     )(numbers, code)
 
 
-def weight_copies(parts, target, sems, at_home, begin):
+def await_quarter(parts, target, sems, quarter):
+    pltpu.make_async_copy(parts[1], target(None, quarter), sems.at[quarter]).wait()
+
+
+def bring_quarters(parts, target, sems, at_home):
     own, first, other_own, second, other_first, other_second = parts
-    if not begin:
-        for quarter in range(4):
-            pltpu.make_async_copy(
-                target(first), target(None, quarter), sems.at[quarter]
-            ).wait()
-        return
-
     def bring(source, quarter):
         pltpu.make_async_copy(
             target(source), target(None, quarter), sems.at[quarter]
@@ -325,8 +322,8 @@
     to_down = lambda source, quarter=None: (
         down.at[quarter * 256 : (quarter + 1) * 256] if source is None else source
     )
-    weight_copies(wide_parts, to_wide, sems.at[0], at_home, True)
-    weight_copies(down_parts, to_down, sems.at[1], at_home, True)
+    bring_quarters(wide_parts, to_wide, sems.at[0], at_home)
+    bring_quarters(down_parts, to_down, sems.at[1], at_home)
 
     squares = jnp.zeros((512, 1), F32)
     for x in range(TP):
@@ -348,14 +345,15 @@
     mark = jnp.sum(jnp.where(is_expert, code, 0.0), axis=1, keepdims=True)
     first_choice = (mark > 64.0).astype(F32)
 
-    weight_copies(wide_parts, to_wide, sems.at[0], at_home, False)
-    for quarter in range(4):
+    for quarter in (0, 3, 1, 2):
+        await_quarter(wide_parts, to_wide, sems.at[0], quarter)
         gate_pre = dot(normed[...], wide[quarter, :FULL])
         up_pre = dot(normed[...], wide[quarter, FULL:])
         hidden[:, quarter * 256 : (quarter + 1) * 256] = (
             gate_pre / (1.0 + jnp.exp(-gate_pre)) * up_pre
         ).astype(BF)
-    weight_copies(down_parts, to_down, sems.at[1], at_home, False)
+    for quarter in range(4):
+        await_quarter(down_parts, to_down, sems.at[1], quarter)
     move = (origin[...] == iota((512, 512), 1)).astype(F32).astype(BF)
     for x in range(TP):
         span = slice(x * COLS, (x + 1) * COLS)
@@ -470,6 +468,8 @@
     squares = squares + shared[0] + shared[1] + shared[2]
     squares, wide = tied(squares, wide)
     wide_first = lax.ppermute(wide, PAIR, first_move)
+    wide_other = lax.ppermute(wide, PAIR, out_of_home)
+    down_other = lax.ppermute(down, PAIR, out_of_home)
     inv = lax.rsqrt(squares / FULL + 1e-05).T
     spot = jnp.arange(ROWS, dtype=jnp.int32)
     positions = offsets[0] + spot
@@ -494,7 +494,9 @@
         decode_cache,
         out_weight,
     )
-    *sends, wide_first = tied(*sends, wide_first)
+    *sends, wide_first, wide_other, down_other = tied(
+        *sends, wide_first, wide_other, down_other
+    )
     state = own
     for step in range(1, TP):
         state = state + around(sends[step - 1], "tp", step).astype(F32)
@@ -525,10 +527,9 @@
 
     up_3, down_3 = around(up_2, "z", 1), around(down_2, "z", -1)
     far = [around(up_3[:64], "z", 1), around(down_3[64:], "z", -1)]
-    *far, down_first = tied(*far, down_first)
+    outgoing = expand(out_hits, [state, up_1, down_1, up_2, down_2, up_3, down_3, *far])
+    outgoing, wide_second, down_first = tied(outgoing, wide_second, down_first)
     down_second = lax.ppermute(down_first, PAIR, second_move)
-    outgoing = expand(out_hits, [state, up_1, down_1, up_2, down_2, up_3, down_3, *far])
-    outgoing, wide_second = tied(outgoing, wide_second)
     arrived = exchanged(outgoing)
     codes = chosen_rows(numbers, code_all)
 
@@ -552,14 +553,14 @@
         [
             own,
             first,
-            lax.ppermute(own, PAIR, out_of_home),
+            other_own,
             second,
             lax.ppermute(first, PAIR, both),
             lax.ppermute(second, PAIR, to_home),
         ]
-        for own, first, second in (
-            (wide, wide_first, wide_second),
-            (down, down_first, down_second),
+        for own, first, other_own, second in (
+            (wide, wide_first, wide_other, wide_second),
+            (down, down_first, down_other, down_second),
         )
     )
     result = expert(

time: 229 us -> 233 us (1.017)
  waiting for transfers between devices: 44.3 us -> 47.9 us
  local copies, waits for them, and re-layouts: 7.35 us -> 9.78 us
    all_to_all x1, waiting for transfers between devices: 11.4 us -> 19 us  [exchanged(): lax.all_to_all(blocks, plane, split_axis=0, concat_axis=0, tiled=True)]
    ppermute x1, waiting for transfers between devices: 7.33 us -> 1.04 us  [per_device(): wide_first = lax.ppermute(wide, PAIR, first_move)]
    ppermute x14, waiting for transfers between devices: 21.7 us -> 24.4 us  [around(): lax.ppermute(value, axis, [(i, (i + step) % count) for i in range(count)])]
    unnamed x38 -> x40, local copies, waits for them, and re-layouts: 1.58 us -> 4.05 us
    all_to_all x1, starting transfers between devices: 8.7 us -> 11 us  [exchanged(): lax.all_to_all(blocks, plane, split_axis=0, concat_axis=0, tiled=True)]
  transfers between devices with their start and end apart: 28 -> 28, of which waited for: 13 -> 14; matrix products, arithmetic and copies ran while one was open for 6% -> 6% of each run, Pallas kernels for 12% -> 12%
where the time goes in v4:
time: 233 us
  blocking collectives  58.2 us (25%)
  waiting for transfers between devices  47.9 us (21%)
  Pallas kernels  46.6 us (20%)
  starting transfers between devices  44 us (19%)
  between operations  15 us (6%)
  other arithmetic  10.7 us (5%)
  local copies, waits for them, and re-layouts  9.78 us (4%)
    all_to_all x1, blocking collectives, exchanged(): lax.all_to_all(blocks, plane, split_axis=0, concat_axis=0, tiled=True)  33 us
    unnamed x1, blocking collectives  25.2 us
    ppermute x14, waiting for transfers between devices, around(): lax.ppermute(value, axis, [(i, (i + step) % count) for i in range(count)])  24.4 us
    all_to_all x1, waiting for transfers between devices, exchanged(): lax.all_to_all(blocks, plane, split_axis=0, concat_axis=0, tiled=True)  19 us
    ppermute x14, starting transfers between devices, around(): lax.ppermute(value, axis, [(i, (i + step) % count) for i in range(count)])  17.8 us
    pallas_call x1, Pallas kernels, expert(): pl.pallas_call(expert_kernel, in_specs=[SM] + [VM] * 5 + [HB] * 12, out_s...  14.3 us
    pallas_call x1, Pallas kernels, attention(): pl.pallas_call(attention_kernel, grid=(HEADS_HERE,), in_specs=[SM, pl.Blo...  11.6 us
    all_to_all x1, starting transfers between devices, exchanged(): lax.all_to_all(blocks, plane, split_axis=0, concat_axis=0, tiled=True)  11 us
  transfers between devices with their start and end apart: 28, of which 14 were waited for; matrix products, arithmetic and copies ran while one was open for 6% of the time, Pallas kernels for 12%

profile of v4, /device:TPU:32, one launch (start us, length us, event | category | flops | bytes accessed | tf_op | source)
XLA Modules:
  0.0 232.7 jit_solution(6128092961077838946)
XLA Ops:
  6.5 1.1 multiply_reduce_fusion
  7.8 2.8 %collective-permute-start.2 = (f32[2,132]{0,1:T(8,128)S(1)}, f32[2,132]{0,1:T(8,128)S(1)}, u32[]{:S(2)}, u32[]{:S(2)}) collective-permute-start(f32[2,132]{0,1:T(8,128)S(1)} %copy.28), channel_id=1, source_target_pairs={{0,3},{1,0},{2,1},{3,2},{4,7},{5,4},{6,5},{7,6},{8,11},{9,8},{10,9... | collective-permute-start | bytes 3176 | tf_op jit(solution)/shard_map/ppermute | solution.py:425
  10.6 0.8 collective-permute-start.1
  11.4 0.9 collective-permute-start
  12.3 1.8 pad_maximum_fusion.refs_0_
  14.1 2.4 %collective-permute-done.1 = f32[2,132]{0,1:T(8,128)S(1)} collective-permute-done((f32[2,132]{0,1:T(8,128)S(1)}, f32[2,132]{0,1:T(8,128)S(1)}, u32[]{:S(2)}, u32[]{:S(2)}) %collective-permute-start.1) | collective-permute-done | bytes 1088 | tf_op jit(solution)/shard_map/ppermute | solution.py:425
  16.5 0.7 collective-permute-done
  17.4 4.0 %collective-permute-start.4 = (bf16[4096,256]{1,0:T(8,128)(2,1)S(1)}, bf16[4096,256]{1,0:T(8,128)(2,1)}, u32[]{:S(2)}, u32[]{:S(2)}) collective-permute-start(bf16[4096,256]{1,0:T(8,128)(2,1)S(1)} %pad_maximum_fusion.refs_0_), channel_id=1, source_target_pairs={{0,4},{1,5},{6,2},{7,3},{8,12},{9,13},{14,10},{15,11},{16,20},{17,... | collective-permute-start | bytes 6291464 | tf_op jit(solution)/shard_map/ppermute | solution.py:471
  21.3 0.4 fusion.2
  21.7 0.7 pad.4
  22.5 2.3 collective-permute-start.5
  25.4 0.6 pad_add_fusion.1.numbers
  26.0 0.7 fusion.34
  26.7 2.4 %fusion.29 = f32[132]{0:T(256)S(1)} fusion(s32[]{:T(128)} %bitcast.52, s32[]{:T(128)} %bitcast.12, s32[]{:T(128)} %bitcast.11, s32[]{:T(128)} %bitcast.10, s32[]{:T(128)} %bitcast.9), kind=kLoop, calls=%fused_computation.73 | loop fusion | flops 1320 | bytes 548 | tf_op jit(solution)/shard_map/convert_element_type | solution.py:480
  29.4 0.8 pad_maximum_fusion.1
  30.2 0.6 rsqrt_bitcast_fusion.inv
  30.8 11.6 %attention.1 = (f32[132,512]{1,0:T(8,128)}, bf16[132,512]{1,0:T(8,128)(2,1)}, bf16[132,512]{1,0:T(8,128)(2,1)}, bf16[132,512]{1,0:T(8,128)(2,1)}) custom-call(s32[6]{0:T(128)} %pad_add_fusion.1.numbers, bf16[3,132,512]{2,1,0:T(8,128)(2,1)} %bitcast.56, f32[132,2]{1,0:T(8,128)} %rsqrt_bitcast_fusion.inv, f32[132,128]{1,0:T(8,128)} %get-tuple-element.66.cosine, ...), custom_call_target="tpu_custom_call" | custom-call | flops 2000000000 | bytes 10000000 | tf_op jit(solution)/shard_map/attention/pallas_call | solution.py:132
  42.4 1.0 collective-permute-done.3.refs_1_
  43.5 1.2 collective-permute-start.8
  44.7 0.9 collective-permute-start.7
  45.6 4.5 %collective-permute-done.8 = bf16[132,512]{1,0:T(8,128)(2,1)S(1)} collective-permute-done((bf16[132,512]{1,0:T(8,128)(2,1)}, bf16[132,512]{1,0:T(8,128)(2,1)S(1)}, u32[]{:S(2)}, u32[]{:S(2)}) %collective-permute-start.8) | collective-permute-done | bytes 135200 | tf_op jit(solution)/shard_map/ppermute | solution.py:425
  50.0 2.4 %collective-permute-done.7 = bf16[132,512]{1,0:T(8,128)(2,1)S(1)} collective-permute-done((bf16[132,512]{1,0:T(8,128)(2,1)}, bf16[132,512]{1,0:T(8,128)(2,1)S(1)}, u32[]{:S(2)}, u32[]{:S(2)}) %collective-permute-start.7) | collective-permute-done | bytes 135200 | tf_op jit(solution)/shard_map/ppermute | solution.py:425
  52.4 1.4 collective-permute-done.6
  53.9 1.1 add_convert_fusion.refs_0_
  55.0 2.0 collective-permute-start.9
  57.1 2.0 collective-permute-start.17
  59.0 1.6 collective-permute-done.9.refs_1_
  60.7 1.6 collective-permute-start.10
  62.2 2.1 collective-permute-start.12
  64.3 2.9 %collective-permute-done.10.refs_3_ = bf16[132,512]{1,0:T(8,128)(2,1)S(1)} collective-permute-done((bf16[132,512]{1,0:T(8,128)(2,1)S(1)}, bf16[132,512]{1,0:T(8,128)(2,1)S(1)}, u32[]{:S(2)}, u32[]{:S(2)}) %collective-permute-start.10) | collective-permute-done | bytes 135200 | tf_op jit(solution)/shard_map/ppermute | solution.py:425
  67.3 0.8 collective-permute-done.12.refs_4_
  68.1 1.7 slice.62.code
  69.8 0.4 collective-permute-start.18
  70.2 3.2 %collective-permute-start.13 = (bf16[132,512]{1,0:T(8,128)(2,1)S(1)}, bf16[132,512]{1,0:T(8,128)(2,1)S(1)}, u32[]{:S(2)}, u32[]{:S(2)}) collective-permute-start(bf16[132,512]{1,0:T(8,128)(2,1)S(1)} %collective-permute-done.10.refs_3_), channel_id=1, source_target_pairs={{0,32},{32,64},{64,96},{96,128},{128,160},{160,192},{192,224},{224... | collective-permute-start | bytes 405512 | tf_op jit(solution)/shard_map/ppermute | solution.py:425
  73.4 0.6 and_select_fusion.order
  74.0 6.8 %collective-permute-done.14.refs_6_ = bf16[132,512]{1,0:T(8,128)(2,1)S(1)} collective-permute-done((bf16[132,512]{1,0:T(8,128)(2,1)S(1)}, bf16[132,512]{1,0:T(8,128)(2,1)S(1)}, u32[]{:S(2)}, u32[]{:S(2)}) %collective-permute-start.14) | collective-permute-done | bytes 135200 | tf_op jit(solution)/shard_map/ppermute | solution.py:425
  80.9 0.7 pad_add_fusion.numbers
  81.6 2.1 collective-permute-start.15
  83.7 2.6 %pair_hits.3.hits = bf16[8,132,512]{2,1,0:T(8,128)(2,1)} custom-call(s32[4]{0:T(128)} %pad_add_fusion.numbers, s32[8]{0:T(128)} %and_select_fusion.order, bf16[8,136,128]{2,1,0:T(8,128)(2,1)} %slice.62.code), custom_call_target="tpu_custom_call" | custom-call | flops 700000000 | bytes 4000000 | tf_op jit(solution)/shard_map/pair_hits/pallas_call | solution.py:187
  86.3 0.8 collective-permute-done.15.refs_7_
  87.2 0.6 copy-done.10
  87.7 0.6 copy-done.9
  88.4 4.3 %expand.1 = bf16[32,64,512]{2,1,0:T(8,128)(2,1)} custom-call(bf16[8,132,512]{2,1,0:T(8,128)(2,1)} %pair_hits.3.hits, bf16[132,512]{1,0:T(8,128)(2,1)} %copy-done.2, bf16[132,512]{1,0:T(8,128)(2,1)} %copy-done.5, bf16[132,512]{1,0:T(8,128)(2,1)} %copy-done.6, bf16[132,512]{1,0:T(8,128)(2,1)} %copy-done.7, bf16[132,512]{1,0:T(8,128)(2,1)} %copy-done.8, ...), custom_call_target="tpu_custom_call" | custom-call | flops 700000000 | bytes 4000000 | tf_op jit(solution)/shard_map/expand/pallas_call | solution.py:218
  92.7 1.6 collective-permute-done.18.refs_7_
  94.3 1.3 collective-permute-start.20
  95.6 0.7 collective-permute-start.21
  96.3 11.0 %all-to-all-start = ((bf16[32,64,512]{2,1,0:T(8,128)(2,1)}), bf16[32,64,512]{2,1,0:T(8,128)(2,1)S(1)}, u32[]{:S(2)}, u32[]{:S(2)}) async-start(bf16[32,64,512]{2,1,0:T(8,128)(2,1)} %expand.1), calls=%async_computation | async-start | bytes 4194304 | tf_op jit(solution)/shard_map/all_to_all | solution.py:526
  107.4 0.4 collective-permute-start.22
  107.8 1.3 collective-permute-start.23
  109.6 0.9 add.164.origin
  110.5 0.5 fusion.31.order
  111.0 6.1 %chosen_rows.1.codes = f32[8,64,128]{2,1,0:T(8,128)} custom-call(s32[4]{0:T(128)} %pad_add_fusion.numbers, bf16[64,136,128]{2,1,0:T(8,128)(2,1)} %all-gather.7.cloned.1.call-done.code), custom_call_target="tpu_custom_call" | custom-call | flops 200000000 | bytes 2000000 | tf_op jit(solution)/shard_map/chosen_rows/pallas_call | solution.py:279
  117.1 3.3 %pair_hits.2.hits = bf16[8,132,512]{2,1,0:T(8,128)(2,1)} custom-call(s32[4]{0:T(128)} %pad_add_fusion.numbers, s32[8]{0:T(128)} %fusion.31.order, bf16[64,136,128]{2,1,0:T(8,128)(2,1)} %all-gather.7.cloned.1.call-done.code), custom_call_target="tpu_custom_call" | custom-call | flops 700000000 | bytes 4000000 | tf_op jit(solution)/shard_map/pair_hits/pallas_call | solution.py:187
  120.4 19.0 %all-to-all-done = bf16[32,64,512]{2,1,0:T(8,128)(2,1)S(1)} async-done(((bf16[32,64,512]{2,1,0:T(8,128)(2,1)}), bf16[32,64,512]{2,1,0:T(8,128)(2,1)S(1)}, u32[]{:S(2)}, u32[]{:S(2)}) %all-to-all-start) | async-done | bytes 2097184 | tf_op jit(solution)/shard_map/all_to_all | solution.py:526
  139.5 1.3 copy-done.1
  140.8 14.3 %expert.1 = bf16[8,4,64,512]{3,2,1,0:T(8,128)(2,1)} custom-call(s32[4]{0:T(128)} %pad_add_fusion.numbers, bf16[8,4,64,512]{3,2,1,0:T(8,128)(2,1)} %bitcast.53, f32[8,64,128]{2,1,0:T(8,128)} %chosen_rows.1.codes, s32[512,1]{1,0:T(8,128)} %add.164.origin, f32[1,2048]{1,0:T(1,128)} %bitcast.74, bf16[64,2048]{1,0:T(8,128)(2,1)} %bitcast.73, ...), custom_call_target="tpu_custom_call" | custom-call | flops 8000000000 | bytes 20000000 | tf_op jit(solution)/shard_map/expert/pallas_call | solution.py:367
  155.1 33.0 %all_to_all.10.answers = bf16[32,64,512]{2,1,0:T(8,128)(2,1)} all-to-all(bf16[32,64,512]{2,1,0:T(8,128)(2,1)} %bitcast.54), channel_id=1, replica_groups=mesh['z'=8,'y'=4,'c'=2,'tp'=4] {'y','c','tp'}, dimensions={0} | all-to-all | bytes 4194304 | tf_op jit(solution)/shard_map/all_to_all | solution.py:526
  188.1 4.4 %combine.1 = bf16[8,132,512]{2,1,0:T(8,128)(2,1)} custom-call(bf16[8,132,512]{2,1,0:T(8,128)(2,1)} %pair_hits.2.hits, bf16[32,64,512]{2,1,0:T(8,128)(2,1)} %all_to_all.10.answers), custom_call_target="tpu_custom_call" | custom-call | flops 600000000 | bytes 4000000 | tf_op jit(solution)/shard_map/combine/pallas_call | solution.py:238
  192.5 1.3 reshape.69
  193.9 25.2 %fusion = bf16[136,512]{1,0:T(8,128)(2,1)S(1)} fusion(bf16[1056,512]{1,0:T(8,128)(2,1)S(1)} %reshape.69), kind=kCustom, calls=%all-reduce-scatter | all-reduce-scatter fusion | flops 557057 | bytes 1221632
  219.1 2.8 %collective-permute-start.24 = (bf16[28,512]{1,0:T(8,128)(2,1)S(1)}, bf16[28,512]{1,0:T(8,128)(2,1)S(1)}, u32[]{:S(2)}, u32[]{:S(2)}) collective-permute-start(bf16[28,512]{1,0:T(8,128)(2,1)S(1)} %slice.68), channel_id=1, source_target_pairs={{0,32},{32,64},{64,96},{96,128},{128,160},{160,192},{192,224},{1,3... | collective-permute-start | bytes 86024
  221.9 0.6 dynamic-slice.8
  223.1 1.7 collective-permute-done.24
  225.1 0.7 constant_dynamic-slice_fusion
  (72 shorter events, 1.7 us)
Async XLA Ops:
  6.5 57.8 %all-gather.5.cloned.1.call-start = ((), (), s32[]{:S(2)}) async-start(), calls=%async_computation.2 | async-start | bytes 1253376 | tf_op jit(solution)/shard_map/all_gather | solution.py:458
  7.8 6.3 %collective-permute-start.2 = (f32[2,132]{0,1:T(8,128)S(1)}, f32[2,132]{0,1:T(8,128)S(1)}, u32[]{:S(2)}, u32[]{:S(2)}) collective-permute-start(f32[2,132]{0,1:T(8,128)S(1)} %copy.28), channel_id=1, source_target_pairs={{0,3},{1,0},{2,1},{3,2},{4,7},{5,4},{6,5},{7,6},{8,11},{9,8},{10,9... | collective-permute-start | bytes 3176 | tf_op jit(solution)/shard_map/ppermute | solution.py:425
  10.6 5.9 %collective-permute-start.1 = (f32[2,132]{0,1:T(8,128)S(1)}, f32[2,132]{0,1:T(8,128)S(1)}, u32[]{:S(2)}, u32[]{:S(2)}) collective-permute-start(f32[2,132]{0,1:T(8,128)S(1)} %copy.28), channel_id=1, source_target_pairs={{0,2},{1,3},{2,0},{3,1},{4,6},{5,7},{6,4},{7,5},{8,10},{9,11},{10,... | collective-permute-start | bytes 3176 | tf_op jit(solution)/shard_map/ppermute | solution.py:425
  11.4 5.8 %collective-permute-start = (f32[2,132]{0,1:T(8,128)S(1)}, f32[2,132]{0,1:T(8,128)S(1)}, u32[]{:S(2)}, u32[]{:S(2)}) collective-permute-start(f32[2,132]{0,1:T(8,128)S(1)} %copy.28), channel_id=1, source_target_pairs={{0,1},{1,2},{2,3},{3,0},{4,5},{5,6},{6,7},{7,4},{8,9},{9,10},{10,1... | collective-permute-start | bytes 3176 | tf_op jit(solution)/shard_map/ppermute | solution.py:425
  12.3 9.0 %copy-start.12 = (s32[132,8]{0,1:T(8,128)S(1)}, s32[132,8]{0,1:T(8,128)}, u32[]{:S(2)}) copy-start(s32[132,8]{0,1:T(8,128)} %param.26) | copy-start | bytes 12676
  12.3 10.2 %copy-start.14 = (bf16[1,256,2048]{2,1,0:T(8,128)(2,1)S(1)}, bf16[1,256,2048]{2,1,0:T(8,128)(2,1)}, u32[]{:S(2)}) copy-start(bf16[1,256,2048]{2,1,0:T(8,128)(2,1)} %param.32) | copy-start | bytes 3145732
  12.3 13.1 %copy-start.11 = (s32[4]{0:T(128)S(1)}, s32[4]{0:T(128)}, u32[]{:S(2)}) copy-start(s32[4]{0:T(128)} %param.24) | copy-start | bytes 52
  14.1 28.4 %copy-start = (bf16[4096,256]{1,0:T(8,128)(2,1)}, bf16[4096,256]{1,0:T(8,128)(2,1)S(1)}, u32[]{:S(2)}) copy-start(bf16[4096,256]{1,0:T(8,128)(2,1)S(1)} %pad_maximum_fusion.refs_0_) | copy-start | bytes 6291460
  17.3 26.2 %collective-permute-start.3 = (bf16[4096,256]{1,0:T(8,128)(2,1)S(1)}, bf16[4096,256]{1,0:T(8,128)(2,1)}, u32[]{:S(2)}, u32[]{:S(2)}) collective-permute-start(bf16[4096,256]{1,0:T(8,128)(2,1)S(1)} %pad_maximum_fusion.refs_0_), channel_id=1, source_target_pairs={{0,1},{1,0},{2,5},{3,4},{6,7},{7,6},{5,2},{4,3},{8,9},{9,8},{10,13... | collective-permute-start | bytes 6291464 | tf_op jit(solution)/shard_map/ppermute | solution.py:470
  17.4 26.1 %collective-permute-start.4 = (bf16[4096,256]{1,0:T(8,128)(2,1)S(1)}, bf16[4096,256]{1,0:T(8,128)(2,1)}, u32[]{:S(2)}, u32[]{:S(2)}) collective-permute-start(bf16[4096,256]{1,0:T(8,128)(2,1)S(1)} %pad_maximum_fusion.refs_0_), channel_id=1, source_target_pairs={{0,4},{1,5},{6,2},{7,3},{8,12},{9,13},{14,10},{15,11},{16,20},{17,... | collective-permute-start | bytes 6291464 | tf_op jit(solution)/shard_map/ppermute | solution.py:471
  22.4 88.6 %all-gather.7.cloned.1.call-start = ((), (), s32[]{:S(2)}) async-start(), calls=%async_computation.3 | async-start | bytes 2506752 | tf_op jit(solution)/shard_map/all_gather | solution.py:518
  22.5 20.0 %collective-permute-start.5 = (bf16[256,2048]{1,0:T(8,128)(2,1)S(1)}, bf16[256,2048]{1,0:T(8,128)(2,1)}, u32[]{:S(2)}, u32[]{:S(2)}) collective-permute-start(bf16[256,2048]{1,0:T(8,128)(2,1)S(1)} %bitcast.71), channel_id=1, source_target_pairs={{0,4},{1,5},{6,2},{7,3},{8,12},{9,13},{14,10},{15,11},{16,20},{17,... | collective-permute-start | bytes 3145736 | tf_op jit(solution)/shard_map/ppermute | solution.py:472
  30.8 42.6 %copy-start.17 = (s32[8]{0:T(128)S(1)}, s32[8]{0:T(128)}, u32[]{:S(2)}) copy-start(s32[8]{0:T(128)} %constant.153.clone) | copy-start | bytes 100
  43.5 6.6 %collective-permute-start.8 = (bf16[132,512]{1,0:T(8,128)(2,1)}, bf16[132,512]{1,0:T(8,128)(2,1)S(1)}, u32[]{:S(2)}, u32[]{:S(2)}) collective-permute-start(bf16[132,512]{1,0:T(8,128)(2,1)} %get-tuple-element.36), channel_id=1, source_target_pairs={{0,3},{1,0},{2,1},{3,2},{4,7},{5,4},{6,5},{7,6},{8,11},{9,8},{10,9... | collective-permute-start | bytes 405512 | tf_op jit(solution)/shard_map/ppermute | solution.py:425
  44.7 7.7 %collective-permute-start.7 = (bf16[132,512]{1,0:T(8,128)(2,1)}, bf16[132,512]{1,0:T(8,128)(2,1)S(1)}, u32[]{:S(2)}, u32[]{:S(2)}) collective-permute-start(bf16[132,512]{1,0:T(8,128)(2,1)} %get-tuple-element.35), channel_id=1, source_target_pairs={{0,2},{1,3},{2,0},{3,1},{4,6},{5,7},{6,4},{7,5},{8,10},{9,11},{10,... | collective-permute-start | bytes 405512 | tf_op jit(solution)/shard_map/ppermute | solution.py:425
  45.6 8.3 %collective-permute-start.6 = (bf16[132,512]{1,0:T(8,128)(2,1)}, bf16[132,512]{1,0:T(8,128)(2,1)S(1)}, u32[]{:S(2)}, u32[]{:S(2)}) collective-permute-start(bf16[132,512]{1,0:T(8,128)(2,1)} %get-tuple-element.34), channel_id=1, source_target_pairs={{0,1},{1,2},{2,3},{3,0},{4,5},{5,6},{6,7},{7,4},{8,9},{9,10},{10,1... | collective-permute-start | bytes 405512 | tf_op jit(solution)/shard_map/ppermute | solution.py:425
  55.0 32.2 %copy-start.2 = (bf16[132,512]{1,0:T(8,128)(2,1)}, bf16[132,512]{1,0:T(8,128)(2,1)S(1)}, u32[]{:S(2)}) copy-start(bf16[132,512]{1,0:T(8,128)(2,1)S(1)} %add_convert_fusion.refs_0_) | copy-start | bytes 405508
  55.0 5.7 %collective-permute-start.9 = (bf16[132,512]{1,0:T(8,128)(2,1)S(1)}, bf16[132,512]{1,0:T(8,128)(2,1)S(1)}, u32[]{:S(2)}, u32[]{:S(2)}) collective-permute-start(bf16[132,512]{1,0:T(8,128)(2,1)S(1)} %add_convert_fusion.refs_0_), channel_id=1, source_target_pairs={{0,32},{32,64},{64,96},{96,128},{128,160},{160,192},{192,224},{224... | collective-permute-start | bytes 405512 | tf_op jit(solution)/shard_map/ppermute | solution.py:425
  57.0 5.3 %collective-permute-start.11 = (bf16[132,512]{1,0:T(8,128)(2,1)S(1)}, bf16[132,512]{1,0:T(8,128)(2,1)S(1)}, u32[]{:S(2)}, u32[]{:S(2)}) collective-permute-start(bf16[132,512]{1,0:T(8,128)(2,1)S(1)} %add_convert_fusion.refs_0_), channel_id=1, source_target_pairs={{0,224},{32,0},{64,32},{96,64},{128,96},{160,128},{192,160},{224,1... | collective-permute-start | bytes 405512 | tf_op jit(solution)/shard_map/ppermute | solution.py:425
  57.1 37.2 %collective-permute-start.17 = (bf16[4096,256]{1,0:T(8,128)(2,1)}, bf16[4096,256]{1,0:T(8,128)(2,1)}, u32[]{:S(2)}, u32[]{:S(2)}) collective-permute-start(bf16[4096,256]{1,0:T(8,128)(2,1)} %collective-permute-done.3.refs_1_), channel_id=1, source_target_pairs={{4,5},{5,4},{2,3},{3,2},{12,13},{13,12},{10,11},{11,10},{20,21},{2... | collective-permute-start | bytes 6291464 | tf_op jit(solution)/shard_map/ppermute | solution.py:512
  60.7 26.5 %copy-start.5 = (bf16[132,512]{1,0:T(8,128)(2,1)}, bf16[132,512]{1,0:T(8,128)(2,1)S(1)}, u32[]{:S(2)}) copy-start(bf16[132,512]{1,0:T(8,128)(2,1)S(1)} %collective-permute-done.9.refs_1_) | copy-start | bytes 405508
  60.7 6.6 %collective-permute-start.10 = (bf16[132,512]{1,0:T(8,128)(2,1)S(1)}, bf16[132,512]{1,0:T(8,128)(2,1)S(1)}, u32[]{:S(2)}, u32[]{:S(2)}) collective-permute-start(bf16[132,512]{1,0:T(8,128)(2,1)S(1)} %collective-permute-done.9.refs_1_), channel_id=1, source_target_pairs={{0,32},{32,64},{64,96},{96,128},{128,160},{160,192},{192,224},{224... | collective-permute-start | bytes 405512 | tf_op jit(solution)/shard_map/ppermute | solution.py:425
  62.2 24.9 %copy-start.6 = (bf16[132,512]{1,0:T(8,128)(2,1)}, bf16[132,512]{1,0:T(8,128)(2,1)S(1)}, u32[]{:S(2)}) copy-start(bf16[132,512]{1,0:T(8,128)(2,1)S(1)} %collective-permute-done.11.refs_2_) | copy-start | bytes 405508
  62.2 5.8 %collective-permute-start.12 = (bf16[132,512]{1,0:T(8,128)(2,1)S(1)}, bf16[132,512]{1,0:T(8,128)(2,1)S(1)}, u32[]{:S(2)}, u32[]{:S(2)}) collective-permute-start(bf16[132,512]{1,0:T(8,128)(2,1)S(1)} %collective-permute-done.11.refs_2_), channel_id=1, source_target_pairs={{0,224},{32,0},{64,32},{96,64},{128,96},{160,128},{192,160},{224,1... | collective-permute-start | bytes 405512 | tf_op jit(solution)/shard_map/ppermute | solution.py:425
  67.3 19.9 %copy-start.7 = (bf16[132,512]{1,0:T(8,128)(2,1)}, bf16[132,512]{1,0:T(8,128)(2,1)S(1)}, u32[]{:S(2)}) copy-start(bf16[132,512]{1,0:T(8,128)(2,1)S(1)} %collective-permute-done.10.refs_3_) | copy-start | bytes 405508
  68.1 19.1 %copy-start.8 = (bf16[132,512]{1,0:T(8,128)(2,1)}, bf16[132,512]{1,0:T(8,128)(2,1)S(1)}, u32[]{:S(2)}) copy-start(bf16[132,512]{1,0:T(8,128)(2,1)S(1)} %collective-permute-done.12.refs_4_) | copy-start | bytes 405508
  69.8 24.5 %collective-permute-start.18 = (bf16[256,2048]{1,0:T(8,128)(2,1)S(1)}, bf16[256,2048]{1,0:T(8,128)(2,1)}, u32[]{:S(2)}, u32[]{:S(2)}) collective-permute-start(bf16[256,2048]{1,0:T(8,128)(2,1)S(1)} %bitcast.72), channel_id=1, source_target_pairs={{0,1},{1,0},{2,5},{3,4},{6,7},{7,6},{5,2},{4,3},{8,9},{9,8},{10,13... | collective-permute-start | bytes 3145736 | tf_op jit(solution)/shard_map/ppermute | solution.py:511
  70.2 11.4 %collective-permute-start.13 = (bf16[132,512]{1,0:T(8,128)(2,1)S(1)}, bf16[132,512]{1,0:T(8,128)(2,1)S(1)}, u32[]{:S(2)}, u32[]{:S(2)}) collective-permute-start(bf16[132,512]{1,0:T(8,128)(2,1)S(1)} %collective-permute-done.10.refs_3_), channel_id=1, source_target_pairs={{0,32},{32,64},{64,96},{96,128},{128,160},{160,192},{192,224},{224... | collective-permute-start | bytes 405512 | tf_op jit(solution)/shard_map/ppermute | solution.py:425
  73.4 7.4 %collective-permute-start.14 = (bf16[132,512]{1,0:T(8,128)(2,1)S(1)}, bf16[132,512]{1,0:T(8,128)(2,1)S(1)}, u32[]{:S(2)}, u32[]{:S(2)}) collective-permute-start(bf16[132,512]{1,0:T(8,128)(2,1)S(1)} %collective-permute-done.12.refs_4_), channel_id=1, source_target_pairs={{0,224},{32,0},{64,32},{96,64},{128,96},{160,128},{192,160},{224,1... | collective-permute-start | bytes 405512 | tf_op jit(solution)/shard_map/ppermute | solution.py:425
  80.8 6.4 %copy-start.3 = (bf16[132,512]{1,0:T(8,128)(2,1)}, bf16[132,512]{1,0:T(8,128)(2,1)S(1)}, u32[]{:S(2)}) copy-start(bf16[132,512]{1,0:T(8,128)(2,1)S(1)} %collective-permute-done.14.refs_6_) | copy-start | bytes 405508
  80.8 6.3 %collective-permute-start.16 = (bf16[68,512]{1,0:T(8,128)(2,1)S(1)}, bf16[68,512]{1,0:T(8,128)(2,1)S(1)}, u32[]{:S(2)}, u32[]{:S(2)}) collective-permute-start(bf16[68,512]{1,0:T(8,128)(2,1)S(1)} %slice.67), channel_id=1, source_target_pairs={{0,224},{32,0},{64,32},{96,64},{128,96},{160,128},{192,160},{224,1... | collective-permute-start | bytes 208904 | tf_op jit(solution)/shard_map/ppermute | solution.py:425
  81.6 38.9 %collective-permute-start.19 = (bf16[4096,256]{1,0:T(8,128)(2,1)}, bf16[4096,256]{1,0:T(8,128)(2,1)}, u32[]{:S(2)}, u32[]{:S(2)}) collective-permute-start(bf16[4096,256]{1,0:T(8,128)(2,1)} %collective-permute-done.3.refs_1_), channel_id=1, source_target_pairs={{0,4},{1,5},{2,6},{3,7},{4,0},{5,1},{6,2},{7,3},{8,12},{9,13},{10,... | collective-permute-start | bytes 6291464 | tf_op jit(solution)/shard_map/ppermute | solution.py:558
  81.6 5.6 %copy-start.4 = (bf16[132,512]{1,0:T(8,128)(2,1)}, bf16[132,512]{1,0:T(8,128)(2,1)S(1)}, u32[]{:S(2)}) copy-start(bf16[132,512]{1,0:T(8,128)(2,1)S(1)} %collective-permute-done.13.refs_5_) | copy-start | bytes 405508
  81.6 5.5 %collective-permute-start.15 = (bf16[64,512]{1,0:T(8,128)(2,1)S(1)}, bf16[64,512]{1,0:T(8,128)(2,1)S(1)}, u32[]{:S(2)}, u32[]{:S(2)}) collective-permute-start(bf16[64,512]{1,0:T(8,128)(2,1)S(1)} %slice.66), channel_id=1, source_target_pairs={{0,32},{32,64},{64,96},{96,128},{128,160},{160,192},{192,224},{224... | collective-permute-start | bytes 196616 | tf_op jit(solution)/shard_map/ppermute | solution.py:425
  87.1 0.6 copy-start.10
  87.7 0.6 copy-start.9
  92.7 16.4 %copy-start.16 = (s32[64]{0:T(128)S(1)}, s32[64]{0:T(128)}, u32[]{:S(2)}) copy-start(s32[64]{0:T(128)} %param.25) | copy-start | bytes 772
  94.3 45.2 %collective-permute-start.20 = (bf16[4096,256]{1,0:T(8,128)(2,1)}, bf16[4096,256]{1,0:T(8,128)(2,1)}, u32[]{:S(2)}, u32[]{:S(2)}) collective-permute-start(bf16[4096,256]{1,0:T(8,128)(2,1)} %collective-permute-done.17.refs_3_), channel_id=1, source_target_pairs={{4,0},{5,1},{2,6},{3,7},{12,8},{13,9},{10,14},{11,15},{20,16},{21,... | collective-permute-start | bytes 6291464 | tf_op jit(solution)/shard_map/ppermute | solution.py:559
  95.6 12.1 %collective-permute-start.21 = (bf16[256,2048]{1,0:T(8,128)(2,1)}, bf16[256,2048]{1,0:T(8,128)(2,1)S(1)}, u32[]{:S(2)}, u32[]{:S(2)}) collective-permute-start(bf16[256,2048]{1,0:T(8,128)(2,1)} %collective-permute-done.18.refs_7_), channel_id=1, source_target_pairs={{4,5},{5,4},{2,3},{3,2},{12,13},{13,12},{10,11},{11,10},{20,21},{2... | collective-permute-start | bytes 3145736 | tf_op jit(solution)/shard_map/ppermute | solution.py:532
  96.3 43.1 %all-to-all-start = ((bf16[32,64,512]{2,1,0:T(8,128)(2,1)}), bf16[32,64,512]{2,1,0:T(8,128)(2,1)S(1)}, u32[]{:S(2)}, u32[]{:S(2)}) async-start(bf16[32,64,512]{2,1,0:T(8,128)(2,1)} %expand.1), calls=%async_computation | async-start | bytes 4194304 | tf_op jit(solution)/shard_map/all_to_all | solution.py:526
  107.4 13.0 %collective-permute-start.22 = (bf16[256,2048]{1,0:T(8,128)(2,1)}, bf16[256,2048]{1,0:T(8,128)(2,1)}, u32[]{:S(2)}, u32[]{:S(2)}) collective-permute-start(bf16[256,2048]{1,0:T(8,128)(2,1)} %collective-permute-done.18.refs_7_), channel_id=1, source_target_pairs={{0,4},{1,5},{2,6},{3,7},{4,0},{5,1},{6,2},{7,3},{8,12},{9,13},{10,... | collective-permute-start | bytes 3145736 | tf_op jit(solution)/shard_map/ppermute | solution.py:558
  107.7 12.7 %copy-start.15 = (bf16[256,2048]{1,0:T(8,128)(2,1)}, bf16[256,2048]{1,0:T(8,128)(2,1)S(1)}, u32[]{:S(2)}) copy-start(bf16[256,2048]{1,0:T(8,128)(2,1)S(1)} %collective-permute-done.21.refs_9_) | copy-start | bytes 3145732
  107.8 31.7 %collective-permute-start.23 = (bf16[256,2048]{1,0:T(8,128)(2,1)S(1)}, bf16[256,2048]{1,0:T(8,128)(2,1)}, u32[]{:S(2)}, u32[]{:S(2)}) collective-permute-start(bf16[256,2048]{1,0:T(8,128)(2,1)S(1)} %collective-permute-done.21.refs_9_), channel_id=1, source_target_pairs={{4,0},{5,1},{2,6},{3,7},{12,8},{13,9},{10,14},{11,15},{20,16},{21,... | collective-permute-start | bytes 3145736 | tf_op jit(solution)/shard_map/ppermute | solution.py:559
  139.5 1.3 copy-start.1
  192.5 29.4 %copy-start.13 = (u32[256]{0:T(256)S(1)}, u32[256]{0:T(256)}, u32[]{:S(2)}) copy-start(u32[256]{0:T(256)} %constant.168) | copy-start | bytes 3076
  219.1 5.8 %collective-permute-start.24 = (bf16[28,512]{1,0:T(8,128)(2,1)S(1)}, bf16[28,512]{1,0:T(8,128)(2,1)S(1)}, u32[]{:S(2)}, u32[]{:S(2)}) collective-permute-start(bf16[28,512]{1,0:T(8,128)(2,1)S(1)} %slice.68), channel_id=1, source_target_pairs={{0,32},{32,64},{64,96},{96,128},{128,160},{160,192},{192,224},{1,3... | collective-permute-start | bytes 86024
Sparse Core Ops, SparseCore 0:
  22.5 39.1 all-gather.4
  69.9 28.7 all-gather.6

commit v5 on v4

--- a/solution.py
+++ b/solution.py
@@ -468,8 +468,6 @@
     squares = squares + shared[0] + shared[1] + shared[2]
     squares, wide = tied(squares, wide)
     wide_first = lax.ppermute(wide, PAIR, first_move)
-    wide_other = lax.ppermute(wide, PAIR, out_of_home)
-    down_other = lax.ppermute(down, PAIR, out_of_home)
     inv = lax.rsqrt(squares / FULL + 1e-05).T
     spot = jnp.arange(ROWS, dtype=jnp.int32)
     positions = offsets[0] + spot
@@ -494,9 +492,7 @@
         decode_cache,
         out_weight,
     )
-    *sends, wide_first, wide_other, down_other = tied(
-        *sends, wide_first, wide_other, down_other
-    )
+    *sends, wide_first = tied(*sends, wide_first)
     state = own
     for step in range(1, TP):
         state = state + around(sends[step - 1], "tp", step).astype(F32)
@@ -513,7 +509,7 @@
 
     up_1, down_1 = around(state, "z", 1), around(state, "z", -1)
     up_2, down_2 = around(up_1, "z", 1), around(down_1, "z", -1)
-    up_2, down_2, code_column = tied(up_2, down_2, code_column)
+    up_2, down_2, code_column, down_first = tied(up_2, down_2, code_column, down_first)
     code_column = code_column[:, :, :LANES]
     code_all = lax.all_gather(code_column, ("y", "c"), axis=0).reshape(
         EXPERTS, PADDED, LANES
@@ -526,10 +522,11 @@
         return lax.all_to_all(blocks, plane, split_axis=0, concat_axis=0, tiled=True)
 
     up_3, down_3 = around(up_2, "z", 1), around(down_2, "z", -1)
+    up_3, down_3, down_first = tied(up_3, down_3, down_first)
+    down_second = lax.ppermute(down_first, PAIR, second_move)
     far = [around(up_3[:64], "z", 1), around(down_3[64:], "z", -1)]
     outgoing = expand(out_hits, [state, up_1, down_1, up_2, down_2, up_3, down_3, *far])
-    outgoing, wide_second, down_first = tied(outgoing, wide_second, down_first)
-    down_second = lax.ppermute(down_first, PAIR, second_move)
+    outgoing, wide_second = tied(outgoing, wide_second)
     arrived = exchanged(outgoing)
     codes = chosen_rows(numbers, code_all)
 
@@ -553,14 +550,14 @@
         [
             own,
             first,
-            other_own,
+            lax.ppermute(own, PAIR, out_of_home),
             second,
             lax.ppermute(first, PAIR, both),
             lax.ppermute(second, PAIR, to_home),
         ]
-        for own, first, other_own, second in (
-            (wide, wide_first, wide_other, wide_second),
-            (down, down_first, down_other, down_second),
+        for own, first, second in (
+            (wide, wide_first, wide_second),
+            (down, down_first, down_second),
         )
     )
     result = expert(

time: 233 us -> 231 us (level)
  waiting for transfers between devices: 47.9 us -> 53.1 us
  starting transfers between devices: 44 us -> 39.9 us
    all_to_all x1, waiting for transfers between devices: 19 us -> 11.4 us  [exchanged(): lax.all_to_all(blocks, plane, split_axis=0, concat_axis=0, tiled=True)]
    ppermute x1, waiting for transfers between devices: 1.04 us -> 7.08 us  [per_device(): wide_first = lax.ppermute(wide, PAIR, first_move)]
    ppermute x1, waiting for transfers between devices: 1.65 us -> 6.95 us  [per_device(): down_first = lax.ppermute(down, PAIR, first_move)]
    all_to_all x1, starting transfers between devices: 11 us -> 7.26 us  [exchanged(): lax.all_to_all(blocks, plane, split_axis=0, concat_axis=0, tiled=True)]
  transfers between devices with their start and end apart: 28 -> 28, of which waited for: 14 -> 15; matrix products, arithmetic and copies ran while one was open for 6% -> 6% of each run, Pallas kernels for 12% -> 12%
where the time goes in v5:
time: 231 us; the launch traced here: 230 us
  blocking collectives  56.3 us (24%)
  waiting for transfers between devices  53.1 us (23%)
  Pallas kernels  46.6 us (20%)
  starting transfers between devices  39.9 us (17%)
  between operations  15.1 us (7%)
  other arithmetic  10.7 us (5%)
  local copies, waits for them, and re-layouts  7.93 us (3%)
    all_to_all x1, blocking collectives, exchanged(): lax.all_to_all(blocks, plane, split_axis=0, concat_axis=0, tiled=True)  33.3 us
    ppermute x14, waiting for transfers between devices, around(): lax.ppermute(value, axis, [(i, (i + step) % count) for i in range(count)])  25.9 us
    unnamed x1, blocking collectives  23 us
    ppermute x14, starting transfers between devices, around(): lax.ppermute(value, axis, [(i, (i + step) % count) for i in range(count)])  17 us
    pallas_call x1, Pallas kernels, expert(): pl.pallas_call(expert_kernel, in_specs=[SM] + [VM] * 5 + [HB] * 12, out_s...  14.2 us
    pallas_call x1, Pallas kernels, attention(): pl.pallas_call(attention_kernel, grid=(HEADS_HERE,), in_specs=[SM, pl.Blo...  11.6 us
    all_to_all x1, waiting for transfers between devices, exchanged(): lax.all_to_all(blocks, plane, split_axis=0, concat_axis=0, tiled=True)  11.4 us
    all_to_all x1, starting transfers between devices, exchanged(): lax.all_to_all(blocks, plane, split_axis=0, concat_axis=0, tiled=True)  7.26 us
  transfers between devices with their start and end apart: 28, of which 15 were waited for; matrix products, arithmetic and copies ran while one was open for 6% of the time, Pallas kernels for 12%

profile of v5, /device:TPU:32, one launch (start us, length us, event | category | flops | bytes accessed | tf_op | source)
XLA Modules:
  0.0 229.9 jit_solution(602572410395478680)
XLA Ops:
  6.5 1.1 multiply_reduce_fusion
  7.8 2.8 %collective-permute-start.2 = (f32[2,132]{0,1:T(8,128)S(1)}, f32[2,132]{0,1:T(8,128)S(1)}, u32[]{:S(2)}, u32[]{:S(2)}) collective-permute-start(f32[2,132]{0,1:T(8,128)S(1)} %copy.28), channel_id=1, source_target_pairs={{0,3},{1,0},{2,1},{3,2},{4,7},{5,4},{6,5},{7,6},{8,11},{9,8},{10,9... | collective-permute-start | bytes 3176 | tf_op jit(solution)/shard_map/ppermute | solution.py:425
  10.6 0.8 collective-permute-start.1
  11.4 0.9 collective-permute-start
  12.3 1.7 pad_maximum_fusion.refs_0_
  14.0 2.5 %collective-permute-done.1 = f32[2,132]{0,1:T(8,128)S(1)} collective-permute-done((f32[2,132]{0,1:T(8,128)S(1)}, f32[2,132]{0,1:T(8,128)S(1)}, u32[]{:S(2)}, u32[]{:S(2)}) %collective-permute-start.1) | collective-permute-done | bytes 1088 | tf_op jit(solution)/shard_map/ppermute | solution.py:425
  16.5 0.7 collective-permute-done
  17.4 0.4 fusion.2
  17.8 0.7 pad.4
  19.2 0.7 fusion.34
  19.9 2.6 %fusion.29 = f32[132]{0:T(256)S(1)} fusion(s32[]{:T(128)} %bitcast.52, s32[]{:T(128)} %bitcast.12, s32[]{:T(128)} %bitcast.11, s32[]{:T(128)} %bitcast.10, s32[]{:T(128)} %bitcast.9), kind=kLoop, calls=%fused_computation.73 | loop fusion | flops 1320 | bytes 548 | tf_op jit(solution)/shard_map/convert_element_type | solution.py:478
  22.5 0.3 fusion.19
  22.8 0.8 pad_maximum_fusion.1
  23.6 0.6 pad_add_fusion.1.numbers
  24.2 0.6 rsqrt_bitcast_fusion.inv
  24.8 11.6 %attention.1 = (f32[132,512]{1,0:T(8,128)}, bf16[132,512]{1,0:T(8,128)(2,1)}, bf16[132,512]{1,0:T(8,128)(2,1)}, bf16[132,512]{1,0:T(8,128)(2,1)}) custom-call(s32[6]{0:T(128)} %pad_add_fusion.1.numbers, bf16[3,132,512]{2,1,0:T(8,128)(2,1)} %bitcast.55, f32[132,2]{1,0:T(8,128)} %rsqrt_bitcast_fusion.inv, f32[132,128]{1,0:T(8,128)} %get-tuple-element.68.cosine, ...), custom_call_target="tpu_custom_call" | custom-call | flops 2000000000 | bytes 10000000 | tf_op jit(solution)/shard_map/attention/pallas_call | solution.py:132
  36.4 7.1 %collective-permute-done.3.refs_1_ = bf16[4096,256]{1,0:T(8,128)(2,1)} collective-permute-done((bf16[4096,256]{1,0:T(8,128)(2,1)S(1)}, bf16[4096,256]{1,0:T(8,128)(2,1)}, u32[]{:S(2)}, u32[]{:S(2)}) %collective-permute-start.3) | collective-permute-done | bytes 2097184 | tf_op jit(solution)/shard_map/ppermute | solution.py:470
  43.5 1.2 collective-permute-start.6
  44.7 0.9 collective-permute-start.5
  45.6 4.5 %collective-permute-done.6 = bf16[132,512]{1,0:T(8,128)(2,1)S(1)} collective-permute-done((bf16[132,512]{1,0:T(8,128)(2,1)}, bf16[132,512]{1,0:T(8,128)(2,1)S(1)}, u32[]{:S(2)}, u32[]{:S(2)}) %collective-permute-start.6) | collective-permute-done | bytes 135200 | tf_op jit(solution)/shard_map/ppermute | solution.py:425
  50.0 2.1 collective-permute-done.5
  52.2 1.0 collective-permute-done.4
  53.2 1.1 add_convert_fusion.refs_0_
  54.5 1.9 collective-permute-start.7
  56.6 2.0 collective-permute-start.16
  58.6 2.5 %collective-permute-done.7.refs_1_ = bf16[132,512]{1,0:T(8,128)(2,1)S(1)} collective-permute-done((bf16[132,512]{1,0:T(8,128)(2,1)S(1)}, bf16[132,512]{1,0:T(8,128)(2,1)S(1)}, u32[]{:S(2)}, u32[]{:S(2)}) %collective-permute-start.7) | collective-permute-done | bytes 135200 | tf_op jit(solution)/shard_map/ppermute | solution.py:425
  61.1 1.9 collective-permute-start.8
  63.0 1.8 collective-permute-start.10
  64.8 3.9 %collective-permute-done.8.refs_3_ = bf16[132,512]{1,0:T(8,128)(2,1)S(1)} collective-permute-done((bf16[132,512]{1,0:T(8,128)(2,1)S(1)}, bf16[132,512]{1,0:T(8,128)(2,1)S(1)}, u32[]{:S(2)}, u32[]{:S(2)}) %collective-permute-start.8) | collective-permute-done | bytes 135200 | tf_op jit(solution)/shard_map/ppermute | solution.py:425
  68.7 1.4 collective-permute-done.10.refs_4_
  70.1 6.9 %collective-permute-done.11.refs_7_ = bf16[256,2048]{1,0:T(8,128)(2,1)} collective-permute-done((bf16[256,2048]{1,0:T(8,128)(2,1)}, bf16[256,2048]{1,0:T(8,128)(2,1)}, u32[]{:S(2)}, u32[]{:S(2)}) %collective-permute-start.11) | collective-permute-done | bytes 1048608 | tf_op jit(solution)/shard_map/ppermute | solution.py:507
  77.0 1.7 slice.62.code
  78.8 2.6 %collective-permute-start.17 = (bf16[4096,256]{1,0:T(8,128)(2,1)S(1)}, bf16[4096,256]{1,0:T(8,128)(2,1)}, u32[]{:S(2)}, u32[]{:S(2)}) collective-permute-start(bf16[4096,256]{1,0:T(8,128)(2,1)S(1)} %pad_maximum_fusion.refs_0_), channel_id=1, source_target_pairs={{0,4},{1,5},{6,2},{7,3},{8,12},{9,13},{14,10},{15,11},{16,20},{17,... | collective-permute-start | bytes 6291464 | tf_op jit(solution)/shard_map/ppermute | solution.py:553
  81.4 1.6 collective-permute-start.12
  83.0 0.4 collective-permute-start.13
  83.4 0.6 and_select_fusion.order
  84.0 2.5 %collective-permute-done.12.refs_5_ = bf16[132,512]{1,0:T(8,128)(2,1)S(1)} collective-permute-done((bf16[132,512]{1,0:T(8,128)(2,1)S(1)}, bf16[132,512]{1,0:T(8,128)(2,1)S(1)}, u32[]{:S(2)}, u32[]{:S(2)}) %collective-permute-start.12) | collective-permute-done | bytes 135200 | tf_op jit(solution)/shard_map/ppermute | solution.py:425
  86.4 1.6 collective-permute-done.13.refs_6_
  88.1 2.6 %collective-permute-start.15 = (bf16[68,512]{1,0:T(8,128)(2,1)S(1)}, bf16[68,512]{1,0:T(8,128)(2,1)S(1)}, u32[]{:S(2)}, u32[]{:S(2)}) collective-permute-start(bf16[68,512]{1,0:T(8,128)(2,1)S(1)} %slice.64), channel_id=1, source_target_pairs={{0,224},{32,0},{64,32},{96,64},{128,96},{160,128},{192,160},{224,1... | collective-permute-start | bytes 208904 | tf_op jit(solution)/shard_map/ppermute | solution.py:425
  90.6 0.6 pad_add_fusion.numbers
  91.3 2.7 %pair_hits.3.hits = bf16[8,132,512]{2,1,0:T(8,128)(2,1)} custom-call(s32[4]{0:T(128)} %pad_add_fusion.numbers, s32[8]{0:T(128)} %and_select_fusion.order, bf16[8,136,128]{2,1,0:T(8,128)(2,1)} %slice.62.code), custom_call_target="tpu_custom_call" | custom-call | flops 700000000 | bytes 4000000 | tf_op jit(solution)/shard_map/pair_hits/pallas_call | solution.py:187
  94.0 3.2 %collective-permute-done.14.refs_7_ = bf16[64,512]{1,0:T(8,128)(2,1)S(1)} collective-permute-done((bf16[64,512]{1,0:T(8,128)(2,1)S(1)}, bf16[64,512]{1,0:T(8,128)(2,1)S(1)}, u32[]{:S(2)}, u32[]{:S(2)}) %collective-permute-start.14) | collective-permute-done | bytes 65568 | tf_op jit(solution)/shard_map/ppermute | solution.py:425
  97.2 1.6 collective-permute-start.21
  98.9 0.6 copy-done.8
  99.6 4.3 %expand.1 = bf16[32,64,512]{2,1,0:T(8,128)(2,1)} custom-call(bf16[8,132,512]{2,1,0:T(8,128)(2,1)} %pair_hits.3.hits, bf16[132,512]{1,0:T(8,128)(2,1)} %copy-done.1, bf16[132,512]{1,0:T(8,128)(2,1)} %copy-done.4, bf16[132,512]{1,0:T(8,128)(2,1)} %copy-done.5, bf16[132,512]{1,0:T(8,128)(2,1)} %copy-done.6, bf16[132,512]{1,0:T(8,128)(2,1)} %copy-done.7, ...), custom_call_target="tpu_custom_call" | custom-call | flops 700000000 | bytes 4000000 | tf_op jit(solution)/shard_map/expand/pallas_call | solution.py:218
  103.9 1.4 collective-permute-start.19
  105.3 7.3 %all-to-all-start = ((bf16[32,64,512]{2,1,0:T(8,128)(2,1)}), bf16[32,64,512]{2,1,0:T(8,128)(2,1)}, u32[]{:S(2)}, u32[]{:S(2)}) async-start(bf16[32,64,512]{2,1,0:T(8,128)(2,1)} %expand.1), calls=%async_computation | async-start | bytes 4194304 | tf_op jit(solution)/shard_map/all_to_all | solution.py:522
  112.6 3.1 %collective-permute-start.20 = (bf16[256,2048]{1,0:T(8,128)(2,1)S(1)}, bf16[256,2048]{1,0:T(8,128)(2,1)}, u32[]{:S(2)}, u32[]{:S(2)}) collective-permute-start(bf16[256,2048]{1,0:T(8,128)(2,1)S(1)} %bitcast.71), channel_id=1, source_target_pairs={{0,4},{1,5},{6,2},{7,3},{8,12},{9,13},{14,10},{15,11},{16,20},{17,... | collective-permute-start | bytes 3145736 | tf_op jit(solution)/shard_map/ppermute | solution.py:553
  115.7 1.5 collective-permute-start.23
  117.8 0.9 add.164.origin
  118.7 0.5 fusion.31.order
  119.2 6.1 %chosen_rows.1.codes = f32[8,64,128]{2,1,0:T(8,128)} custom-call(s32[4]{0:T(128)} %pad_add_fusion.numbers, bf16[64,136,128]{2,1,0:T(8,128)(2,1)} %all-gather.7.cloned.1.call-done.code), custom_call_target="tpu_custom_call" | custom-call | flops 200000000 | bytes 2000000 | tf_op jit(solution)/shard_map/chosen_rows/pallas_call | solution.py:279
  125.3 3.3 %pair_hits.2.hits = bf16[8,132,512]{2,1,0:T(8,128)(2,1)} custom-call(s32[4]{0:T(128)} %pad_add_fusion.numbers, s32[8]{0:T(128)} %fusion.31.order, bf16[64,136,128]{2,1,0:T(8,128)(2,1)} %all-gather.7.cloned.1.call-done.code), custom_call_target="tpu_custom_call" | custom-call | flops 700000000 | bytes 4000000 | tf_op jit(solution)/shard_map/pair_hits/pallas_call | solution.py:187
  128.6 11.4 %all-to-all-done = bf16[32,64,512]{2,1,0:T(8,128)(2,1)} async-done(((bf16[32,64,512]{2,1,0:T(8,128)(2,1)}), bf16[32,64,512]{2,1,0:T(8,128)(2,1)}, u32[]{:S(2)}, u32[]{:S(2)}) %all-to-all-start) | async-done | bytes 2097184 | tf_op jit(solution)/shard_map/all_to_all | solution.py:522
  140.0 14.2 %expert.1 = bf16[8,4,64,512]{3,2,1,0:T(8,128)(2,1)} custom-call(s32[4]{0:T(128)} %pad_add_fusion.numbers, bf16[8,4,64,512]{3,2,1,0:T(8,128)(2,1)} %bitcast.26.arrived, f32[8,64,128]{2,1,0:T(8,128)} %chosen_rows.1.codes, s32[512,1]{1,0:T(8,128)} %add.164.origin, f32[1,2048]{1,0:T(1,128)} %bitcast.73, bf16[64,2048]{1,0:T(8,128)(2,1)} %bitcast.72, ...), custom_call_target="tpu_custom_call" | custom-call | flops 8000000000 | bytes 20000000 | tf_op jit(solution)/shard_map/expert/pallas_call | solution.py:367
  154.3 33.3 %all_to_all.10.answers = bf16[32,64,512]{2,1,0:T(8,128)(2,1)} all-to-all(bf16[32,64,512]{2,1,0:T(8,128)(2,1)} %bitcast.53), channel_id=1, replica_groups=mesh['z'=8,'y'=4,'c'=2,'tp'=4] {'y','c','tp'}, dimensions={0} | all-to-all | bytes 4194304 | tf_op jit(solution)/shard_map/all_to_all | solution.py:522
  187.6 4.4 %combine.1 = bf16[8,132,512]{2,1,0:T(8,128)(2,1)} custom-call(bf16[8,132,512]{2,1,0:T(8,128)(2,1)} %pair_hits.2.hits, bf16[32,64,512]{2,1,0:T(8,128)(2,1)} %all_to_all.10.answers), custom_call_target="tpu_custom_call" | custom-call | flops 600000000 | bytes 4000000 | tf_op jit(solution)/shard_map/combine/pallas_call | solution.py:238
  192.0 1.3 reshape.69
  193.3 23.0 %fusion = bf16[136,512]{1,0:T(8,128)(2,1)S(1)} fusion(bf16[1056,512]{1,0:T(8,128)(2,1)S(1)} %reshape.69), kind=kCustom, calls=%all-reduce-scatter | all-reduce-scatter fusion | flops 557057 | bytes 1221632
  216.4 2.9 %collective-permute-start.24 = (bf16[28,512]{1,0:T(8,128)(2,1)S(1)}, bf16[28,512]{1,0:T(8,128)(2,1)S(1)}, u32[]{:S(2)}, u32[]{:S(2)}) collective-permute-start(bf16[28,512]{1,0:T(8,128)(2,1)S(1)} %slice.66), channel_id=1, source_target_pairs={{0,32},{32,64},{64,96},{96,128},{128,160},{160,192},{192,224},{1,3... | collective-permute-start | bytes 86024
  219.2 0.6 dynamic-slice.8
  220.5 1.7 collective-permute-done.24
  222.2 0.2 concatenate.16
  222.4 0.7 constant_dynamic-slice_fusion
  (70 shorter events, 1.4 us)
Async XLA Ops:
  6.5 58.3 %all-gather.5.cloned.1.call-start = ((), (), s32[]{:S(2)}) async-start(), calls=%async_computation.2 | async-start | bytes 1253376 | tf_op jit(solution)/shard_map/all_gather | solution.py:458
  7.8 6.2 %collective-permute-start.2 = (f32[2,132]{0,1:T(8,128)S(1)}, f32[2,132]{0,1:T(8,128)S(1)}, u32[]{:S(2)}, u32[]{:S(2)}) collective-permute-start(f32[2,132]{0,1:T(8,128)S(1)} %copy.28), channel_id=1, source_target_pairs={{0,3},{1,0},{2,1},{3,2},{4,7},{5,4},{6,5},{7,6},{8,11},{9,8},{10,9... | collective-permute-start | bytes 3176 | tf_op jit(solution)/shard_map/ppermute | solution.py:425
  10.6 5.9 %collective-permute-start.1 = (f32[2,132]{0,1:T(8,128)S(1)}, f32[2,132]{0,1:T(8,128)S(1)}, u32[]{:S(2)}, u32[]{:S(2)}) collective-permute-start(f32[2,132]{0,1:T(8,128)S(1)} %copy.28), channel_id=1, source_target_pairs={{0,2},{1,3},{2,0},{3,1},{4,6},{5,7},{6,4},{7,5},{8,10},{9,11},{10,... | collective-permute-start | bytes 3176 | tf_op jit(solution)/shard_map/ppermute | solution.py:425
  11.4 5.8 %collective-permute-start = (f32[2,132]{0,1:T(8,128)S(1)}, f32[2,132]{0,1:T(8,128)S(1)}, u32[]{:S(2)}, u32[]{:S(2)}) collective-permute-start(f32[2,132]{0,1:T(8,128)S(1)} %copy.28), channel_id=1, source_target_pairs={{0,1},{1,2},{2,3},{3,0},{4,5},{5,6},{6,7},{7,4},{8,9},{9,10},{10,1... | collective-permute-start | bytes 3176 | tf_op jit(solution)/shard_map/ppermute | solution.py:425
  12.3 5.1 %copy-start.11 = (s32[132,8]{0,1:T(8,128)S(1)}, s32[132,8]{0,1:T(8,128)}, u32[]{:S(2)}) copy-start(s32[132,8]{0,1:T(8,128)} %param.26) | copy-start | bytes 12676
  12.3 6.9 %copy-start.10 = (s32[4]{0:T(128)S(1)}, s32[4]{0:T(128)}, u32[]{:S(2)}) copy-start(s32[4]{0:T(128)} %param.24) | copy-start | bytes 52
  14.0 64.8 %copy-start = (bf16[4096,256]{1,0:T(8,128)(2,1)}, bf16[4096,256]{1,0:T(8,128)(2,1)S(1)}, u32[]{:S(2)}) copy-start(bf16[4096,256]{1,0:T(8,128)(2,1)S(1)} %pad_maximum_fusion.refs_0_) | copy-start | bytes 6291460
  17.3 26.2 %collective-permute-start.3 = (bf16[4096,256]{1,0:T(8,128)(2,1)S(1)}, bf16[4096,256]{1,0:T(8,128)(2,1)}, u32[]{:S(2)}, u32[]{:S(2)}) collective-permute-start(bf16[4096,256]{1,0:T(8,128)(2,1)S(1)} %pad_maximum_fusion.refs_0_), channel_id=1, source_target_pairs={{0,1},{1,0},{2,5},{3,4},{6,7},{7,6},{5,2},{4,3},{8,9},{9,8},{10,13... | collective-permute-start | bytes 6291464 | tf_op jit(solution)/shard_map/ppermute | solution.py:470
  18.5 100.7 %all-gather.7.cloned.1.call-start = ((), (), s32[]{:S(2)}) async-start(), calls=%async_computation.3 | async-start | bytes 2506752 | tf_op jit(solution)/shard_map/all_gather | solution.py:514
  24.8 58.6 %copy-start.16 = (s32[8]{0:T(128)S(1)}, s32[8]{0:T(128)}, u32[]{:S(2)}) copy-start(s32[8]{0:T(128)} %constant.153.clone) | copy-start | bytes 100
  43.5 6.6 %collective-permute-start.6 = (bf16[132,512]{1,0:T(8,128)(2,1)}, bf16[132,512]{1,0:T(8,128)(2,1)S(1)}, u32[]{:S(2)}, u32[]{:S(2)}) collective-permute-start(bf16[132,512]{1,0:T(8,128)(2,1)} %get-tuple-element.37), channel_id=1, source_target_pairs={{0,3},{1,0},{2,1},{3,2},{4,7},{5,4},{6,5},{7,6},{8,11},{9,8},{10,9... | collective-permute-start | bytes 405512 | tf_op jit(solution)/shard_map/ppermute | solution.py:425
  44.7 7.5 %collective-permute-start.5 = (bf16[132,512]{1,0:T(8,128)(2,1)}, bf16[132,512]{1,0:T(8,128)(2,1)S(1)}, u32[]{:S(2)}, u32[]{:S(2)}) collective-permute-start(bf16[132,512]{1,0:T(8,128)(2,1)} %get-tuple-element.36), channel_id=1, source_target_pairs={{0,2},{1,3},{2,0},{3,1},{4,6},{5,7},{6,4},{7,5},{8,10},{9,11},{10,... | collective-permute-start | bytes 405512 | tf_op jit(solution)/shard_map/ppermute | solution.py:425
  45.6 7.7 %collective-permute-start.4 = (bf16[132,512]{1,0:T(8,128)(2,1)}, bf16[132,512]{1,0:T(8,128)(2,1)S(1)}, u32[]{:S(2)}, u32[]{:S(2)}) collective-permute-start(bf16[132,512]{1,0:T(8,128)(2,1)} %get-tuple-element.35), channel_id=1, source_target_pairs={{0,1},{1,2},{2,3},{3,0},{4,5},{5,6},{6,7},{7,4},{8,9},{9,10},{10,1... | collective-permute-start | bytes 405512 | tf_op jit(solution)/shard_map/ppermute | solution.py:425
  54.3 44.6 %copy-start.1 = (bf16[132,512]{1,0:T(8,128)(2,1)}, bf16[132,512]{1,0:T(8,128)(2,1)S(1)}, u32[]{:S(2)}) copy-start(bf16[132,512]{1,0:T(8,128)(2,1)S(1)} %add_convert_fusion.refs_0_) | copy-start | bytes 405508
  54.3 22.7 %collective-permute-start.11 = (bf16[256,2048]{1,0:T(8,128)(2,1)}, bf16[256,2048]{1,0:T(8,128)(2,1)}, u32[]{:S(2)}, u32[]{:S(2)}) collective-permute-start(bf16[256,2048]{1,0:T(8,128)(2,1)} %bitcast.69), channel_id=1, source_target_pairs={{0,1},{1,0},{2,5},{3,4},{6,7},{7,6},{5,2},{4,3},{8,9},{9,8},{10,13... | collective-permute-start | bytes 3145736 | tf_op jit(solution)/shard_map/ppermute | solution.py:507
  54.5 6.5 %collective-permute-start.7 = (bf16[132,512]{1,0:T(8,128)(2,1)S(1)}, bf16[132,512]{1,0:T(8,128)(2,1)S(1)}, u32[]{:S(2)}, u32[]{:S(2)}) collective-permute-start(bf16[132,512]{1,0:T(8,128)(2,1)S(1)} %add_convert_fusion.refs_0_), channel_id=1, source_target_pairs={{0,32},{32,64},{64,96},{96,128},{128,160},{160,192},{192,224},{224... | collective-permute-start | bytes 405512 | tf_op jit(solution)/shard_map/ppermute | solution.py:425
  56.5 6.5 %collective-permute-start.9 = (bf16[132,512]{1,0:T(8,128)(2,1)S(1)}, bf16[132,512]{1,0:T(8,128)(2,1)S(1)}, u32[]{:S(2)}, u32[]{:S(2)}) collective-permute-start(bf16[132,512]{1,0:T(8,128)(2,1)S(1)} %add_convert_fusion.refs_0_), channel_id=1, source_target_pairs={{0,224},{32,0},{64,32},{96,64},{128,96},{160,128},{192,160},{224,1... | collective-permute-start | bytes 405512 | tf_op jit(solution)/shard_map/ppermute | solution.py:425
  56.6 47.3 %collective-permute-start.16 = (bf16[4096,256]{1,0:T(8,128)(2,1)}, bf16[4096,256]{1,0:T(8,128)(2,1)}, u32[]{:S(2)}, u32[]{:S(2)}) collective-permute-start(bf16[4096,256]{1,0:T(8,128)(2,1)} %collective-permute-done.3.refs_1_), channel_id=1, source_target_pairs={{4,5},{5,4},{2,3},{3,2},{12,13},{13,12},{10,11},{11,10},{20,21},{2... | collective-permute-start | bytes 6291464 | tf_op jit(solution)/shard_map/ppermute | solution.py:508
  61.1 37.8 %copy-start.4 = (bf16[132,512]{1,0:T(8,128)(2,1)}, bf16[132,512]{1,0:T(8,128)(2,1)S(1)}, u32[]{:S(2)}) copy-start(bf16[132,512]{1,0:T(8,128)(2,1)S(1)} %collective-permute-done.7.refs_1_) | copy-start | bytes 405508
  61.1 7.6 %collective-permute-start.8 = (bf16[132,512]{1,0:T(8,128)(2,1)S(1)}, bf16[132,512]{1,0:T(8,128)(2,1)S(1)}, u32[]{:S(2)}, u32[]{:S(2)}) collective-permute-start(bf16[132,512]{1,0:T(8,128)(2,1)S(1)} %collective-permute-done.7.refs_1_), channel_id=1, source_target_pairs={{0,32},{32,64},{64,96},{96,128},{128,160},{160,192},{192,224},{224... | collective-permute-start | bytes 405512 | tf_op jit(solution)/shard_map/ppermute | solution.py:425
  63.0 35.9 %copy-start.5 = (bf16[132,512]{1,0:T(8,128)(2,1)}, bf16[132,512]{1,0:T(8,128)(2,1)S(1)}, u32[]{:S(2)}) copy-start(bf16[132,512]{1,0:T(8,128)(2,1)S(1)} %collective-permute-done.9.refs_2_) | copy-start | bytes 405508
  63.0 7.1 %collective-permute-start.10 = (bf16[132,512]{1,0:T(8,128)(2,1)S(1)}, bf16[132,512]{1,0:T(8,128)(2,1)S(1)}, u32[]{:S(2)}, u32[]{:S(2)}) collective-permute-start(bf16[132,512]{1,0:T(8,128)(2,1)S(1)} %collective-permute-done.9.refs_2_), channel_id=1, source_target_pairs={{0,224},{32,0},{64,32},{96,64},{128,96},{160,128},{192,160},{224,1... | collective-permute-start | bytes 405512 | tf_op jit(solution)/shard_map/ppermute | solution.py:425
  68.7 30.2 %copy-start.6 = (bf16[132,512]{1,0:T(8,128)(2,1)}, bf16[132,512]{1,0:T(8,128)(2,1)S(1)}, u32[]{:S(2)}) copy-start(bf16[132,512]{1,0:T(8,128)(2,1)S(1)} %collective-permute-done.8.refs_3_) | copy-start | bytes 405508
  70.1 28.8 %copy-start.7 = (bf16[132,512]{1,0:T(8,128)(2,1)}, bf16[132,512]{1,0:T(8,128)(2,1)S(1)}, u32[]{:S(2)}) copy-start(bf16[132,512]{1,0:T(8,128)(2,1)S(1)} %collective-permute-done.10.refs_4_) | copy-start | bytes 405508
  78.8 36.9 %collective-permute-start.17 = (bf16[4096,256]{1,0:T(8,128)(2,1)S(1)}, bf16[4096,256]{1,0:T(8,128)(2,1)}, u32[]{:S(2)}, u32[]{:S(2)}) collective-permute-start(bf16[4096,256]{1,0:T(8,128)(2,1)S(1)} %pad_maximum_fusion.refs_0_), channel_id=1, source_target_pairs={{0,4},{1,5},{6,2},{7,3},{8,12},{9,13},{14,10},{15,11},{16,20},{17,... | collective-permute-start | bytes 6291464 | tf_op jit(solution)/shard_map/ppermute | solution.py:553
  81.4 5.1 %collective-permute-start.12 = (bf16[132,512]{1,0:T(8,128)(2,1)S(1)}, bf16[132,512]{1,0:T(8,128)(2,1)S(1)}, u32[]{:S(2)}, u32[]{:S(2)}) collective-permute-start(bf16[132,512]{1,0:T(8,128)(2,1)S(1)} %collective-permute-done.8.refs_3_), channel_id=1, source_target_pairs={{0,32},{32,64},{64,96},{96,128},{128,160},{160,192},{192,224},{224... | collective-permute-start | bytes 405512 | tf_op jit(solution)/shard_map/ppermute | solution.py:425
  83.0 5.1 %collective-permute-start.13 = (bf16[132,512]{1,0:T(8,128)(2,1)S(1)}, bf16[132,512]{1,0:T(8,128)(2,1)S(1)}, u32[]{:S(2)}, u32[]{:S(2)}) collective-permute-start(bf16[132,512]{1,0:T(8,128)(2,1)S(1)} %collective-permute-done.10.refs_4_), channel_id=1, source_target_pairs={{0,224},{32,0},{64,32},{96,64},{128,96},{160,128},{192,160},{224,1... | collective-permute-start | bytes 405512 | tf_op jit(solution)/shard_map/ppermute | solution.py:425
  86.4 12.5 %copy-start.3 = (bf16[132,512]{1,0:T(8,128)(2,1)}, bf16[132,512]{1,0:T(8,128)(2,1)S(1)}, u32[]{:S(2)}) copy-start(bf16[132,512]{1,0:T(8,128)(2,1)S(1)} %collective-permute-done.12.refs_5_) | copy-start | bytes 405508
  88.0 10.9 %copy-start.2 = (bf16[132,512]{1,0:T(8,128)(2,1)}, bf16[132,512]{1,0:T(8,128)(2,1)S(1)}, u32[]{:S(2)}) copy-start(bf16[132,512]{1,0:T(8,128)(2,1)S(1)} %collective-permute-done.13.refs_6_) | copy-start | bytes 405508
  88.1 10.8 %collective-permute-start.15 = (bf16[68,512]{1,0:T(8,128)(2,1)S(1)}, bf16[68,512]{1,0:T(8,128)(2,1)S(1)}, u32[]{:S(2)}, u32[]{:S(2)}) collective-permute-start(bf16[68,512]{1,0:T(8,128)(2,1)S(1)} %slice.64), channel_id=1, source_target_pairs={{0,224},{32,0},{64,32},{96,64},{128,96},{160,128},{192,160},{224,1... | collective-permute-start | bytes 208904 | tf_op jit(solution)/shard_map/ppermute | solution.py:425
  91.2 37.4 %collective-permute-start.18 = (bf16[4096,256]{1,0:T(8,128)(2,1)}, bf16[4096,256]{1,0:T(8,128)(2,1)}, u32[]{:S(2)}, u32[]{:S(2)}) collective-permute-start(bf16[4096,256]{1,0:T(8,128)(2,1)} %collective-permute-done.3.refs_1_), channel_id=1, source_target_pairs={{0,4},{1,5},{2,6},{3,7},{4,0},{5,1},{6,2},{7,3},{8,12},{9,13},{10,... | collective-permute-start | bytes 6291464 | tf_op jit(solution)/shard_map/ppermute | solution.py:555
  91.2 6.0 %collective-permute-start.14 = (bf16[64,512]{1,0:T(8,128)(2,1)S(1)}, bf16[64,512]{1,0:T(8,128)(2,1)S(1)}, u32[]{:S(2)}, u32[]{:S(2)}) collective-permute-start(bf16[64,512]{1,0:T(8,128)(2,1)S(1)} %slice.63), channel_id=1, source_target_pairs={{0,32},{32,64},{64,96},{96,128},{128,160},{160,192},{192,224},{224... | collective-permute-start | bytes 196616 | tf_op jit(solution)/shard_map/ppermute | solution.py:425
  97.2 1.7 copy-start.9
  97.2 18.5 %collective-permute-start.21 = (bf16[256,2048]{1,0:T(8,128)(2,1)}, bf16[256,2048]{1,0:T(8,128)(2,1)}, u32[]{:S(2)}, u32[]{:S(2)}) collective-permute-start(bf16[256,2048]{1,0:T(8,128)(2,1)} %collective-permute-done.11.refs_7_), channel_id=1, source_target_pairs={{4,5},{5,4},{2,3},{3,2},{12,13},{13,12},{10,11},{11,10},{20,21},{2... | collective-permute-start | bytes 3145736 | tf_op jit(solution)/shard_map/ppermute | solution.py:526
  98.9 0.6 copy-start.8
  103.8 8.7 %copy-start.13 = (bf16[1,256,2048]{2,1,0:T(8,128)(2,1)S(1)}, bf16[1,256,2048]{2,1,0:T(8,128)(2,1)}, u32[]{:S(2)}) copy-start(bf16[1,256,2048]{2,1,0:T(8,128)(2,1)} %param.32) | copy-start | bytes 3145732
  103.9 13.4 %copy-start.15 = (s32[64]{0:T(128)S(1)}, s32[64]{0:T(128)}, u32[]{:S(2)}) copy-start(s32[64]{0:T(128)} %param.25) | copy-start | bytes 772
  103.9 36.1 %collective-permute-start.19 = (bf16[4096,256]{1,0:T(8,128)(2,1)}, bf16[4096,256]{1,0:T(8,128)(2,1)}, u32[]{:S(2)}, u32[]{:S(2)}) collective-permute-start(bf16[4096,256]{1,0:T(8,128)(2,1)} %collective-permute-done.16.refs_3_), channel_id=1, source_target_pairs={{4,0},{5,1},{2,6},{3,7},{12,8},{13,9},{10,14},{11,15},{20,16},{21,... | collective-permute-start | bytes 6291464 | tf_op jit(solution)/shard_map/ppermute | solution.py:556
  105.3 34.7 %all-to-all-start = ((bf16[32,64,512]{2,1,0:T(8,128)(2,1)}), bf16[32,64,512]{2,1,0:T(8,128)(2,1)}, u32[]{:S(2)}, u32[]{:S(2)}) async-start(bf16[32,64,512]{2,1,0:T(8,128)(2,1)} %expand.1), calls=%async_computation | async-start | bytes 4194304 | tf_op jit(solution)/shard_map/all_to_all | solution.py:522
  112.6 16.0 %collective-permute-start.20 = (bf16[256,2048]{1,0:T(8,128)(2,1)S(1)}, bf16[256,2048]{1,0:T(8,128)(2,1)}, u32[]{:S(2)}, u32[]{:S(2)}) collective-permute-start(bf16[256,2048]{1,0:T(8,128)(2,1)S(1)} %bitcast.71), channel_id=1, source_target_pairs={{0,4},{1,5},{6,2},{7,3},{8,12},{9,13},{14,10},{15,11},{16,20},{17,... | collective-permute-start | bytes 3145736 | tf_op jit(solution)/shard_map/ppermute | solution.py:553
  115.7 12.9 %collective-permute-start.22 = (bf16[256,2048]{1,0:T(8,128)(2,1)}, bf16[256,2048]{1,0:T(8,128)(2,1)S(1)}, u32[]{:S(2)}, u32[]{:S(2)}) collective-permute-start(bf16[256,2048]{1,0:T(8,128)(2,1)} %collective-permute-done.11.refs_7_), channel_id=1, source_target_pairs={{0,4},{1,5},{2,6},{3,7},{4,0},{5,1},{6,2},{7,3},{8,12},{9,13},{10,... | collective-permute-start | bytes 3145736 | tf_op jit(solution)/shard_map/ppermute | solution.py:555
  115.7 12.9 %collective-permute-start.23 = (bf16[256,2048]{1,0:T(8,128)(2,1)}, bf16[256,2048]{1,0:T(8,128)(2,1)}, u32[]{:S(2)}, u32[]{:S(2)}) collective-permute-start(bf16[256,2048]{1,0:T(8,128)(2,1)} %collective-permute-done.21.refs_9_), channel_id=1, source_target_pairs={{4,0},{5,1},{2,6},{3,7},{12,8},{13,9},{10,14},{11,15},{20,16},{21,... | collective-permute-start | bytes 3145736 | tf_op jit(solution)/shard_map/ppermute | solution.py:556
  128.6 11.4 %copy-start.14 = (bf16[256,2048]{1,0:T(8,128)(2,1)}, bf16[256,2048]{1,0:T(8,128)(2,1)S(1)}, u32[]{:S(2)}) copy-start(bf16[256,2048]{1,0:T(8,128)(2,1)S(1)} %collective-permute-done.22.refs_10_) | copy-start | bytes 3145732
  192.0 27.3 %copy-start.12 = (u32[256]{0:T(256)S(1)}, u32[256]{0:T(256)}, u32[]{:S(2)}) copy-start(u32[256]{0:T(256)} %constant.168) | copy-start | bytes 3076
  216.4 5.8 %collective-permute-start.24 = (bf16[28,512]{1,0:T(8,128)(2,1)S(1)}, bf16[28,512]{1,0:T(8,128)(2,1)S(1)}, u32[]{:S(2)}, u32[]{:S(2)}) collective-permute-start(bf16[28,512]{1,0:T(8,128)(2,1)S(1)} %slice.66), channel_id=1, source_target_pairs={{0,32},{32,64},{64,96},{96,128},{128,160},{160,192},{192,224},{1,3... | collective-permute-start | bytes 86024
Sparse Core Ops, SparseCore 0:
  18.6 39.8 all-gather.4
  78.9 27.8 all-gather.6

commit v6 on v5

--- a/solution.py
+++ b/solution.py
@@ -509,7 +509,7 @@
 
     up_1, down_1 = around(state, "z", 1), around(state, "z", -1)
     up_2, down_2 = around(up_1, "z", 1), around(down_1, "z", -1)
-    up_2, down_2, code_column, down_first = tied(up_2, down_2, code_column, down_first)
+    up_2, down_2, code_column = tied(up_2, down_2, code_column)
     code_column = code_column[:, :, :LANES]
     code_all = lax.all_gather(code_column, ("y", "c"), axis=0).reshape(
         EXPERTS, PADDED, LANES
@@ -522,11 +522,10 @@
         return lax.all_to_all(blocks, plane, split_axis=0, concat_axis=0, tiled=True)
 
     up_3, down_3 = around(up_2, "z", 1), around(down_2, "z", -1)
-    up_3, down_3, down_first = tied(up_3, down_3, down_first)
-    down_second = lax.ppermute(down_first, PAIR, second_move)
     far = [around(up_3[:64], "z", 1), around(down_3[64:], "z", -1)]
     outgoing = expand(out_hits, [state, up_1, down_1, up_2, down_2, up_3, down_3, *far])
-    outgoing, wide_second = tied(outgoing, wide_second)
+    outgoing, wide_second, down_first = tied(outgoing, wide_second, down_first)
+    down_second = lax.ppermute(down_first, PAIR, second_move)
     arrived = exchanged(outgoing)
     codes = chosen_rows(numbers, code_all)
 

time: 231 us -> 232 us (level)
  waiting for transfers between devices: 53.1 us -> 48 us
  starting transfers between devices: 39.9 us -> 44.3 us
    ppermute x1, waiting for transfers between devices: 6.95 us -> 0.01 us  [per_device(): down_first = lax.ppermute(down, PAIR, first_move)]
    all_to_all x1, waiting for transfers between devices: 11.4 us -> 16.3 us  [exchanged(): lax.all_to_all(blocks, plane, split_axis=0, concat_axis=0, tiled=True)]
    ppermute x14, waiting for transfers between devices: 25.9 us -> 21.7 us  [around(): lax.ppermute(value, axis, [(i, (i + step) % count) for i in range(count)])]
    all_to_all x1, starting transfers between devices: 7.26 us -> 9.96 us  [exchanged(): lax.all_to_all(blocks, plane, split_axis=0, concat_axis=0, tiled=True)]
  transfers between devices with their start and end apart: 28 -> 28, of which waited for: 15 -> 12; matrix products, arithmetic and copies ran while one was open for 6% -> 6% of each run, Pallas kernels for 12% -> 12%
where the time goes in v6:
time: 232 us
  blocking collectives  58.2 us (25%)
  waiting for transfers between devices  48 us (21%)
  Pallas kernels  46.6 us (20%)
  starting transfers between devices  44.3 us (19%)
  between operations  15.1 us (7%)
  other arithmetic  10.5 us (5%)
  local copies, waits for them, and re-layouts  8.5 us (4%)
    all_to_all x1, blocking collectives, exchanged(): lax.all_to_all(blocks, plane, split_axis=0, concat_axis=0, tiled=True)  33 us
    unnamed x1, blocking collectives  25.2 us
    ppermute x14, waiting for transfers between devices, around(): lax.ppermute(value, axis, [(i, (i + step) % count) for i in range(count)])  21.7 us
    ppermute x14, starting transfers between devices, around(): lax.ppermute(value, axis, [(i, (i + step) % count) for i in range(count)])  18 us
    all_to_all x1, waiting for transfers between devices, exchanged(): lax.all_to_all(blocks, plane, split_axis=0, concat_axis=0, tiled=True)  16.3 us
    pallas_call x1, Pallas kernels, expert(): pl.pallas_call(expert_kernel, in_specs=[SM] + [VM] * 5 + [HB] * 12, out_s...  14.3 us
    pallas_call x1, Pallas kernels, attention(): pl.pallas_call(attention_kernel, grid=(HEADS_HERE,), in_specs=[SM, pl.Blo...  11.6 us
    all_to_all x1, starting transfers between devices, exchanged(): lax.all_to_all(blocks, plane, split_axis=0, concat_axis=0, tiled=True)  9.96 us
  transfers between devices with their start and end apart: 28, of which 12 were waited for; matrix products, arithmetic and copies ran while one was open for 6% of the time, Pallas kernels for 12%

profile of v6, /device:TPU:32, one launch (start us, length us, event | category | flops | bytes accessed | tf_op | source)
XLA Modules:
  0.0 231.5 jit_solution(7152881565947373541)
XLA Ops:
  6.5 1.1 multiply_reduce_fusion
  7.8 2.8 %collective-permute-start.2 = (f32[2,132]{0,1:T(8,128)S(1)}, f32[2,132]{0,1:T(8,128)S(1)}, u32[]{:S(2)}, u32[]{:S(2)}) collective-permute-start(f32[2,132]{0,1:T(8,128)S(1)} %copy.28), channel_id=1, source_target_pairs={{0,3},{1,0},{2,1},{3,2},{4,7},{5,4},{6,5},{7,6},{8,11},{9,8},{10,9... | collective-permute-start | bytes 3176 | tf_op jit(solution)/shard_map/ppermute | solution.py:425
  10.6 0.8 collective-permute-start.1
  11.4 0.9 collective-permute-start
  12.3 1.7 pad_maximum_fusion.refs_0_
  14.0 2.5 %collective-permute-done.1 = f32[2,132]{0,1:T(8,128)S(1)} collective-permute-done((f32[2,132]{0,1:T(8,128)S(1)}, f32[2,132]{0,1:T(8,128)S(1)}, u32[]{:S(2)}, u32[]{:S(2)}) %collective-permute-start.1) | collective-permute-done | bytes 1088 | tf_op jit(solution)/shard_map/ppermute | solution.py:425
  16.5 0.7 collective-permute-done
  17.4 0.4 fusion.2
  17.8 0.7 pad.4
  19.2 0.6 pad_add_fusion.1.numbers
  19.8 0.7 fusion.34
  20.4 2.4 %fusion.29 = f32[132]{0:T(256)S(1)} fusion(s32[]{:T(128)} %bitcast.52, s32[]{:T(128)} %bitcast.12, s32[]{:T(128)} %bitcast.11, s32[]{:T(128)} %bitcast.10, s32[]{:T(128)} %bitcast.9), kind=kLoop, calls=%fused_computation.73 | loop fusion | flops 1320 | bytes 548 | tf_op jit(solution)/shard_map/convert_element_type | solution.py:478
  22.8 0.3 fusion.19
  23.2 0.8 pad_maximum_fusion.1
  23.9 0.6 rsqrt_bitcast_fusion.inv
  24.6 11.6 %attention.1 = (f32[132,512]{1,0:T(8,128)}, bf16[132,512]{1,0:T(8,128)(2,1)}, bf16[132,512]{1,0:T(8,128)(2,1)}, bf16[132,512]{1,0:T(8,128)(2,1)}) custom-call(s32[6]{0:T(128)} %pad_add_fusion.1.numbers, bf16[3,132,512]{2,1,0:T(8,128)(2,1)} %bitcast.55, f32[132,2]{1,0:T(8,128)} %rsqrt_bitcast_fusion.inv, f32[132,128]{1,0:T(8,128)} %get-tuple-element.62.cosine, ...), custom_call_target="tpu_custom_call" | custom-call | flops 2000000000 | bytes 10000000 | tf_op jit(solution)/shard_map/attention/pallas_call | solution.py:132
  36.2 7.3 %collective-permute-done.3.refs_1_ = bf16[4096,256]{1,0:T(8,128)(2,1)} collective-permute-done((bf16[4096,256]{1,0:T(8,128)(2,1)S(1)}, bf16[4096,256]{1,0:T(8,128)(2,1)}, u32[]{:S(2)}, u32[]{:S(2)}) %collective-permute-start.3) | collective-permute-done | bytes 2097184 | tf_op jit(solution)/shard_map/ppermute | solution.py:470
  43.5 1.2 collective-permute-start.6
  44.7 0.9 collective-permute-start.5
  45.6 4.5 %collective-permute-done.6 = bf16[132,512]{1,0:T(8,128)(2,1)S(1)} collective-permute-done((bf16[132,512]{1,0:T(8,128)(2,1)}, bf16[132,512]{1,0:T(8,128)(2,1)S(1)}, u32[]{:S(2)}, u32[]{:S(2)}) %collective-permute-start.6) | collective-permute-done | bytes 135200 | tf_op jit(solution)/shard_map/ppermute | solution.py:425
  50.0 2.1 collective-permute-done.5
  52.2 1.0 collective-permute-done.4
  53.2 1.1 add_convert_fusion.refs_0_
  54.3 2.0 collective-permute-start.7
  56.3 0.1 collective-permute-start.9
  56.4 2.0 collective-permute-start.15
  58.5 1.1 collective-permute-done.7.refs_1_
  59.6 2.5 %collective-permute-start.8 = (bf16[132,512]{1,0:T(8,128)(2,1)S(1)}, bf16[132,512]{1,0:T(8,128)(2,1)S(1)}, u32[]{:S(2)}, u32[]{:S(2)}) collective-permute-start(bf16[132,512]{1,0:T(8,128)(2,1)S(1)} %collective-permute-done.7.refs_1_), channel_id=1, source_target_pairs={{0,32},{32,64},{64,96},{96,128},{128,160},{160,192},{192,224},{224... | collective-permute-start | bytes 405512 | tf_op jit(solution)/shard_map/ppermute | solution.py:425
  62.1 1.4 collective-permute-start.10
  63.5 2.9 %collective-permute-done.8.refs_3_ = bf16[132,512]{1,0:T(8,128)(2,1)S(1)} collective-permute-done((bf16[132,512]{1,0:T(8,128)(2,1)S(1)}, bf16[132,512]{1,0:T(8,128)(2,1)S(1)}, u32[]{:S(2)}, u32[]{:S(2)}) %collective-permute-start.8) | collective-permute-done | bytes 135200 | tf_op jit(solution)/shard_map/ppermute | solution.py:425
  66.4 1.0 collective-permute-done.10.refs_4_
  67.4 1.8 slice.62.code
  69.2 0.2 collective-permute-start.16
  69.4 4.3 %collective-permute-start.17 = (bf16[4096,256]{1,0:T(8,128)(2,1)S(1)}, bf16[4096,256]{1,0:T(8,128)(2,1)}, u32[]{:S(2)}, u32[]{:S(2)}) collective-permute-start(bf16[4096,256]{1,0:T(8,128)(2,1)S(1)} %pad_maximum_fusion.refs_0_), channel_id=1, source_target_pairs={{0,4},{1,5},{6,2},{7,3},{8,12},{9,13},{14,10},{15,11},{16,20},{17,... | collective-permute-start | bytes 6291464 | tf_op jit(solution)/shard_map/ppermute | solution.py:552
  73.7 3.2 %collective-permute-start.11 = (bf16[132,512]{1,0:T(8,128)(2,1)S(1)}, bf16[132,512]{1,0:T(8,128)(2,1)S(1)}, u32[]{:S(2)}, u32[]{:S(2)}) collective-permute-start(bf16[132,512]{1,0:T(8,128)(2,1)S(1)} %collective-permute-done.8.refs_3_), channel_id=1, source_target_pairs={{0,32},{32,64},{64,96},{96,128},{128,160},{160,192},{192,224},{224... | collective-permute-start | bytes 405512 | tf_op jit(solution)/shard_map/ppermute | solution.py:425
  77.0 0.6 and_select_fusion.order
  77.5 5.7 %collective-permute-done.12.refs_6_ = bf16[132,512]{1,0:T(8,128)(2,1)S(1)} collective-permute-done((bf16[132,512]{1,0:T(8,128)(2,1)S(1)}, bf16[132,512]{1,0:T(8,128)(2,1)S(1)}, u32[]{:S(2)}, u32[]{:S(2)}) %collective-permute-start.12) | collective-permute-done | bytes 135200 | tf_op jit(solution)/shard_map/ppermute | solution.py:425
  83.3 0.6 pad_add_fusion.numbers
  83.9 2.1 collective-permute-start.13
  86.0 2.7 %pair_hits.3.hits = bf16[8,132,512]{2,1,0:T(8,128)(2,1)} custom-call(s32[4]{0:T(128)} %pad_add_fusion.numbers, s32[8]{0:T(128)} %and_select_fusion.order, bf16[8,136,128]{2,1,0:T(8,128)(2,1)} %slice.62.code), custom_call_target="tpu_custom_call" | custom-call | flops 700000000 | bytes 4000000 | tf_op jit(solution)/shard_map/pair_hits/pallas_call | solution.py:187
  88.8 0.5 copy-done.9
  89.3 0.6 copy-done.8
  90.0 4.3 %expand.1 = bf16[32,64,512]{2,1,0:T(8,128)(2,1)} custom-call(bf16[8,132,512]{2,1,0:T(8,128)(2,1)} %pair_hits.3.hits, bf16[132,512]{1,0:T(8,128)(2,1)} %copy-done.1, bf16[132,512]{1,0:T(8,128)(2,1)} %copy-done.4, bf16[132,512]{1,0:T(8,128)(2,1)} %copy-done.5, bf16[132,512]{1,0:T(8,128)(2,1)} %copy-done.6, bf16[132,512]{1,0:T(8,128)(2,1)} %copy-done.7, ...), custom_call_target="tpu_custom_call" | custom-call | flops 700000000 | bytes 4000000 | tf_op jit(solution)/shard_map/expand/pallas_call | solution.py:218
  94.3 1.4 collective-permute-start.19
  95.7 1.7 collective-permute-start.21
  97.4 10.0 %all-to-all-start = ((bf16[32,64,512]{2,1,0:T(8,128)(2,1)}), bf16[32,64,512]{2,1,0:T(8,128)(2,1)}, u32[]{:S(2)}, u32[]{:S(2)}) async-start(bf16[32,64,512]{2,1,0:T(8,128)(2,1)} %expand.1), calls=%async_computation | async-start | bytes 4194304 | tf_op jit(solution)/shard_map/all_to_all | solution.py:522
  107.3 3.1 %collective-permute-start.20 = (bf16[256,2048]{1,0:T(8,128)(2,1)S(1)}, bf16[256,2048]{1,0:T(8,128)(2,1)}, u32[]{:S(2)}, u32[]{:S(2)}) collective-permute-start(bf16[256,2048]{1,0:T(8,128)(2,1)S(1)} %bitcast.71), channel_id=1, source_target_pairs={{0,4},{1,5},{6,2},{7,3},{8,12},{9,13},{14,10},{15,11},{16,20},{17,... | collective-permute-start | bytes 3145736 | tf_op jit(solution)/shard_map/ppermute | solution.py:552
  110.4 1.5 collective-permute-start.23
  112.2 0.2 dynamic-slice_reduce_fusion
  112.5 0.9 add.164.origin
  113.4 0.5 fusion.31.order
  114.0 6.1 %chosen_rows.1.codes = f32[8,64,128]{2,1,0:T(8,128)} custom-call(s32[4]{0:T(128)} %pad_add_fusion.numbers, bf16[64,136,128]{2,1,0:T(8,128)(2,1)} %all-gather.7.cloned.1.call-done.code), custom_call_target="tpu_custom_call" | custom-call | flops 200000000 | bytes 2000000 | tf_op jit(solution)/shard_map/chosen_rows/pallas_call | solution.py:279
  120.1 3.3 %pair_hits.2.hits = bf16[8,132,512]{2,1,0:T(8,128)(2,1)} custom-call(s32[4]{0:T(128)} %pad_add_fusion.numbers, s32[8]{0:T(128)} %fusion.31.order, bf16[64,136,128]{2,1,0:T(8,128)(2,1)} %all-gather.7.cloned.1.call-done.code), custom_call_target="tpu_custom_call" | custom-call | flops 700000000 | bytes 4000000 | tf_op jit(solution)/shard_map/pair_hits/pallas_call | solution.py:187
  123.4 16.3 %all-to-all-done = bf16[32,64,512]{2,1,0:T(8,128)(2,1)} async-done(((bf16[32,64,512]{2,1,0:T(8,128)(2,1)}), bf16[32,64,512]{2,1,0:T(8,128)(2,1)}, u32[]{:S(2)}, u32[]{:S(2)}) %all-to-all-start) | async-done | bytes 2097184 | tf_op jit(solution)/shard_map/all_to_all | solution.py:522
  139.7 14.3 %expert.1 = bf16[8,4,64,512]{3,2,1,0:T(8,128)(2,1)} custom-call(s32[4]{0:T(128)} %pad_add_fusion.numbers, bf16[8,4,64,512]{3,2,1,0:T(8,128)(2,1)} %bitcast.26.arrived, f32[8,64,128]{2,1,0:T(8,128)} %chosen_rows.1.codes, s32[512,1]{1,0:T(8,128)} %add.164.origin, f32[1,2048]{1,0:T(1,128)} %bitcast.73, bf16[64,2048]{1,0:T(8,128)(2,1)} %bitcast.72, ...), custom_call_target="tpu_custom_call" | custom-call | flops 8000000000 | bytes 20000000 | tf_op jit(solution)/shard_map/expert/pallas_call | solution.py:367
  154.0 33.0 %all_to_all.10.answers = bf16[32,64,512]{2,1,0:T(8,128)(2,1)} all-to-all(bf16[32,64,512]{2,1,0:T(8,128)(2,1)} %bitcast.53), channel_id=1, replica_groups=mesh['z'=8,'y'=4,'c'=2,'tp'=4] {'y','c','tp'}, dimensions={0} | all-to-all | bytes 4194304 | tf_op jit(solution)/shard_map/all_to_all | solution.py:522
  187.0 4.4 %combine.1 = bf16[8,132,512]{2,1,0:T(8,128)(2,1)} custom-call(bf16[8,132,512]{2,1,0:T(8,128)(2,1)} %pair_hits.2.hits, bf16[32,64,512]{2,1,0:T(8,128)(2,1)} %all_to_all.10.answers), custom_call_target="tpu_custom_call" | custom-call | flops 600000000 | bytes 4000000 | tf_op jit(solution)/shard_map/combine/pallas_call | solution.py:238
  191.4 1.3 reshape.69
  192.8 25.2 %fusion = bf16[136,512]{1,0:T(8,128)(2,1)S(1)} fusion(bf16[1056,512]{1,0:T(8,128)(2,1)S(1)} %reshape.69), kind=kCustom, calls=%all-reduce-scatter | all-reduce-scatter fusion | flops 557057 | bytes 1221632
  217.9 1.9 collective-permute-start.24
  219.9 0.6 dynamic-slice.8
  221.1 2.6 %collective-permute-done.24 = bf16[28,512]{1,0:T(8,128)(2,1)S(1)} collective-permute-done((bf16[28,512]{1,0:T(8,128)(2,1)S(1)}, bf16[28,512]{1,0:T(8,128)(2,1)S(1)}, u32[]{:S(2)}, u32[]{:S(2)}) %collective-permute-start.24) | collective-permute-done | bytes 28704
  223.8 0.2 concatenate.16
  224.0 0.7 constant_dynamic-slice_fusion
  (70 shorter events, 0.9 us)
Async XLA Ops:
  6.5 57.0 %all-gather.5.cloned.1.call-start = ((), (), s32[]{:S(2)}) async-start(), calls=%async_computation.2 | async-start | bytes 1253376 | tf_op jit(solution)/shard_map/all_gather | solution.py:458
  7.8 6.2 %collective-permute-start.2 = (f32[2,132]{0,1:T(8,128)S(1)}, f32[2,132]{0,1:T(8,128)S(1)}, u32[]{:S(2)}, u32[]{:S(2)}) collective-permute-start(f32[2,132]{0,1:T(8,128)S(1)} %copy.28), channel_id=1, source_target_pairs={{0,3},{1,0},{2,1},{3,2},{4,7},{5,4},{6,5},{7,6},{8,11},{9,8},{10,9... | collective-permute-start | bytes 3176 | tf_op jit(solution)/shard_map/ppermute | solution.py:425
  10.6 5.9 %collective-permute-start.1 = (f32[2,132]{0,1:T(8,128)S(1)}, f32[2,132]{0,1:T(8,128)S(1)}, u32[]{:S(2)}, u32[]{:S(2)}) collective-permute-start(f32[2,132]{0,1:T(8,128)S(1)} %copy.28), channel_id=1, source_target_pairs={{0,2},{1,3},{2,0},{3,1},{4,6},{5,7},{6,4},{7,5},{8,10},{9,11},{10,... | collective-permute-start | bytes 3176 | tf_op jit(solution)/shard_map/ppermute | solution.py:425
  11.4 5.8 %collective-permute-start = (f32[2,132]{0,1:T(8,128)S(1)}, f32[2,132]{0,1:T(8,128)S(1)}, u32[]{:S(2)}, u32[]{:S(2)}) collective-permute-start(f32[2,132]{0,1:T(8,128)S(1)} %copy.28), channel_id=1, source_target_pairs={{0,1},{1,2},{2,3},{3,0},{4,5},{5,6},{6,7},{7,4},{8,9},{9,10},{10,1... | collective-permute-start | bytes 3176 | tf_op jit(solution)/shard_map/ppermute | solution.py:425
  12.3 5.1 %copy-start.11 = (s32[132,8]{0,1:T(8,128)S(1)}, s32[132,8]{0,1:T(8,128)}, u32[]{:S(2)}) copy-start(s32[132,8]{0,1:T(8,128)} %param.26) | copy-start | bytes 12676
  12.3 6.9 %copy-start.10 = (s32[4]{0:T(128)S(1)}, s32[4]{0:T(128)}, u32[]{:S(2)}) copy-start(s32[4]{0:T(128)} %param.24) | copy-start | bytes 52
  14.0 55.4 %copy-start = (bf16[4096,256]{1,0:T(8,128)(2,1)}, bf16[4096,256]{1,0:T(8,128)(2,1)S(1)}, u32[]{:S(2)}) copy-start(bf16[4096,256]{1,0:T(8,128)(2,1)S(1)} %pad_maximum_fusion.refs_0_) | copy-start | bytes 6291460
  17.3 26.2 %collective-permute-start.3 = (bf16[4096,256]{1,0:T(8,128)(2,1)S(1)}, bf16[4096,256]{1,0:T(8,128)(2,1)}, u32[]{:S(2)}, u32[]{:S(2)}) collective-permute-start(bf16[4096,256]{1,0:T(8,128)(2,1)S(1)} %pad_maximum_fusion.refs_0_), channel_id=1, source_target_pairs={{0,1},{1,0},{2,5},{3,4},{6,7},{7,6},{5,2},{4,3},{8,9},{9,8},{10,13... | collective-permute-start | bytes 6291464 | tf_op jit(solution)/shard_map/ppermute | solution.py:470
  18.5 95.5 %all-gather.7.cloned.1.call-start = ((), (), s32[]{:S(2)}) async-start(), calls=%async_computation.3 | async-start | bytes 2506752 | tf_op jit(solution)/shard_map/all_gather | solution.py:514
  24.6 52.4 %copy-start.16 = (s32[8]{0:T(128)S(1)}, s32[8]{0:T(128)}, u32[]{:S(2)}) copy-start(s32[8]{0:T(128)} %constant.153.clone) | copy-start | bytes 100
  43.5 6.6 %collective-permute-start.6 = (bf16[132,512]{1,0:T(8,128)(2,1)}, bf16[132,512]{1,0:T(8,128)(2,1)S(1)}, u32[]{:S(2)}, u32[]{:S(2)}) collective-permute-start(bf16[132,512]{1,0:T(8,128)(2,1)} %get-tuple-element.34), channel_id=1, source_target_pairs={{0,3},{1,0},{2,1},{3,2},{4,7},{5,4},{6,5},{7,6},{8,11},{9,8},{10,9... | collective-permute-start | bytes 405512 | tf_op jit(solution)/shard_map/ppermute | solution.py:425
  44.7 7.5 %collective-permute-start.5 = (bf16[132,512]{1,0:T(8,128)(2,1)}, bf16[132,512]{1,0:T(8,128)(2,1)S(1)}, u32[]{:S(2)}, u32[]{:S(2)}) collective-permute-start(bf16[132,512]{1,0:T(8,128)(2,1)} %get-tuple-element.33), channel_id=1, source_target_pairs={{0,2},{1,3},{2,0},{3,1},{4,6},{5,7},{6,4},{7,5},{8,10},{9,11},{10,... | collective-permute-start | bytes 405512 | tf_op jit(solution)/shard_map/ppermute | solution.py:425
  45.6 7.7 %collective-permute-start.4 = (bf16[132,512]{1,0:T(8,128)(2,1)}, bf16[132,512]{1,0:T(8,128)(2,1)S(1)}, u32[]{:S(2)}, u32[]{:S(2)}) collective-permute-start(bf16[132,512]{1,0:T(8,128)(2,1)} %get-tuple-element.32), channel_id=1, source_target_pairs={{0,1},{1,2},{2,3},{3,0},{4,5},{5,6},{6,7},{7,4},{8,9},{9,10},{10,1... | collective-permute-start | bytes 405512 | tf_op jit(solution)/shard_map/ppermute | solution.py:425
  54.3 34.4 %copy-start.1 = (bf16[132,512]{1,0:T(8,128)(2,1)}, bf16[132,512]{1,0:T(8,128)(2,1)S(1)}, u32[]{:S(2)}) copy-start(bf16[132,512]{1,0:T(8,128)(2,1)S(1)} %add_convert_fusion.refs_0_) | copy-start | bytes 405508
  54.3 5.3 %collective-permute-start.7 = (bf16[132,512]{1,0:T(8,128)(2,1)S(1)}, bf16[132,512]{1,0:T(8,128)(2,1)S(1)}, u32[]{:S(2)}, u32[]{:S(2)}) collective-permute-start(bf16[132,512]{1,0:T(8,128)(2,1)S(1)} %add_convert_fusion.refs_0_), channel_id=1, source_target_pairs={{0,32},{32,64},{64,96},{96,128},{128,160},{160,192},{192,224},{224... | collective-permute-start | bytes 405512 | tf_op jit(solution)/shard_map/ppermute | solution.py:425
  56.3 5.8 %collective-permute-start.9 = (bf16[132,512]{1,0:T(8,128)(2,1)S(1)}, bf16[132,512]{1,0:T(8,128)(2,1)S(1)}, u32[]{:S(2)}, u32[]{:S(2)}) collective-permute-start(bf16[132,512]{1,0:T(8,128)(2,1)S(1)} %add_convert_fusion.refs_0_), channel_id=1, source_target_pairs={{0,224},{32,0},{64,32},{96,64},{128,96},{160,128},{192,160},{224,1... | collective-permute-start | bytes 405512 | tf_op jit(solution)/shard_map/ppermute | solution.py:425
  56.4 37.8 %collective-permute-start.15 = (bf16[4096,256]{1,0:T(8,128)(2,1)}, bf16[4096,256]{1,0:T(8,128)(2,1)}, u32[]{:S(2)}, u32[]{:S(2)}) collective-permute-start(bf16[4096,256]{1,0:T(8,128)(2,1)} %collective-permute-done.3.refs_1_), channel_id=1, source_target_pairs={{4,5},{5,4},{2,3},{3,2},{12,13},{13,12},{10,11},{11,10},{20,21},{2... | collective-permute-start | bytes 6291464 | tf_op jit(solution)/shard_map/ppermute | solution.py:508
  59.6 29.1 %copy-start.4 = (bf16[132,512]{1,0:T(8,128)(2,1)}, bf16[132,512]{1,0:T(8,128)(2,1)S(1)}, u32[]{:S(2)}) copy-start(bf16[132,512]{1,0:T(8,128)(2,1)S(1)} %collective-permute-done.7.refs_1_) | copy-start | bytes 405508
  59.6 6.8 %collective-permute-start.8 = (bf16[132,512]{1,0:T(8,128)(2,1)S(1)}, bf16[132,512]{1,0:T(8,128)(2,1)S(1)}, u32[]{:S(2)}, u32[]{:S(2)}) collective-permute-start(bf16[132,512]{1,0:T(8,128)(2,1)S(1)} %collective-permute-done.7.refs_1_), channel_id=1, source_target_pairs={{0,32},{32,64},{64,96},{96,128},{128,160},{160,192},{192,224},{224... | collective-permute-start | bytes 405512 | tf_op jit(solution)/shard_map/ppermute | solution.py:425
  62.1 26.6 %copy-start.5 = (bf16[132,512]{1,0:T(8,128)(2,1)}, bf16[132,512]{1,0:T(8,128)(2,1)S(1)}, u32[]{:S(2)}) copy-start(bf16[132,512]{1,0:T(8,128)(2,1)S(1)} %collective-permute-done.9.refs_2_) | copy-start | bytes 405508
  62.1 5.3 %collective-permute-start.10 = (bf16[132,512]{1,0:T(8,128)(2,1)S(1)}, bf16[132,512]{1,0:T(8,128)(2,1)S(1)}, u32[]{:S(2)}, u32[]{:S(2)}) collective-permute-start(bf16[132,512]{1,0:T(8,128)(2,1)S(1)} %collective-permute-done.9.refs_2_), channel_id=1, source_target_pairs={{0,224},{32,0},{64,32},{96,64},{128,96},{160,128},{192,160},{224,1... | collective-permute-start | bytes 405512 | tf_op jit(solution)/shard_map/ppermute | solution.py:425
  66.4 22.3 %copy-start.6 = (bf16[132,512]{1,0:T(8,128)(2,1)}, bf16[132,512]{1,0:T(8,128)(2,1)S(1)}, u32[]{:S(2)}) copy-start(bf16[132,512]{1,0:T(8,128)(2,1)S(1)} %collective-permute-done.8.refs_3_) | copy-start | bytes 405508
  67.4 21.3 %copy-start.7 = (bf16[132,512]{1,0:T(8,128)(2,1)}, bf16[132,512]{1,0:T(8,128)(2,1)S(1)}, u32[]{:S(2)}) copy-start(bf16[132,512]{1,0:T(8,128)(2,1)S(1)} %collective-permute-done.10.refs_4_) | copy-start | bytes 405508
  69.2 25.1 %collective-permute-start.16 = (bf16[256,2048]{1,0:T(8,128)(2,1)}, bf16[256,2048]{1,0:T(8,128)(2,1)}, u32[]{:S(2)}, u32[]{:S(2)}) collective-permute-start(bf16[256,2048]{1,0:T(8,128)(2,1)} %bitcast.69), channel_id=1, source_target_pairs={{0,1},{1,0},{2,5},{3,4},{6,7},{7,6},{5,2},{4,3},{8,9},{9,8},{10,13... | collective-permute-start | bytes 3145736 | tf_op jit(solution)/shard_map/ppermute | solution.py:507
  69.4 41.0 %collective-permute-start.17 = (bf16[4096,256]{1,0:T(8,128)(2,1)S(1)}, bf16[4096,256]{1,0:T(8,128)(2,1)}, u32[]{:S(2)}, u32[]{:S(2)}) collective-permute-start(bf16[4096,256]{1,0:T(8,128)(2,1)S(1)} %pad_maximum_fusion.refs_0_), channel_id=1, source_target_pairs={{0,4},{1,5},{6,2},{7,3},{8,12},{9,13},{14,10},{15,11},{16,20},{17,... | collective-permute-start | bytes 6291464 | tf_op jit(solution)/shard_map/ppermute | solution.py:552
  73.7 10.2 %collective-permute-start.11 = (bf16[132,512]{1,0:T(8,128)(2,1)S(1)}, bf16[132,512]{1,0:T(8,128)(2,1)S(1)}, u32[]{:S(2)}, u32[]{:S(2)}) collective-permute-start(bf16[132,512]{1,0:T(8,128)(2,1)S(1)} %collective-permute-done.8.refs_3_), channel_id=1, source_target_pairs={{0,32},{32,64},{64,96},{96,128},{128,160},{160,192},{192,224},{224... | collective-permute-start | bytes 405512 | tf_op jit(solution)/shard_map/ppermute | solution.py:425
  77.0 6.3 %collective-permute-start.12 = (bf16[132,512]{1,0:T(8,128)(2,1)S(1)}, bf16[132,512]{1,0:T(8,128)(2,1)S(1)}, u32[]{:S(2)}, u32[]{:S(2)}) collective-permute-start(bf16[132,512]{1,0:T(8,128)(2,1)S(1)} %collective-permute-done.10.refs_4_), channel_id=1, source_target_pairs={{0,224},{32,0},{64,32},{96,64},{128,96},{160,128},{192,160},{224,1... | collective-permute-start | bytes 405512 | tf_op jit(solution)/shard_map/ppermute | solution.py:425
  83.2 5.5 %copy-start.2 = (bf16[132,512]{1,0:T(8,128)(2,1)}, bf16[132,512]{1,0:T(8,128)(2,1)S(1)}, u32[]{:S(2)}) copy-start(bf16[132,512]{1,0:T(8,128)(2,1)S(1)} %collective-permute-done.12.refs_6_) | copy-start | bytes 405508
  83.3 5.5 %collective-permute-start.14 = (bf16[68,512]{1,0:T(8,128)(2,1)S(1)}, bf16[68,512]{1,0:T(8,128)(2,1)S(1)}, u32[]{:S(2)}, u32[]{:S(2)}) collective-permute-start(bf16[68,512]{1,0:T(8,128)(2,1)S(1)} %slice.67), channel_id=1, source_target_pairs={{0,224},{32,0},{64,32},{96,64},{128,96},{160,128},{192,160},{224,1... | collective-permute-start | bytes 208904 | tf_op jit(solution)/shard_map/ppermute | solution.py:425
  83.9 4.9 %copy-start.3 = (bf16[132,512]{1,0:T(8,128)(2,1)}, bf16[132,512]{1,0:T(8,128)(2,1)S(1)}, u32[]{:S(2)}) copy-start(bf16[132,512]{1,0:T(8,128)(2,1)S(1)} %collective-permute-done.11.refs_5_) | copy-start | bytes 405508
  83.9 4.8 %collective-permute-start.13 = (bf16[64,512]{1,0:T(8,128)(2,1)S(1)}, bf16[64,512]{1,0:T(8,128)(2,1)S(1)}, u32[]{:S(2)}, u32[]{:S(2)}) collective-permute-start(bf16[64,512]{1,0:T(8,128)(2,1)S(1)} %slice.66), channel_id=1, source_target_pairs={{0,32},{32,64},{64,96},{96,128},{128,160},{160,192},{192,224},{224... | collective-permute-start | bytes 196616 | tf_op jit(solution)/shard_map/ppermute | solution.py:425
  88.7 0.6 copy-start.9
  88.7 34.7 %collective-permute-start.18 = (bf16[4096,256]{1,0:T(8,128)(2,1)}, bf16[4096,256]{1,0:T(8,128)(2,1)}, u32[]{:S(2)}, u32[]{:S(2)}) collective-permute-start(bf16[4096,256]{1,0:T(8,128)(2,1)} %collective-permute-done.3.refs_1_), channel_id=1, source_target_pairs={{0,4},{1,5},{2,6},{3,7},{4,0},{5,1},{6,2},{7,3},{8,12},{9,13},{10,... | collective-permute-start | bytes 6291464 | tf_op jit(solution)/shard_map/ppermute | solution.py:554
  89.3 0.6 copy-start.8
  94.3 13.1 %copy-start.13 = (bf16[1,256,2048]{2,1,0:T(8,128)(2,1)S(1)}, bf16[1,256,2048]{2,1,0:T(8,128)(2,1)}, u32[]{:S(2)}) copy-start(bf16[1,256,2048]{2,1,0:T(8,128)(2,1)} %param.32) | copy-start | bytes 3145732
  94.3 17.7 %copy-start.15 = (s32[64]{0:T(128)S(1)}, s32[64]{0:T(128)}, u32[]{:S(2)}) copy-start(s32[64]{0:T(128)} %param.25) | copy-start | bytes 772
  94.3 45.4 %collective-permute-start.19 = (bf16[4096,256]{1,0:T(8,128)(2,1)}, bf16[4096,256]{1,0:T(8,128)(2,1)}, u32[]{:S(2)}, u32[]{:S(2)}) collective-permute-start(bf16[4096,256]{1,0:T(8,128)(2,1)} %collective-permute-done.15.refs_3_), channel_id=1, source_target_pairs={{4,0},{5,1},{2,6},{3,7},{12,8},{13,9},{10,14},{11,15},{20,16},{21,... | collective-permute-start | bytes 6291464 | tf_op jit(solution)/shard_map/ppermute | solution.py:555
  95.7 14.7 %collective-permute-start.21 = (bf16[256,2048]{1,0:T(8,128)(2,1)}, bf16[256,2048]{1,0:T(8,128)(2,1)}, u32[]{:S(2)}, u32[]{:S(2)}) collective-permute-start(bf16[256,2048]{1,0:T(8,128)(2,1)} %collective-permute-done.16.refs_7_), channel_id=1, source_target_pairs={{4,5},{5,4},{2,3},{3,2},{12,13},{13,12},{10,11},{11,10},{20,21},{2... | collective-permute-start | bytes 3145736 | tf_op jit(solution)/shard_map/ppermute | solution.py:528
  97.4 42.3 %all-to-all-start = ((bf16[32,64,512]{2,1,0:T(8,128)(2,1)}), bf16[32,64,512]{2,1,0:T(8,128)(2,1)}, u32[]{:S(2)}, u32[]{:S(2)}) async-start(bf16[32,64,512]{2,1,0:T(8,128)(2,1)} %expand.1), calls=%async_computation | async-start | bytes 4194304 | tf_op jit(solution)/shard_map/all_to_all | solution.py:522
  107.3 16.0 %collective-permute-start.20 = (bf16[256,2048]{1,0:T(8,128)(2,1)S(1)}, bf16[256,2048]{1,0:T(8,128)(2,1)}, u32[]{:S(2)}, u32[]{:S(2)}) collective-permute-start(bf16[256,2048]{1,0:T(8,128)(2,1)S(1)} %bitcast.71), channel_id=1, source_target_pairs={{0,4},{1,5},{6,2},{7,3},{8,12},{9,13},{14,10},{15,11},{16,20},{17,... | collective-permute-start | bytes 3145736 | tf_op jit(solution)/shard_map/ppermute | solution.py:552
  110.4 12.9 %collective-permute-start.22 = (bf16[256,2048]{1,0:T(8,128)(2,1)}, bf16[256,2048]{1,0:T(8,128)(2,1)S(1)}, u32[]{:S(2)}, u32[]{:S(2)}) collective-permute-start(bf16[256,2048]{1,0:T(8,128)(2,1)} %collective-permute-done.16.refs_7_), channel_id=1, source_target_pairs={{0,4},{1,5},{2,6},{3,7},{4,0},{5,1},{6,2},{7,3},{8,12},{9,13},{10,... | collective-permute-start | bytes 3145736 | tf_op jit(solution)/shard_map/ppermute | solution.py:554
  110.4 29.2 %collective-permute-start.23 = (bf16[256,2048]{1,0:T(8,128)(2,1)}, bf16[256,2048]{1,0:T(8,128)(2,1)}, u32[]{:S(2)}, u32[]{:S(2)}) collective-permute-start(bf16[256,2048]{1,0:T(8,128)(2,1)} %collective-permute-done.21.refs_9_), channel_id=1, source_target_pairs={{4,0},{5,1},{2,6},{3,7},{12,8},{13,9},{10,14},{11,15},{20,16},{21,... | collective-permute-start | bytes 3145736 | tf_op jit(solution)/shard_map/ppermute | solution.py:555
  123.4 16.3 %copy-start.14 = (bf16[256,2048]{1,0:T(8,128)(2,1)}, bf16[256,2048]{1,0:T(8,128)(2,1)S(1)}, u32[]{:S(2)}) copy-start(bf16[256,2048]{1,0:T(8,128)(2,1)S(1)} %collective-permute-done.22.refs_10_) | copy-start | bytes 3145732
  191.4 28.5 %copy-start.12 = (u32[256]{0:T(256)S(1)}, u32[256]{0:T(256)}, u32[]{:S(2)}) copy-start(u32[256]{0:T(256)} %constant.168) | copy-start | bytes 3076
  217.9 5.8 %collective-permute-start.24 = (bf16[28,512]{1,0:T(8,128)(2,1)S(1)}, bf16[28,512]{1,0:T(8,128)(2,1)S(1)}, u32[]{:S(2)}, u32[]{:S(2)}) collective-permute-start(bf16[28,512]{1,0:T(8,128)(2,1)S(1)} %slice.68), channel_id=1, source_target_pairs={{0,32},{32,64},{64,96},{96,128},{128,160},{160,192},{192,224},{1,3... | collective-permute-start | bytes 86024
Sparse Core Ops, SparseCore 0:
  18.6 40.0 all-gather.4
  69.3 29.3 all-gather.6
